TPU v7x, 32 devices: a whole 2x2x4 slice. The times are simulated.
32 devices in a mesh: peer: 4 (over y, x), vocab: 8 (over z, core).
Axes of the slice: x: 2, y: 2, z: 4, core: 2. Of those that a mesh axis runs over, the one named last changes fastest.
Arguments:
- hidden: bfloat16 [4, 512, 4096], P('peer'), may hold values from -200 to 200
- head_weight: bfloat16 [4, 4096, 10240], P('peer', None, 'vocab'), may hold values from -0.484375 to 0.484375
- labels: int32 [512], replicated, may hold values from -100 to 10239, as said below
- segments: int32 [512], replicated, may hold values from 0 to 7, never falling along the last dimension, each value on 1 to 128 neighbouring positions
Outputs:
- grad_hidden: float32 [4, 512, 4096], P('peer', None, 'vocab')
- token_loss: float32 [4, 512], P('peer')
Inputs may be any that keep to these rules, and one draw needn't show every extreme that they name: `labels`: exactly 256 tokens carry the ignore label -100; every other label names a vocabulary entry.
All inputs are finite; a program needn't handle non-finite values.
Results may differ from a plain program's by a relative error of at most 0.0009.
The roundings to bfloat16 on the way count: a program that leaves them out, or rounds other values in their place, can miss the bound.
Values may be sent and summed in bfloat16 or wider, within the bound.
No kernel may reach another device: no remote copies, remote signals or barrier semaphores. Data moves between devices by JAX's collectives and lax.ppermute only.
A program may use at most 128 MiB of HBM per device.

v0:
```python
import jax
import jax.numpy as jnp
from jax import lax
from jax.sharding import PartitionSpec as P

SEGS = 8


def token_terms(
    row_peak, exp_total, cross_sum, target, labels, segments, own_peer, peers, group_tokens
):
    log_norm = row_peak + jnp.log(exp_total)
    expected = cross_sum / exp_total[:, None, :]
    self_term = jnp.diagonal(expected, axis1=0, axis2=1).T
    divergence = self_term[:, None, :] - expected - log_norm[:, None, :] + log_norm[None, :, :]
    forward_div = lax.dynamic_index_in_dim(divergence, own_peer, 0, False)
    backward_div = lax.dynamic_index_in_dim(divergence, own_peer, 1, False)
    labelled = (labels >= 0).astype(jnp.float32)
    own_norm = lax.dynamic_index_in_dim(log_norm, own_peer, 0, False)
    sym_div = jnp.sum(forward_div + backward_div, axis=0) / (peers - 1)
    token_loss = labelled * (own_norm - target + sym_div)
    member = (segments[:, None] == jnp.arange(SEGS, dtype=jnp.int32)[None, :]).astype(jnp.float32)
    seg_totals = jnp.sum(member * labelled[:, None], axis=0)
    seg_count = jnp.sum(member * seg_totals[None, :], axis=1)
    weight = labelled * group_tokens / (SEGS * jnp.maximum(seg_count, 1.0))
    return (log_norm, forward_div, token_loss, weight)


def logit_gradient(peer_tiles, log_norm, forward_div, weight, target_mask, own_peer, peers):
    log_probs = peer_tiles - log_norm[:, :, None]
    probs = jnp.exp(log_probs)
    own_probs = lax.dynamic_index_in_dim(probs, own_peer, 0, False)
    own_logp = lax.dynamic_index_in_dim(log_probs, own_peer, 0, False)
    mixed = peers * own_probs - jnp.sum(probs, axis=0)
    spread = peers * own_logp - jnp.sum(log_probs, axis=0) - jnp.sum(forward_div, axis=0)[:, None]
    logit_grad = own_probs - target_mask + (mixed + own_probs * spread) / (peers - 1)
    return (weight[:, None] * logit_grad).astype(jnp.bfloat16)


def moments(peer_tiles, row_peak):
    scaled = jnp.exp(peer_tiles - row_peak[:, :, None])
    exp_total = jnp.sum(scaled, axis=2)
    cross_sum = jnp.einsum("itv,jtv->ijt", scaled, peer_tiles, precision=lax.Precision.HIGHEST)
    return (exp_total, cross_sum)


def projector(weight_block, grad_rows):
    return lax.dot_general(
        weight_block, grad_rows, (((1,), (1,)), ((), ())), preferred_element_type=jnp.float32
    )


def on_device(hidden, head_weight, labels, segments):
    shard_width = head_weight.shape[2]
    token_count = hidden.shape[1]
    peers = lax.axis_size("peer")
    own_peer = lax.axis_index("peer")
    work_hidden = hidden[0]
    own_logits = jnp.dot(work_hidden, head_weight[0], preferred_element_type=jnp.float32).astype(
        jnp.bfloat16
    )
    peer_tiles = lax.all_gather(own_logits[None], "peer", axis=0, tiled=True).astype(jnp.float32)
    column_ids = lax.axis_index("vocab") * shard_width + lax.broadcasted_iota(
        jnp.int32, (1, shard_width), 1
    )
    target_mask = (labels[:, None] == column_ids).astype(jnp.float32)
    own_tile = lax.dynamic_index_in_dim(peer_tiles, own_peer, 0, False)
    target_part = jnp.sum(own_tile * target_mask, axis=1)
    local_peak = jnp.max(peer_tiles, axis=2)
    row_peak = lax.pmax(local_peak, "vocab")
    total_part, cross_part = moments(peer_tiles, row_peak)
    exp_total, cross_sum, target = lax.psum((total_part, cross_part, target_part), "vocab")
    log_norm, forward_div, token_loss, weight = token_terms(
        row_peak, exp_total, cross_sum, target, labels, segments, own_peer, peers, token_count
    )
    logit_grad = logit_gradient(
        peer_tiles, log_norm, forward_div, weight, target_mask, own_peer, peers
    )
    reduced = lax.psum_scatter(
        projector(head_weight[0], logit_grad), "vocab", scatter_dimension=0, tiled=True
    )
    grad_hidden = reduced.T
    return (grad_hidden[None], token_loss[None])


def solution(mesh):
    in_specs = (P("peer", None, None), P("peer", None, "vocab"), P(), P())
    out_specs = (P("peer", None, "vocab"), P("peer", None))
    return jax.shard_map(
        on_device, mesh=mesh, in_specs=in_specs, out_specs=out_specs, check_vma=False
    )
```

profile of v0, /device:TPU:0, one launch (start us, length us, event | category | flops | bytes accessed | tf_op | source)
XLA Modules:
  0.0 340.1 jit_solution(63557855215172167)
XLA Ops:
  7.2 0.0 all-gather.3.cloned.1.call-start
  7.2 11.2 %fusion.13 = bf16[512,1280]{1,0:T(8,128)(2,1)} fusion(bf16[1,4096,1280]{2,1,0:T(8,128)(2,1)} %param.5, bf16[1,512,4096]{2,1,0:T(8,128)(2,1)} %param.4), kind=kOutput, calls=%fused_computation.14 | convolution fusion | flops 5369364480 | bytes 15990784 | tf_op jit(solution)/shard_map/dot_general | solution.py:59
  18.5 0.0 all-gather.3.cloned.1.call-update
  18.5 0.0 reduce-scatter.2.cloned.1.call-start
  18.6 64.2 %all-gather.3.cloned.1.call-done = bf16[2048,1280]{1,0:T(8,128)(2,1)} async-done(((bf16[512,1280]{1,0:T(8,128)(2,1)}), bf16[2048,1280]{1,0:T(8,128)(2,1)}) %all-gather.3.cloned.1.call-update) | async-done | bytes 5242896 | tf_op jit(solution)/shard_map/all_gather | solution.py:62
  82.8 0.0 slice-start
  82.8 7.3 %bitcast_convert_fusion = (f32[4,512,1280]{2,1,0:T(8,128)}, bf16[2048]{0:T(1024)(128)(2,1)S(1)}) fusion(bf16[2048,1280]{1,0:T(8,128)(2,1)} %all-gather.3.cloned.1.call-done), kind=kLoop, calls=%fused_computation.52 | loop fusion | flops 5240832 | bytes 15732736 | tf_op jit(solution)/shard_map/convert_element_type | solution.py:62
  90.0 16.6 %pmax.7 = f32[4,512]{1,0:T(4,128)S(1)} all-reduce(f32[4,512]{1,0:T(4,128)S(1)} %reshape.86), channel_id=1, replica_groups=mesh['peer'=4,'vocab'=8] {'vocab'}, use_global_device_ids=true, to_apply=%region_3.4 | all-reduce | flops 2048 | bytes 16384 | tf_op jit(solution)/shard_map/pmax | solution.py:70
  106.6 0.0 slice-start.1
  106.6 8.8 %subtract_exponential_fusion = (f32[4,512,1280]{2,1,0:T(8,128)}, f32[4,512]{1,0:T(4,128)S(1)}) fusion(f32[4,512]{1,0:T(4,128)S(1)} %pmax.7, bf16[2048,1280]{1,0:T(8,128)(2,1)} %all-gather.3.cloned.1.call-done, bf16[4,512,1280]{2,1,0:T(8,128)(2,1)} %bitcast.71), kind=kLoop, calls=%fused_computation.7 | loop fusion | flops 13105152 | bytes 20987904 | tf_op jit(solution)/shard_map/exp | solution.py:41
  115.4 0.0 slice-done
  115.5 0.0 slice-done.1
  115.5 0.0 copy-start.1
  115.5 32.8 %fusion.28 = f32[4,4,512]{0,1,2:T(4,128)S(1)} fusion(f32[4,512,1280]{2,1,0:T(8,128)} %get-tuple-element.17, bf16[4,512,1280]{2,1,0:T(8,128)(2,1)S(1)} %bitcast.75), kind=kOutput, calls=%fused_computation.28 | convolution fusion | flops 125829120 | bytes 15761408 | tf_op jit(solution)/shard_map/itv,jtv->ijt/dot_general | solution.py:43
  148.2 0.0 copy-done.1
  148.3 2.1 fusion.18
  150.4 56.2 %all-reduce = (f32[4,512]{1,0:T(4,128)S(1)}, f32[4,4,512]{0,1,2:T(4,128)S(1)}, f32[512]{0:T(512)S(1)}) all-reduce(f32[4,512]{1,0:T(4,128)S(1)} %get-tuple-element.18, f32[4,4,512]{0,1,2:T(4,128)S(1)} %fusion.28, f32[512]{0:T(512)S(1)} %fusion.18), channel_id=1, replica_groups=mesh['peer'=4,'vocab'=8] {'vocab'}, use_global_device_ids=true, to_apply=%region_5.6 | all-reduce | flops 10752 | bytes 86016 | tf_op jit(solution)/shard_map/psum | solution.py:72
  206.6 0.1 copy.29
  206.8 0.1 copy.32
  206.9 0.3 fusion.44
  207.2 0.0 copy-start
  207.2 0.4 copy.30
  207.6 0.6 gather_fusion
  208.2 0.1 copy.31
  208.3 0.7 subtract_add_fusion
  209.0 0.2 constant_dynamic-slice_fusion
  209.3 3.9 %fusion.45 = (f32[512]{0:T(512)S(1)}, f32[1,4,512]{0,1,2:T(4,128)S(1)}) fusion(f32[4,4,512]{0,1,2:T(4,128)S(1)} %subtract_add_fusion, s32[]{:T(128)S(6)} %select_n.16), kind=kLoop, calls=%fused_computation.56 | loop fusion | flops 1536 | bytes 18436 | tf_op jit(solution)/shard_map/reduce_sum | solution.py:35
  213.2 0.1 copy.35
  213.3 0.4 copy.34
  213.7 0.6 add_select_fusion
  214.3 0.0 copy-done
  214.3 0.1 select_reduce_fusion.1
  214.4 0.1 select_reduce_fusion
  214.5 14.7 %fusion.12 = (f32[4,512,1280]{2,1,0:T(8,128)}, f32[4,512,1280]{2,1,0:T(8,128)}, f32[512,1280]{1,0:T(8,128)S(1)}, f32[512,1280]{1,0:T(8,128)}) fusion(f32[4,512]{1,0:T(4,128)S(1)} %log_add_fusion, bf16[2048,1280]{1,0:T(8,128)(2,1)} %all-gather.3.cloned.1.call-done, bf16[4,512,1280]{2,1,0:T(8,128)(2,1)} %bitcast.72), kind=kLoop, calls=%fused_computation.13 | loop fusion | flops 14417920 | bytes 36708352 | tf_op jit(solution)/shard_map/exp | solution.py:31
  229.2 14.2 %fusion.6 = f32[4096,512]{0,1:T(8,128)} fusion(bf16[1,4096,1280]{2,1,0:T(8,128)(2,1)} %param.5, f32[512,1280]{1,0:T(8,128)S(1)} %get-tuple-element.15, f32[512,1280]{1,0:T(8,128)} %get-tuple-element.16, f32[4,512,1280]{2,1,0:T(8,128)} %get-tuple-element.12, s32[]{:T(128)S(6)} %select_n.16, f32[4,512,1280]{2,1,0:T(8,128)} %get-tuple-element.11, ...), kind=kOutput, calls=%fused_computation.8 | convolution fusion | flops 5377884160 | bytes 29371396 | tf_op jit(solution)/shard_map/dot_general | solution.py:48
  243.4 0.0 reduce-scatter.2.cloned.1.call-update
  243.4 89.8 %reduce-scatter.2.cloned.1.call-done = f32[512,512]{0,1:T(8,128)} async-done(((f32[4096,512]{0,1:T(8,128)}), f32[512,512]{0,1:T(8,128)}) %reduce-scatter.2.cloned.1.call-update) | async-done | bytes 1048592 | tf_op jit(solution)/shard_map/reduce_scatter | solution.py:79
  (9 shorter events, 0.1 us)
Async XLA Ops:
  7.2 75.6 %all-gather.3.cloned.1.call-start = ((), (), s32[]{:S(2)}) async-start(), calls=%async_computation.2 | async-start | bytes 6553600 | tf_op jit(solution)/shard_map/all_gather | solution.py:62
  18.5 314.8 %reduce-scatter.2.cloned.1.call-start = ((), (), s32[]{:S(2)}) async-start(), calls=%async_computation.1 | async-start | bytes 9437184 | tf_op jit(solution)/shard_map/reduce_scatter | solution.py:79
  82.8 32.7 %slice-start = ((s8[5242880]{0:T(1024)(128)(4,1)}), s8[1048576]{0:T(1024)(128)(4,1)S(1)}, s32[]{:S(2)}) async-start(s8[5242880]{0:T(1024)(128)(4,1)} %bitcast.73), calls=%async_computation.3 | async-start | bytes 2097152
  106.6 8.8 %slice-start.1 = ((s8[5242880]{0:T(1024)(128)(4,1)}), s8[4194304]{0:T(1024)(128)(4,1)S(1)}, s32[]{:S(2)}) async-start(s8[5242880]{0:T(1024)(128)(4,1)} %bitcast.73), calls=%async_computation.4 | async-start | bytes 8388608
  115.5 32.8 %copy-start.1 = (s32[512]{0:T(512)S(1)}, s32[512]{0:T(512)}, u32[]{:S(2)}) copy-start(s32[512]{0:T(512)} %param.6) | copy-start | bytes 6148
  207.2 7.1 %copy-start = (s32[512]{0:T(512)S(1)}, s32[512]{0:T(512)}, u32[]{:S(2)}) copy-start(s32[512]{0:T(512)} %param.7) | copy-start | bytes 6148
Sparse Core Ops, SparseCore 0:
  18.6 64.1 all-gather.2
  243.5 89.6 reduce-scatter.1
where the time goes:
time: 340 us
  waiting for transfers between devices  154 us (45%)
  blocking collectives  72.8 us (21%)
  matrix products  58.2 us (17%)
  other arithmetic  38.6 us (11%)
  between operations  14.2 us (4%)
    reduce_scatter x1, waiting for transfers between devices, on_device(): lax.psum_scatter(projector(head_weight[0], logit_grad), 'vocab', scatter_...  89.8 us
    all_gather x1, waiting for transfers between devices, on_device(): lax.all_gather(own_logits[None], 'peer', axis=0, tiled=True)  64.2 us
    psum x1, blocking collectives, on_device(): lax.psum((total_part, cross_part, target_part), 'vocab')  56.2 us
    dot_general x1, matrix products, moments(): jnp.einsum('itv,jtv->ijt', scaled, peer_tiles, precision=lax.Precision.HI...  32.8 us
    pmax x1, blocking collectives, on_device(): row_peak = lax.pmax(local_peak, 'vocab')  16.6 us
    exp x1, other arithmetic, logit_gradient(): probs = jnp.exp(log_probs)  14.7 us
    dot_general x1, matrix products, projector(): lax.dot_general(weight_block, grad_rows, (((1,), (1,)), ((), ())), prefer...  14.2 us
    dot_general x1, matrix products, on_device(): jnp.dot(work_hidden, head_weight[0], preferred_element_type=jnp.float32)  11.2 us
  transfers between devices with their start and end apart: 2, of which 2 were waited for; matrix products, arithmetic and copies ran while one was open for 0% of the time, Pallas kernels for 0%

commit v1 on v0

v1 whole, which is shorter than its diff:
```python
import functools
import jax
import jax.numpy as jnp
from jax import lax
from jax.experimental import pallas as pl
from jax.experimental.pallas import tpu as pltpu
from jax.sharding import PartitionSpec as P

SEGS = 8
IGNORED = 256
GROUP = 16
LANES = 128
CODE_ROWS = 16
CODE_STEPS = 64.0
CODE_TOP = 32766.0
VMEM = pltpu.CompilerParams(vmem_limit_bytes=48 * 1024 * 1024)


def lane_ids(rows):
    return lax.broadcasted_iota(jnp.int32, (rows, LANES), 1)


def wanted_rank(row, own, block):
    return (own ^ (row // block)) * block + row % block + 1


def project_kernel(own_ref, lab_ref, seg_ref, hid_ref, w_ref, meta_ref, *rest):
    out_refs, (pick_ref, acc_ref) = rest[:-2], rest[-2:]
    step = pl.program_id(0)
    rows, tokens = pick_ref.shape
    block = out_refs[0].shape[0]

    @pl.when(step == 0)
    def _():
        lab = lab_ref[...]
        seg = seg_ref[...]
        on = lab >= 0
        flags = jnp.broadcast_to(on.astype(jnp.float32), (8, tokens)).astype(jnp.bfloat16)
        src = lax.broadcasted_iota(jnp.int32, (tokens, tokens), 0)
        dst = lax.broadcasted_iota(jnp.int32, (tokens, tokens), 1)
        upto = (src <= dst).astype(jnp.float32).astype(jnp.bfloat16)
        rank = jnp.dot(flags, upto, preferred_element_type=jnp.float32)[0:1, :].astype(jnp.int32)
        rank = jnp.where(on, rank, 0)
        row = lax.broadcasted_iota(jnp.int32, (rows, tokens), 0)
        pick = rank == wanted_rank(row, own_ref[0], block)
        pick_ref[...] = pick.astype(jnp.float32).astype(jnp.bfloat16)
        row = lax.broadcasted_iota(jnp.int32, (block, tokens), 0)
        mine = rank == wanted_rank(row, own_ref[0], block)
        label = jnp.sum(jnp.where(mine, lab, 0).astype(jnp.float32), axis=1, keepdims=True)
        doc = jnp.sum(jnp.where(mine, seg, 0).astype(jnp.float32), axis=1, keepdims=True)
        same = on & (seg.astype(jnp.float32) == doc)
        count = jnp.sum(jnp.where(same, 1.0, 0.0), axis=1, keepdims=True)
        weight = float(tokens) / (SEGS * jnp.maximum(count, 1.0))
        lane = lane_ids(block)
        meta_ref[...] = jnp.where(lane == 0, label, jnp.where(lane == 1, weight, 0.0))
        acc_ref[...] = jnp.zeros_like(acc_ref)

    hid = jnp.dot(pick_ref[...], hid_ref[0], preferred_element_type=jnp.float32)
    acc_ref[...] += jnp.dot(hid.astype(jnp.bfloat16), w_ref[0], preferred_element_type=jnp.float32)

    @pl.when(step == pl.num_programs(0) - 1)
    def _():
        for k, out_ref in enumerate(out_refs):
            out_ref[...] = acc_ref[k * block : (k + 1) * block, :].astype(jnp.bfloat16)


def project(own, labels, segments, hidden, head_weight, peers):
    tokens, depth = hidden.shape[1:]
    width = head_weight.shape[2]
    rows = tokens - IGNORED
    block = rows // peers
    part = 512
    whole = lambda shape: pl.BlockSpec(shape, lambda k: (0,) * len(shape))
    return pl.pallas_call(
        project_kernel,
        grid=(depth // part,),
        in_specs=[
            pl.BlockSpec(memory_space=pltpu.SMEM),
            whole((1, tokens)),
            whole((1, tokens)),
            pl.BlockSpec((1, tokens, part), lambda k: (0, 0, k)),
            pl.BlockSpec((1, part, width), lambda k: (0, k, 0)),
        ],
        out_specs=[whole((block, LANES))] + [whole((block, width))] * peers,
        out_shape=[jax.ShapeDtypeStruct((block, LANES), jnp.float32)]
        + [jax.ShapeDtypeStruct((block, width), jnp.bfloat16)] * peers,
        scratch_shapes=[pltpu.VMEM((rows, tokens), jnp.bfloat16), pltpu.VMEM((rows, width), jnp.float32)],
        compiler_params=VMEM,
        cost_estimate=pl.CostEstimate(
            flops=2 * rows * depth * (width + tokens), bytes_accessed=2 * depth * (width + tokens), transcendentals=0
        ),
        name="project",
    )(own, labels, segments, hidden, head_weight)


def pair_list(peers):
    return [(i, j) for i in range(peers) for j in range(peers) if i != j]


def stat_slots(peers):
    pairs = pair_list(peers)
    return peers, {p: peers + n for n, p in enumerate(pairs)}, peers + len(pairs)


def stats_kernel(base_ref, meta_ref, *refs):
    logit_refs, out_ref = refs[:-1], refs[-1]
    peers = len(logit_refs)
    block, width = logit_refs[0].shape
    _, pair_slot, target_slot = stat_slots(peers)
    span = LANES * GROUP // block
    lane = lane_ids(GROUP)
    sums = jnp.zeros((GROUP, LANES), jnp.float32)
    peaks = jnp.zeros((GROUP, LANES), jnp.float32)
    for g in range(block // GROUP):
        rows = slice(g * GROUP, (g + 1) * GROUP)
        label = meta_ref[rows, 0:1].astype(jnp.int32) - base_ref[0]
        peak = []
        for ref in logit_refs:
            top = ref[rows, 0:LANES].astype(jnp.float32)
            for c in range(LANES, width, LANES):
                top = jnp.maximum(top, ref[rows, c : c + LANES].astype(jnp.float32))
            peak.append(jnp.max(top, axis=1, keepdims=True))
        total = [jnp.zeros((GROUP, LANES), jnp.float32) for _ in range(peers)]
        target = [jnp.zeros((GROUP, LANES), jnp.float32) for _ in range(peers)]
        cross = {p: jnp.zeros((GROUP, LANES), jnp.float32) for p in pair_slot}
        for c in range(0, width, LANES):
            l = [ref[rows, c : c + LANES].astype(jnp.float32) for ref in logit_refs]
            e = [jnp.exp(l[k] - peak[k]) for k in range(peers)]
            hit = (lane + c) == label
            for i in range(peers):
                total[i] += e[i]
                target[i] += jnp.where(hit, l[i], 0.0)
                for j in range(i + 1, peers):
                    gap = l[i] - l[j]
                    cross[i, j] += e[i] * gap
                    cross[j, i] -= e[j] * gap

        def put(slot, vals, top):
            nonlocal sums, peaks
            here = lane == g * span + slot
            sums = jnp.where(here, jnp.sum(vals, axis=1, keepdims=True), sums)
            if top is not None:
                peaks = jnp.where(here, top, peaks)

        for i in range(peers):
            put(i, total[i], peak[i])
            put(target_slot + i, target[i], None)
        for (i, j), slot in pair_slot.items():
            put(slot, cross[i, j], peak[i])
    out_ref[0:GROUP, :] = sums
    out_ref[GROUP : 2 * GROUP, :] = peaks


def stats(base, meta, logits):
    block, width = logits[0].shape
    peers = len(logits)
    return pl.pallas_call(
        stats_kernel,
        in_specs=[pl.BlockSpec(memory_space=pltpu.SMEM)] + [pl.BlockSpec(memory_space=pltpu.VMEM)] * (1 + peers),
        out_shape=jax.ShapeDtypeStruct((2 * GROUP, LANES), jnp.float32),
        compiler_params=VMEM,
        cost_estimate=pl.CostEstimate(
            flops=40 * block * width * peers, bytes_accessed=2 * block * width * peers, transcendentals=block * width * peers
        ),
        name="stats",
    )(base, meta, *logits)


def merged(parts):
    top = parts[0][GROUP:, :]
    for part in parts[1:]:
        top = jnp.maximum(top, part[GROUP:, :])
    total = jnp.zeros_like(top)
    for part in parts:
        total += part[:GROUP, :] * jnp.exp(part[GROUP:, :] - top)
    return total, top


def merge_kernel(*refs):
    total, top = merged([ref[...] for ref in refs[:-1]])
    refs[-1][:GROUP, :] = total
    refs[-1][GROUP:, :] = top


def merge(parts):
    return pl.pallas_call(
        merge_kernel,
        in_specs=[pl.BlockSpec(memory_space=pltpu.VMEM)] * len(parts),
        out_shape=jax.ShapeDtypeStruct(parts[0].shape, jnp.float32),
        name="merge",
    )(*parts)


def grad_kernel(count, base_ref, meta_ref, *refs):
    stat_refs, refs = refs[:count], refs[count:]
    peers = len(refs) // 3
    logit_refs, grad_refs, loss_refs = refs[:peers], refs[peers : 2 * peers], refs[2 * peers :]
    block, width = logit_refs[0].shape
    _, pair_slot, target_slot = stat_slots(peers)
    span = LANES * GROUP // block
    lane = lane_ids(GROUP)
    total, top = merged([ref[...] for ref in stat_refs])
    norm = top + jnp.log(jnp.maximum(total, 1e-37))
    losses = [jnp.zeros((GROUP, LANES), jnp.float32) for _ in range(peers)]
    third = 1.0 / (peers - 1)
    for g in range(block // GROUP):
        rows = slice(g * GROUP, (g + 1) * GROUP)
        at = lambda array, slot: array[:, g * span + slot : g * span + slot + 1]
        label = meta_ref[rows, 0:1].astype(jnp.int32) - base_ref[0]
        weight = meta_ref[rows, 1:2]
        inverse = [1.0 / at(total, i) for i in range(peers)]
        norms = [at(norm, i) for i in range(peers)]
        mean = {p: at(total, slot) * inverse[p[0]] for p, slot in pair_slot.items()}
        shift = []
        for i in range(peers):
            ahead = sum(mean[i, j] for j in range(peers) if j != i)
            back = sum(mean[j, i] for j in range(peers) if j != i)
            loss = norms[i] - at(total, target_slot + i) + (ahead + back) * third
            losses[i] = jnp.where(lane == g * span, loss, losses[i])
            shift.append(1.0 + (peers - ahead) * third)
        for c in range(0, width, LANES):
            l = [ref[rows, c : c + LANES].astype(jnp.float32) for ref in logit_refs]
            p = [jnp.exp(l[k] - norms[k]) for k in range(peers)]
            common = sum(l) * third
            rest = sum(p) * third + jnp.where((lane + c) == label, 1.0, 0.0)
            for i in range(peers):
                grad = p[i] * (shift[i] + (l[i] * (peers * third) - common)) - rest
                grad_refs[i][rows, c : c + LANES] = (weight * grad).astype(jnp.bfloat16)
    for i in range(peers):
        loss_refs[i][...] = losses[i]


def gradients(base, meta, parts, logits):
    block, width = logits[0].shape
    peers = len(logits)
    outs = pl.pallas_call(
        functools.partial(grad_kernel, len(parts)),
        in_specs=[pl.BlockSpec(memory_space=pltpu.SMEM)]
        + [pl.BlockSpec(memory_space=pltpu.VMEM)] * (1 + len(parts) + peers),
        out_shape=[jax.ShapeDtypeStruct((block, width), jnp.bfloat16)] * peers
        + [jax.ShapeDtypeStruct((GROUP, LANES), jnp.float32)] * peers,
        compiler_params=VMEM,
        cost_estimate=pl.CostEstimate(
            flops=20 * block * width * peers, bytes_accessed=4 * block * width * peers, transcendentals=block * width * peers
        ),
        name="gradients",
    )(base, meta, *parts, *logits)
    return outs[:peers], outs[peers:]


def share_kernel(order_ref, *refs):
    w_ref, out_ref, all_ref = refs[-3:]
    block = refs[0].shape[0]

    @pl.when(pl.program_id(0) == 0)
    def _():
        for k, ref in enumerate(refs[:-3]):
            all_ref[k * block : (k + 1) * block, :] = ref[...]

    out_ref[0] = lax.dot_general(
        w_ref[0], all_ref[...], (((1,), (1,)), ((), ())), preferred_element_type=jnp.float32
    )


def share(order, grads, head_weight, depth):
    block, width = grads[0].shape
    rows = block * len(grads)
    count = order.shape[0]
    return pl.pallas_call(
        share_kernel,
        grid_spec=pltpu.PrefetchScalarGridSpec(
            num_scalar_prefetch=1,
            grid=(count,),
            in_specs=[pl.BlockSpec((block, width), lambda n, order: (0, 0))] * len(grads)
            + [pl.BlockSpec((1, depth, width), lambda n, order: (0, order[n], 0))],
            out_specs=pl.BlockSpec((1, depth, rows), lambda n, order: (n, 0, 0)),
            scratch_shapes=[pltpu.VMEM((rows, width), jnp.bfloat16)],
        ),
        out_shape=jax.ShapeDtypeStruct((count, depth, rows), jnp.float32),
        compiler_params=VMEM,
        cost_estimate=pl.CostEstimate(
            flops=2 * rows * width * depth * count, bytes_accessed=2 * width * depth * count, transcendentals=0
        ),
        name="share",
    )(order, *grads, head_weight)


def encode_kernel(a_ref, b_ref, out_ref):
    value = a_ref[0] + b_ref[0]
    depth = value.shape[0]
    top = jnp.maximum(jnp.max(jnp.abs(value), axis=0, keepdims=True), 1e-30)
    code = jnp.ceil(jnp.log2(top) * CODE_STEPS)
    unit = jnp.exp2(code * (-1.0 / CODE_STEPS)) * CODE_TOP
    coded = jnp.clip(jnp.round(value * unit), -CODE_TOP - 1, CODE_TOP + 1)
    out_ref[:depth, :] = coded.astype(jnp.int32).astype(jnp.int16)
    codes = jnp.broadcast_to(code, (CODE_ROWS, value.shape[1]))
    out_ref[depth:, :] = codes.astype(jnp.int32).astype(jnp.int16)


def encode(a, b, index):
    _, depth, rows = a.shape
    spec = pl.BlockSpec((1, depth, rows), lambda _: (index, 0, 0))
    return pl.pallas_call(
        encode_kernel,
        grid=(1,),
        in_specs=[spec, spec],
        out_specs=pl.BlockSpec((depth + CODE_ROWS, rows), lambda _: (0, 0)),
        out_shape=jax.ShapeDtypeStruct((depth + CODE_ROWS, rows), jnp.int16),
        compiler_params=VMEM,
        cost_estimate=pl.CostEstimate(flops=8 * depth * rows, bytes_accessed=10 * depth * rows, transcendentals=0),
        name="encode",
    )(a, b)


def finish_kernel(peers, own_ref, row_ref, col_ref, a_ref, b_ref, *refs):
    loss_refs, refs = refs[:peers], refs[peers:]
    coded_refs, (out_ref, loss_ref) = refs[:-2], refs[-2:]
    depth, rows = a_ref.shape[1:]
    tokens = row_ref.shape[1]
    block = rows // peers
    value = a_ref[0] + b_ref[0]
    for ref in coded_refs:
        code = ref[depth : depth + CODE_ROWS, :].astype(jnp.int32).astype(jnp.float32)[0:1, :]
        unit = jnp.exp2(code * (1.0 / CODE_STEPS)) * (1.0 / CODE_TOP)
        value += ref[:depth, :].astype(jnp.int32).astype(jnp.float32) * unit

    src = lax.broadcasted_iota(jnp.int32, (tokens, tokens), 0)
    dst = lax.broadcasted_iota(jnp.int32, (tokens, tokens), 1)
    on = row_ref[...] >= 0
    flags = jnp.broadcast_to(on.astype(jnp.float32), (8, tokens)).astype(jnp.bfloat16)
    upto = (src <= dst).astype(jnp.float32).astype(jnp.bfloat16)
    rank = jnp.dot(flags, upto, preferred_element_type=jnp.float32)[0:1, :].astype(jnp.int32)
    rank = jnp.where(on, rank, 0)
    losses = jnp.zeros((1, tokens), jnp.float32)
    span = LANES * GROUP // block
    for k in range(peers):
        for g in range(block // GROUP):
            row = lax.broadcasted_iota(jnp.int32, (GROUP, tokens), 0) + (k * block + g * GROUP)
            here = rank == wanted_rank(row, own_ref[0], block)
            piece = loss_refs[k][:, g * span : g * span + 1]
            losses += jnp.sum(jnp.where(here, piece, 0.0), axis=0, keepdims=True)
    loss_ref[...] = losses

    on = col_ref[...] >= 0
    flags = jnp.broadcast_to(on.astype(jnp.float32), (tokens, LANES)).astype(jnp.bfloat16)
    upto = (dst <= src).astype(jnp.float32).astype(jnp.bfloat16)
    rank = jnp.dot(upto, flags, preferred_element_type=jnp.float32)[:, 0:1].astype(jnp.int32)
    rank = jnp.where(on, rank, 0)
    row = lax.broadcasted_iota(jnp.int32, (tokens, rows), 1)
    place = (rank == wanted_rank(row, own_ref[0], block)).astype(jnp.float32).astype(jnp.bfloat16)
    result = jnp.zeros((tokens, depth), jnp.float32)
    for _ in range(3):
        piece = value.astype(jnp.bfloat16)
        value = value - piece.astype(jnp.float32)
        result += lax.dot_general(place, piece, (((1,), (1,)), ((), ())), preferred_element_type=jnp.float32)
    out_ref[0] = result


def finish(own, labels, a, b, losses, coded):
    _, depth, rows = a.shape
    tokens = labels.shape[0]
    first = pl.BlockSpec((1, depth, rows), lambda _: (0, 0, 0))
    whole = lambda shape: pl.BlockSpec(shape, lambda _: (0,) * len(shape))
    return pl.pallas_call(
        functools.partial(finish_kernel, len(losses)),
        grid=(1,),
        in_specs=[pl.BlockSpec(memory_space=pltpu.SMEM), whole((1, tokens)), whole((tokens, 1)), first, first]
        + [whole((GROUP, LANES))] * len(losses)
        + [whole((depth + CODE_ROWS, rows))] * len(coded),
        out_specs=[whole((1, tokens, depth)), whole((1, tokens))],
        out_shape=[
            jax.ShapeDtypeStruct((1, tokens, depth), jnp.float32),
            jax.ShapeDtypeStruct((1, tokens), jnp.float32),
        ],
        compiler_params=VMEM,
        cost_estimate=pl.CostEstimate(
            flops=6 * tokens * depth * rows, bytes_accessed=4 * tokens * depth, transcendentals=0
        ),
        name="finish",
    )(own, labels[None, :], labels[:, None], a, b, *losses, *coded)


def swap(array, axis, size, mask):
    return lax.ppermute(array, axis, [(i, i ^ mask) for i in range(size)])


def on_device(hidden, head_weight, labels, segments):
    peers = lax.axis_size("peer")
    shards = lax.axis_size("vocab")
    width = head_weight.shape[2]
    own = lax.axis_index("peer").astype(jnp.int32)
    shard = lax.axis_index("vocab").astype(jnp.int32)
    own_arr = own.reshape(1)
    base = (shard * width).reshape(1)
    depth = head_weight.shape[1] // shards
    chips = [2 * c for c in range(1, shards // 2)]

    meta, *blocks = project(own_arr, labels[None, :], segments[None, :], hidden, head_weight, peers)
    logits = [blocks[0]] + [swap(blocks[k], "peer", peers, k) for k in range(1, peers)]

    part = stats(base, meta, logits)
    part = merge([part, swap(part, "vocab", shards, 1)])
    parts = [part] + [swap(part, "vocab", shards, mask) for mask in chips]
    grads, losses = gradients(base, meta, parts, logits)
    grads = [grads[0]] + [swap(grads[k], "peer", peers, k) for k in range(1, peers)]
    losses = [losses[0]] + [swap(losses[k], "peer", peers, k) for k in range(1, peers)]

    masks = jnp.array([0] + chips, jnp.int32)
    theirs = share((shard ^ 1) ^ masks, grads, head_weight, depth)
    given = swap(theirs, "vocab", shards, 1)
    mine = share(shard ^ masks, grads, head_weight, depth)
    coded = [
        swap(encode(mine, given, n + 1), "vocab", shards, mask) for n, mask in enumerate(chips)
    ]
    grad_hidden, token_loss = finish(own_arr, labels, mine, given, losses, coded)
    return grad_hidden, token_loss


def solution(mesh):
    in_specs = (P("peer", None, None), P("peer", None, "vocab"), P(), P())
    out_specs = (P("peer", None, "vocab"), P("peer", None))
    return jax.shard_map(on_device, mesh=mesh, in_specs=in_specs, out_specs=out_specs, check_vma=False)
```

time: 340 us -> 90.6 us (0.27)
  waiting for transfers between devices: 154 us -> 34.2 us
  blocking collectives: 72.8 us -> 0 us
  matrix products: 58.2 us -> 0 us
  other arithmetic: 38.6 us -> 0.01 us
  Pallas kernels: 0 us -> 27.4 us
  starting transfers between devices: 0.08 us -> 20.9 us
  between operations: 14.2 us -> 0.76 us
  local copies, waits for them, and re-layouts: 2.14 us -> 6.61 us
    reduce_scatter x1 -> x0, waiting for transfers between devices: 89.8 us -> none  [on_device(): lax.psum_scatter(projector(head_weight[0], logit_grad), 'vocab', scatter_...]
    all_gather x1 -> x0, waiting for transfers between devices: 64.2 us -> none  [on_device(): lax.all_gather(own_logits[None], 'peer', axis=0, tiled=True)]
    dot_general x3 -> x0, matrix products: 58.2 us -> none  [the longest x1 32.8 us: moments(): jnp.einsum('itv,jtv->ijt', scaled, peer_tiles, precision=lax.Precision.HI...]
    psum x1 -> x0, blocking collectives: 56.2 us -> none  [on_device(): lax.psum((total_part, cross_part, target_part), 'vocab')]
    ppermute x0 -> x17, waiting for transfers between devices: none -> 34.2 us  [swap(): return lax.ppermute(array, axis, [(i, i ^ mask) for i in range(size)])]
    pallas_call x0 -> x10, Pallas kernels: none -> 27.4 us  [the longest x1 10.2 us: project(): pl.pallas_call(project_kernel, grid=(depth // part,), in_specs=[pl.BlockS...]
    exp x2 -> x0, other arithmetic: 23.5 us -> none  [the longest x1 14.7 us: logit_gradient(): probs = jnp.exp(log_probs)]
    ppermute x0 -> x17, starting transfers between devices: none -> 20.9 us  [swap(): return lax.ppermute(array, axis, [(i, i ^ mask) for i in range(size)])]
  transfers between devices with their start and end apart: 2 -> 17, of which waited for: 2 -> 10; matrix products, arithmetic and copies ran while one was open for 0% -> 0% of each run, Pallas kernels for 0% -> 7%
where the time goes in v1:
time: 90.6 us; the launch traced here: 90 us
  waiting for transfers between devices  34.2 us (38%)
  Pallas kernels  27.4 us (30%)
  starting transfers between devices  20.9 us (23%)
  local copies, waits for them, and re-layouts  6.61 us (7%)
    ppermute x17, waiting for transfers between devices, swap(): return lax.ppermute(array, axis, [(i, i ^ mask) for i in range(size)])  34.2 us
    ppermute x17, starting transfers between devices, swap(): return lax.ppermute(array, axis, [(i, i ^ mask) for i in range(size)])  20.9 us
    pallas_call x1, Pallas kernels, project(): pl.pallas_call(project_kernel, grid=(depth // part,), in_specs=[pl.BlockS...  10.2 us
    pallas_call x2, Pallas kernels, share(): pl.pallas_call(share_kernel, grid_spec=pltpu.PrefetchScalarGridSpec(num_s...  9.99 us
    unnamed x18, local copies, waits for them, and re-layouts  6.47 us
    pallas_call x1, Pallas kernels, finish(): pl.pallas_call(functools.partial(finish_kernel, len(losses)), grid=(1,),...  2.23 us
    pallas_call x3, Pallas kernels, encode(): pl.pallas_call(encode_kernel, grid=(1,), in_specs=[spec, spec], out_specs...  1.88 us
  transfers between devices with their start and end apart: 17, of which 10 were waited for; matrix products, arithmetic and copies ran while one was open for 0% of the time, Pallas kernels for 7%

profile of v1, /device:TPU:0, one launch (start us, length us, event | category | flops | bytes accessed | tf_op | source)
XLA Modules:
  0.0 90.0 jit_solution(16458913252474063698)
XLA Ops:
  0.6 0.0 copy-start.2
  0.6 2.2 %copy-done.2 = bf16[1,512,4096]{2,1,0:T(8,128)(2,1)S(1)} copy-done((bf16[1,512,4096]{2,1,0:T(8,128)(2,1)S(1)}, bf16[1,512,4096]{2,1,0:T(8,128)(2,1)}, u32[]{:S(2)}) %copy-start.2) | copy-done | bytes 4194328
  2.8 0.0 copy-start.5
  2.8 0.7 copy-done.5
  3.5 0.0 copy-start.7
  3.5 0.7 copy-done.7
  4.2 10.2 %project.1 = (f32[64,128]{1,0:T(8,128)S(1)}, bf16[64,1280]{1,0:T(8,128)(2,1)S(1)}, bf16[64,1280]{1,0:T(8,128)(2,1)S(1)}, bf16[64,1280]{1,0:T(8,128)(2,1)S(1)}, bf16[64,1280]{1,0:T(8,128)(2,1)S(1)}) custom-call(s32[1]{0:T(128)} %bitcast.own_ref, s32[1,512]{1,0:T(1,128)S(1)} %bitcast.5, s32[1,512]{1,0:T(1,128)S(1)} %bitcast.8, ...), custom_call_target="tpu_custom_call" | custom-call | flops 3758096384 | bytes 14680064 | tf_op jit(solution)/shard_map/project/pallas_call | solution.py:74
  14.4 3.0 %collective-permute-start = (bf16[64,1280]{1,0:T(8,128)(2,1)S(1)}, bf16[64,1280]{1,0:T(8,128)(2,1)S(1)}, u32[]{:S(2)}, u32[]{:S(2)}) collective-permute-start(bf16[64,1280]{1,0:T(8,128)(2,1)S(1)} %get-tuple-element.17), channel_id=1, source_target_pairs={{0,8},{8,0},{16,24},{24,16},{1,9},{9,1},{17,25},{25,17},{2,10},{10... | collective-permute-start | bytes 491528 | tf_op jit(solution)/shard_map/ppermute | solution.py:384
  17.4 1.5 %collective-permute-start.1 = (bf16[64,1280]{1,0:T(8,128)(2,1)S(1)}, bf16[64,1280]{1,0:T(8,128)(2,1)S(1)}, u32[]{:S(2)}, u32[]{:S(2)}) collective-permute-start(bf16[64,1280]{1,0:T(8,128)(2,1)S(1)} %get-tuple-element.18), channel_id=1, source_target_pairs={{0,16},{8,24},{16,0},{24,8},{1,17},{9,25},{17,1},{25,9},{2,18},{10... | collective-permute-start | bytes 491528 | tf_op jit(solution)/shard_map/ppermute | solution.py:384
  19.0 0.0 collective-permute-start.2
  19.0 3.5 %collective-permute-done.refs_1_.refs_5_ = bf16[64,1280]{1,0:T(8,128)(2,1)S(1)} collective-permute-done((bf16[64,1280]{1,0:T(8,128)(2,1)S(1)}, bf16[64,1280]{1,0:T(8,128)(2,1)S(1)}, u32[]{:S(2)}, u32[]{:S(2)}) %collective-permute-start) | collective-permute-done | bytes 163872 | tf_op jit(solution)/shard_map/ppermute | solution.py:384
  22.5 4.1 %collective-permute-done.1.refs_2_.refs_6_ = bf16[64,1280]{1,0:T(8,128)(2,1)S(1)} collective-permute-done((bf16[64,1280]{1,0:T(8,128)(2,1)S(1)}, bf16[64,1280]{1,0:T(8,128)(2,1)S(1)}, u32[]{:S(2)}, u32[]{:S(2)}) %collective-permute-start.1) | collective-permute-done | bytes 163872 | tf_op jit(solution)/shard_map/ppermute | solution.py:384
  26.6 0.0 collective-permute-done.2.refs_3_.refs_7_
  26.6 0.9 stats.1.refs_0_
  27.5 0.0 copy-start.4
  27.5 0.1 collective-permute-start.3
  27.6 1.2 %collective-permute-done.3.refs_1_ = f32[32,128]{1,0:T(8,128)S(1)} collective-permute-done((f32[32,128]{1,0:T(8,128)S(1)}, f32[32,128]{1,0:T(8,128)S(1)}, u32[]{:S(2)}, u32[]{:S(2)}) %collective-permute-start.3) | collective-permute-done | bytes 16416 | tf_op jit(solution)/shard_map/ppermute | solution.py:384
  28.7 0.0 copy-done.4
  28.7 0.0 copy-start.8
  28.7 0.6 copy-done.8
  29.3 1.3 %merge.1.refs_0_ = f32[32,128]{1,0:T(8,128)} custom-call(f32[32,128]{1,0:T(8,128)} %copy-done.4, f32[32,128]{1,0:T(8,128)} %copy-done.8), custom_call_target="tpu_custom_call" | custom-call | tf_op jit(solution)/shard_map/merge/pallas_call | solution.py:186
  30.7 1.6 %collective-permute-start.4 = (f32[32,128]{1,0:T(8,128)}, f32[32,128]{1,0:T(8,128)S(1)}, u32[]{:S(2)}, u32[]{:S(2)}) collective-permute-start(f32[32,128]{1,0:T(8,128)} %merge.1.refs_0_), channel_id=1, source_target_pairs={{0,2},{1,3},{2,0},{3,1},{4,6},{5,7},{6,4},{7,5},{8,10},{9,11},{10,... | collective-permute-start | bytes 49160 | tf_op jit(solution)/shard_map/ppermute | solution.py:384
  32.3 2.6 %collective-permute-start.5 = (f32[32,128]{1,0:T(8,128)}, f32[32,128]{1,0:T(8,128)S(1)}, u32[]{:S(2)}, u32[]{:S(2)}) collective-permute-start(f32[32,128]{1,0:T(8,128)} %merge.1.refs_0_), channel_id=1, source_target_pairs={{0,4},{1,5},{2,6},{3,7},{4,0},{5,1},{6,2},{7,3},{8,12},{9,13},{10,... | collective-permute-start | bytes 49160 | tf_op jit(solution)/shard_map/ppermute | solution.py:384
  34.9 0.2 collective-permute-start.6
  35.1 0.0 collective-permute-done.4.refs_1_
  35.1 2.1 %collective-permute-done.5.refs_2_ = f32[32,128]{1,0:T(8,128)S(1)} collective-permute-done((f32[32,128]{1,0:T(8,128)}, f32[32,128]{1,0:T(8,128)S(1)}, u32[]{:S(2)}, u32[]{:S(2)}) %collective-permute-start.5) | collective-permute-done | bytes 16416 | tf_op jit(solution)/shard_map/ppermute | solution.py:384
  37.2 3.4 %collective-permute-done.6.refs_3_ = f32[32,128]{1,0:T(8,128)S(1)} collective-permute-done((f32[32,128]{1,0:T(8,128)}, f32[32,128]{1,0:T(8,128)S(1)}, u32[]{:S(2)}, u32[]{:S(2)}) %collective-permute-start.6) | collective-permute-done | bytes 16416 | tf_op jit(solution)/shard_map/ppermute | solution.py:384
  40.6 0.0 copy-start.3
  40.6 0.7 copy-done.3
  41.3 0.9 gradients.1
  42.2 1.3 %collective-permute-start.7 = (bf16[64,1280]{1,0:T(8,128)(2,1)S(1)}, bf16[64,1280]{1,0:T(8,128)(2,1)S(1)}, u32[]{:S(2)}, u32[]{:S(2)}) collective-permute-start(bf16[64,1280]{1,0:T(8,128)(2,1)S(1)} %get-tuple-element.21), channel_id=1, source_target_pairs={{0,8},{8,0},{16,24},{24,16},{1,9},{9,1},{17,25},{25,17},{2,10},{10... | collective-permute-start | bytes 491528 | tf_op jit(solution)/shard_map/ppermute | solution.py:384
  43.5 0.8 collective-permute-start.8
  44.4 1.4 %collective-permute-start.9 = (bf16[64,1280]{1,0:T(8,128)(2,1)S(1)}, bf16[64,1280]{1,0:T(8,128)(2,1)S(1)}, u32[]{:S(2)}, u32[]{:S(2)}) collective-permute-start(bf16[64,1280]{1,0:T(8,128)(2,1)S(1)} %get-tuple-element.23), channel_id=1, source_target_pairs={{0,24},{8,16},{16,8},{24,0},{1,25},{9,17},{17,9},{25,1},{2,26},{10... | collective-permute-start | bytes 491528 | tf_op jit(solution)/shard_map/ppermute | solution.py:384
  45.8 3.2 %collective-permute-done.7.refs_1_ = bf16[64,1280]{1,0:T(8,128)(2,1)S(1)} collective-permute-done((bf16[64,1280]{1,0:T(8,128)(2,1)S(1)}, bf16[64,1280]{1,0:T(8,128)(2,1)S(1)}, u32[]{:S(2)}, u32[]{:S(2)}) %collective-permute-start.7) | collective-permute-done | bytes 163872 | tf_op jit(solution)/shard_map/ppermute | solution.py:384
  49.0 2.4 %collective-permute-done.8.refs_2_ = bf16[64,1280]{1,0:T(8,128)(2,1)S(1)} collective-permute-done((bf16[64,1280]{1,0:T(8,128)(2,1)S(1)}, bf16[64,1280]{1,0:T(8,128)(2,1)S(1)}, u32[]{:S(2)}, u32[]{:S(2)}) %collective-permute-start.8) | collective-permute-done | bytes 163872 | tf_op jit(solution)/shard_map/ppermute | solution.py:384
  51.4 0.0 collective-permute-done.9.refs_3_
  51.4 5.0 %share.3 = f32[4,512,256]{2,1,0:T(8,128)S(1)} custom-call(s32[4]{0:T(128)S(1)} %fusion.order_ref, bf16[64,1280]{1,0:T(8,128)(2,1)S(1)} %get-tuple-element.20.refs_0_, bf16[64,1280]{1,0:T(8,128)(2,1)S(1)} %collective-permute-done.7.refs_1_, bf16[64,1280]{1,0:T(8,128)(2,1)S(1)} %collective-permute-done.8.refs_2_, ...), custom_call_target="tpu_custom_call" | custom-call | flops 1342177280 | bytes 5242880 | tf_op jit(solution)/shard_map/share/pallas_call | solution.py:269
  56.4 0.1 collective-permute-start.10
  56.5 5.0 %share.2.a_ref = f32[4,512,256]{2,1,0:T(8,128)S(1)} custom-call(s32[4]{0:T(128)S(1)} %fusion.1.order_ref, bf16[64,1280]{1,0:T(8,128)(2,1)S(1)} %get-tuple-element.20.refs_0_, bf16[64,1280]{1,0:T(8,128)(2,1)S(1)} %collective-permute-done.7.refs_1_, bf16[64,1280]{1,0:T(8,128)(2,1)S(1)} %collective-permute-done.8.refs_2_, ...), custom_call_target="tpu_custom_call" | custom-call | flops 1342177280 | bytes 5242880 | tf_op jit(solution)/shard_map/share/pallas_call | solution.py:269
  61.5 0.0 collective-permute-done.10.b_ref
  61.5 0.0 copy-start
  61.5 0.2 encode.5
  61.7 0.5 collective-permute-start.16
  62.2 0.9 encode.4
  63.1 0.0 copy-start.6
  63.1 0.0 collective-permute-start.15
  63.1 0.0 copy-done
  63.1 0.9 encode.3
  64.0 3.9 %collective-permute-start.14 = (s16[528,256]{1,0:T(8,128)(2,1)}, s16[528,256]{1,0:T(8,128)(2,1)S(1)}, u32[]{:S(2)}, u32[]{:S(2)}) collective-permute-start(s16[528,256]{1,0:T(8,128)(2,1)} %encode.3), channel_id=1, source_target_pairs={{0,2},{1,3},{2,0},{3,1},{4,6},{5,7},{6,4},{7,5},{8,10},{9,11},{10,... | collective-permute-start | bytes 811016 | tf_op jit(solution)/shard_map/ppermute | solution.py:384
  67.9 1.3 %collective-permute-start.11 = (f32[16,128]{1,0:T(8,128)S(1)}, f32[16,128]{1,0:T(8,128)S(1)}, u32[]{:S(2)}, u32[]{:S(2)}) collective-permute-start(f32[16,128]{1,0:T(8,128)S(1)} %get-tuple-element.25), channel_id=1, source_target_pairs={{0,8},{8,0},{16,24},{24,16},{1,9},{9,1},{17,25},{25,17},{2,10},{10... | collective-permute-start | bytes 24584 | tf_op jit(solution)/shard_map/ppermute | solution.py:384
  69.2 0.9 collective-permute-start.12
  70.1 1.4 %collective-permute-done.11.refs_1_ = f32[16,128]{1,0:T(8,128)S(1)} collective-permute-done((f32[16,128]{1,0:T(8,128)S(1)}, f32[16,128]{1,0:T(8,128)S(1)}, u32[]{:S(2)}, u32[]{:S(2)}) %collective-permute-start.11) | collective-permute-done | bytes 8224 | tf_op jit(solution)/shard_map/ppermute | solution.py:384
  71.5 1.6 %collective-permute-start.13 = (f32[16,128]{1,0:T(8,128)S(1)}, f32[16,128]{1,0:T(8,128)S(1)}, u32[]{:S(2)}, u32[]{:S(2)}) collective-permute-start(f32[16,128]{1,0:T(8,128)S(1)} %get-tuple-element.27), channel_id=1, source_target_pairs={{0,24},{8,16},{16,8},{24,0},{1,25},{9,17},{17,9},{25,1},{2,26},{10... | collective-permute-start | bytes 24584 | tf_op jit(solution)/shard_map/ppermute | solution.py:384
  73.2 0.0 copy-done.6
  73.2 0.1 copy.7.col_ref
  73.3 0.0 collective-permute-done.12.refs_2_
  73.3 2.7 %collective-permute-done.13.refs_3_ = f32[16,128]{1,0:T(8,128)S(1)} collective-permute-done((f32[16,128]{1,0:T(8,128)S(1)}, f32[16,128]{1,0:T(8,128)S(1)}, u32[]{:S(2)}, u32[]{:S(2)}) %collective-permute-start.13) | collective-permute-done | bytes 8224 | tf_op jit(solution)/shard_map/ppermute | solution.py:384
  76.1 0.0 collective-permute-done.16.refs_6_
  76.1 10.0 %collective-permute-done.15.refs_5_ = s16[528,256]{1,0:T(8,128)(2,1)S(1)} collective-permute-done((s16[528,256]{1,0:T(8,128)(2,1)}, s16[528,256]{1,0:T(8,128)(2,1)S(1)}, u32[]{:S(2)}, u32[]{:S(2)}) %collective-permute-start.15) | collective-permute-done | bytes 270368 | tf_op jit(solution)/shard_map/ppermute | solution.py:384
  86.1 0.0 collective-permute-done.14.refs_4_
  86.1 0.0 copy-start.1
  86.1 1.6 %copy-done.1 = f32[4,512,256]{2,1,0:T(8,128)S(1)} copy-done((f32[4,512,256]{2,1,0:T(8,128)S(1)}, f32[4,512,256]{2,1,0:T(8,128)}, u32[]{:S(2)}) %copy-start.1) | copy-done | bytes 2097176
  87.7 2.2 %finish.1 = (f32[1,512,512]{2,1,0:T(8,128)}, f32[1,512]{1,0:T(1,128)}) custom-call(s32[1]{0:T(128)} %bitcast.own_ref, s32[1,512]{1,0:T(1,128)S(1)} %bitcast.7, s32[512,1]{1,0:T(8,128)S(1)} %copy.7.col_ref, f32[4,512,256]{2,1,0:T(8,128)S(1)} %share.2.a_ref, f32[4,512,256]{2,1,0:T(8,128)S(1)} %copy-done.1, f32[16,128]{1,0:T(8,128)S(1)} %get-tuple-element.24.refs_0_, ...), custom_call_target="tpu_custom_call" | custom-call | flops 402653184 | bytes 1048576 | tf_op jit(solution)/shard_map/finish/pallas_call | solution.py:364
  (2 shorter events, 0.0 us)
Async XLA Ops:
  0.6 2.2 %copy-start.2 = (bf16[1,512,4096]{2,1,0:T(8,128)(2,1)S(1)}, bf16[1,512,4096]{2,1,0:T(8,128)(2,1)}, u32[]{:S(2)}) copy-start(bf16[1,512,4096]{2,1,0:T(8,128)(2,1)} %hid_ref.1) | copy-start | bytes 12582916
  2.8 0.7 copy-start.5
  3.5 0.7 copy-start.7
  14.4 8.0 %collective-permute-start = (bf16[64,1280]{1,0:T(8,128)(2,1)S(1)}, bf16[64,1280]{1,0:T(8,128)(2,1)S(1)}, u32[]{:S(2)}, u32[]{:S(2)}) collective-permute-start(bf16[64,1280]{1,0:T(8,128)(2,1)S(1)} %get-tuple-element.17), channel_id=1, source_target_pairs={{0,8},{8,0},{16,24},{24,16},{1,9},{9,1},{17,25},{25,17},{2,10},{10... | collective-permute-start | bytes 491528 | tf_op jit(solution)/shard_map/ppermute | solution.py:384
  17.4 9.2 %collective-permute-start.1 = (bf16[64,1280]{1,0:T(8,128)(2,1)S(1)}, bf16[64,1280]{1,0:T(8,128)(2,1)S(1)}, u32[]{:S(2)}, u32[]{:S(2)}) collective-permute-start(bf16[64,1280]{1,0:T(8,128)(2,1)S(1)} %get-tuple-element.18), channel_id=1, source_target_pairs={{0,16},{8,24},{16,0},{24,8},{1,17},{9,25},{17,1},{25,9},{2,18},{10... | collective-permute-start | bytes 491528 | tf_op jit(solution)/shard_map/ppermute | solution.py:384
  19.0 7.7 %collective-permute-start.2 = (bf16[64,1280]{1,0:T(8,128)(2,1)S(1)}, bf16[64,1280]{1,0:T(8,128)(2,1)S(1)}, u32[]{:S(2)}, u32[]{:S(2)}) collective-permute-start(bf16[64,1280]{1,0:T(8,128)(2,1)S(1)} %get-tuple-element.19), channel_id=1, source_target_pairs={{0,24},{8,16},{16,8},{24,0},{1,25},{9,17},{17,9},{25,1},{2,26},{10... | collective-permute-start | bytes 491528 | tf_op jit(solution)/shard_map/ppermute | solution.py:384
  27.5 1.3 %copy-start.4 = (f32[32,128]{1,0:T(8,128)}, f32[32,128]{1,0:T(8,128)S(1)}, u32[]{:S(2)}) copy-start(f32[32,128]{1,0:T(8,128)S(1)} %stats.1.refs_0_) | copy-start | bytes 49156
  27.5 1.2 %collective-permute-start.3 = (f32[32,128]{1,0:T(8,128)S(1)}, f32[32,128]{1,0:T(8,128)S(1)}, u32[]{:S(2)}, u32[]{:S(2)}) collective-permute-start(f32[32,128]{1,0:T(8,128)S(1)} %stats.1.refs_0_), channel_id=1, source_target_pairs={{0,1},{1,0},{2,3},{3,2},{4,5},{5,4},{6,7},{7,6},{8,9},{9,8},{10,11... | collective-permute-start | bytes 49160 | tf_op jit(solution)/shard_map/ppermute | solution.py:384
  28.7 0.6 copy-start.8
  30.7 4.4 %collective-permute-start.4 = (f32[32,128]{1,0:T(8,128)}, f32[32,128]{1,0:T(8,128)S(1)}, u32[]{:S(2)}, u32[]{:S(2)}) collective-permute-start(f32[32,128]{1,0:T(8,128)} %merge.1.refs_0_), channel_id=1, source_target_pairs={{0,2},{1,3},{2,0},{3,1},{4,6},{5,7},{6,4},{7,5},{8,10},{9,11},{10,... | collective-permute-start | bytes 49160 | tf_op jit(solution)/shard_map/ppermute | solution.py:384
  32.3 4.9 %collective-permute-start.5 = (f32[32,128]{1,0:T(8,128)}, f32[32,128]{1,0:T(8,128)S(1)}, u32[]{:S(2)}, u32[]{:S(2)}) collective-permute-start(f32[32,128]{1,0:T(8,128)} %merge.1.refs_0_), channel_id=1, source_target_pairs={{0,4},{1,5},{2,6},{3,7},{4,0},{5,1},{6,2},{7,3},{8,12},{9,13},{10,... | collective-permute-start | bytes 49160 | tf_op jit(solution)/shard_map/ppermute | solution.py:384
  34.9 5.7 %collective-permute-start.6 = (f32[32,128]{1,0:T(8,128)}, f32[32,128]{1,0:T(8,128)S(1)}, u32[]{:S(2)}, u32[]{:S(2)}) collective-permute-start(f32[32,128]{1,0:T(8,128)} %merge.1.refs_0_), channel_id=1, source_target_pairs={{0,6},{1,7},{2,4},{3,5},{4,2},{5,3},{6,0},{7,1},{8,14},{9,15},{10,... | collective-permute-start | bytes 49160 | tf_op jit(solution)/shard_map/ppermute | solution.py:384
  40.6 0.7 copy-start.3
  42.2 6.8 %collective-permute-start.7 = (bf16[64,1280]{1,0:T(8,128)(2,1)S(1)}, bf16[64,1280]{1,0:T(8,128)(2,1)S(1)}, u32[]{:S(2)}, u32[]{:S(2)}) collective-permute-start(bf16[64,1280]{1,0:T(8,128)(2,1)S(1)} %get-tuple-element.21), channel_id=1, source_target_pairs={{0,8},{8,0},{16,24},{24,16},{1,9},{9,1},{17,25},{25,17},{2,10},{10... | collective-permute-start | bytes 491528 | tf_op jit(solution)/shard_map/ppermute | solution.py:384
  43.5 7.9 %collective-permute-start.8 = (bf16[64,1280]{1,0:T(8,128)(2,1)S(1)}, bf16[64,1280]{1,0:T(8,128)(2,1)S(1)}, u32[]{:S(2)}, u32[]{:S(2)}) collective-permute-start(bf16[64,1280]{1,0:T(8,128)(2,1)S(1)} %get-tuple-element.22), channel_id=1, source_target_pairs={{0,16},{8,24},{16,0},{24,8},{1,17},{9,25},{17,1},{25,9},{2,18},{10... | collective-permute-start | bytes 491528 | tf_op jit(solution)/shard_map/ppermute | solution.py:384
  44.4 7.1 %collective-permute-start.9 = (bf16[64,1280]{1,0:T(8,128)(2,1)S(1)}, bf16[64,1280]{1,0:T(8,128)(2,1)S(1)}, u32[]{:S(2)}, u32[]{:S(2)}) collective-permute-start(bf16[64,1280]{1,0:T(8,128)(2,1)S(1)} %get-tuple-element.23), channel_id=1, source_target_pairs={{0,24},{8,16},{16,8},{24,0},{1,25},{9,17},{17,9},{25,1},{2,26},{10... | collective-permute-start | bytes 491528 | tf_op jit(solution)/shard_map/ppermute | solution.py:384
  56.4 5.1 %collective-permute-start.10 = (f32[4,512,256]{2,1,0:T(8,128)S(1)}, f32[4,512,256]{2,1,0:T(8,128)S(1)}, u32[]{:S(2)}, u32[]{:S(2)}) collective-permute-start(f32[4,512,256]{2,1,0:T(8,128)S(1)} %share.3), channel_id=1, source_target_pairs={{0,1},{1,0},{2,3},{3,2},{4,5},{5,4},{6,7},{7,6},{8,9},{9,8},{10,11... | collective-permute-start | bytes 6291464 | tf_op jit(solution)/shard_map/ppermute | solution.py:384
  61.5 1.6 %copy-start = (f32[4,512,256]{2,1,0:T(8,128)}, f32[4,512,256]{2,1,0:T(8,128)S(1)}, u32[]{:S(2)}) copy-start(f32[4,512,256]{2,1,0:T(8,128)S(1)} %collective-permute-done.10.b_ref) | copy-start | bytes 6291460
  61.7 14.4 %collective-permute-start.16 = (s16[528,256]{1,0:T(8,128)(2,1)S(1)}, s16[528,256]{1,0:T(8,128)(2,1)S(1)}, u32[]{:S(2)}, u32[]{:S(2)}) collective-permute-start(s16[528,256]{1,0:T(8,128)(2,1)S(1)} %encode.5), channel_id=1, source_target_pairs={{0,6},{1,7},{2,4},{3,5},{4,2},{5,3},{6,0},{7,1},{8,14},{9,15},{10,... | collective-permute-start | bytes 811016 | tf_op jit(solution)/shard_map/ppermute | solution.py:384
  63.1 10.1 %copy-start.6 = (s32[512]{0:T(512)S(1)}, s32[512]{0:T(512)}, u32[]{:S(2)}) copy-start(s32[512]{0:T(512)} %param.7) | copy-start | bytes 6148
  63.1 23.0 %collective-permute-start.15 = (s16[528,256]{1,0:T(8,128)(2,1)}, s16[528,256]{1,0:T(8,128)(2,1)S(1)}, u32[]{:S(2)}, u32[]{:S(2)}) collective-permute-start(s16[528,256]{1,0:T(8,128)(2,1)} %encode.4), channel_id=1, source_target_pairs={{0,4},{1,5},{2,6},{3,7},{4,0},{5,1},{6,2},{7,3},{8,12},{9,13},{10,... | collective-permute-start | bytes 811016 | tf_op jit(solution)/shard_map/ppermute | solution.py:384
  64.0 22.1 %collective-permute-start.14 = (s16[528,256]{1,0:T(8,128)(2,1)}, s16[528,256]{1,0:T(8,128)(2,1)S(1)}, u32[]{:S(2)}, u32[]{:S(2)}) collective-permute-start(s16[528,256]{1,0:T(8,128)(2,1)} %encode.3), channel_id=1, source_target_pairs={{0,2},{1,3},{2,0},{3,1},{4,6},{5,7},{6,4},{7,5},{8,10},{9,11},{10,... | collective-permute-start | bytes 811016 | tf_op jit(solution)/shard_map/ppermute | solution.py:384
  67.9 3.7 %collective-permute-start.11 = (f32[16,128]{1,0:T(8,128)S(1)}, f32[16,128]{1,0:T(8,128)S(1)}, u32[]{:S(2)}, u32[]{:S(2)}) collective-permute-start(f32[16,128]{1,0:T(8,128)S(1)} %get-tuple-element.25), channel_id=1, source_target_pairs={{0,8},{8,0},{16,24},{24,16},{1,9},{9,1},{17,25},{25,17},{2,10},{10... | collective-permute-start | bytes 24584 | tf_op jit(solution)/shard_map/ppermute | solution.py:384
  69.2 4.1 %collective-permute-start.12 = (f32[16,128]{1,0:T(8,128)S(1)}, f32[16,128]{1,0:T(8,128)S(1)}, u32[]{:S(2)}, u32[]{:S(2)}) collective-permute-start(f32[16,128]{1,0:T(8,128)S(1)} %get-tuple-element.26), channel_id=1, source_target_pairs={{0,16},{8,24},{16,0},{24,8},{1,17},{9,25},{17,1},{25,9},{2,18},{10... | collective-permute-start | bytes 24584 | tf_op jit(solution)/shard_map/ppermute | solution.py:384
  71.5 4.5 %collective-permute-start.13 = (f32[16,128]{1,0:T(8,128)S(1)}, f32[16,128]{1,0:T(8,128)S(1)}, u32[]{:S(2)}, u32[]{:S(2)}) collective-permute-start(f32[16,128]{1,0:T(8,128)S(1)} %get-tuple-element.27), channel_id=1, source_target_pairs={{0,24},{8,16},{16,8},{24,0},{1,25},{9,17},{17,9},{25,1},{2,26},{10... | collective-permute-start | bytes 24584 | tf_op jit(solution)/shard_map/ppermute | solution.py:384
  86.1 1.6 %copy-start.1 = (f32[4,512,256]{2,1,0:T(8,128)S(1)}, f32[4,512,256]{2,1,0:T(8,128)}, u32[]{:S(2)}) copy-start(f32[4,512,256]{2,1,0:T(8,128)} %copy-done) | copy-start | bytes 6291460

commit v2 on v0

v2 whole, which is shorter than its diff:
```python
import functools
import jax
import jax.numpy as jnp
from jax import lax
from jax.experimental import pallas as pl
from jax.experimental.pallas import tpu as pltpu
from jax.sharding import PartitionSpec as P

SEGS = 8
IGNORED = 256
GROUP = 16
LANES = 128
PLAIN_CHUNKS = 4
IN_FLIGHT = 4
LOSS_TERMS = 3
CODE_ROWS = 16
CODE_STEPS = 64.0
CODE_TOP = 32766.0
LARGE = pltpu.CompilerParams(vmem_limit_bytes=32 * 1024 * 1024)
SMALL = pltpu.CompilerParams(vmem_limit_bytes=16 * 1024 * 1024)


def lane_ids(rows):
    return lax.broadcasted_iota(jnp.int32, (rows, LANES), 1)


def wanted_ranks(first, count, own, block):
    row = lax.broadcasted_iota(jnp.int32, (count, 1), 0) + first
    return (own ^ (row // block)) * block + row % block + 1


def ranks_along(labels):
    tokens = labels.shape[1]
    on = labels >= 0
    flags = jnp.broadcast_to(on.astype(jnp.float32), (8, tokens)).astype(jnp.bfloat16)
    src = lax.broadcasted_iota(jnp.int32, (tokens, tokens), 0)
    dst = lax.broadcasted_iota(jnp.int32, (tokens, tokens), 1)
    upto = (src <= dst).astype(jnp.float32).astype(jnp.bfloat16)
    rank = jnp.dot(flags, upto, preferred_element_type=jnp.float32)[0:1, :].astype(jnp.int32)
    return jnp.where(on, rank, 0)


def project_kernel(chunk_start, own_ref, shard_ref, lab_hbm, seg_hbm, hid_hbm, w_hbm, mine_ref, theirs_ref, meta_ref, *rest):
    out_refs, (lab_ref, seg_ref, hid_ref, few_ref, acc_ref, small_sem, hid_sem, w_sem) = rest[:-8], rest[-8:]
    tokens, depth = hid_ref.shape
    rows = few_ref.shape[0]
    block = out_refs[0].shape[0]
    part = depth // hid_sem.shape[0]
    spans = [pl.ds(n, part) for n in range(0, depth, part)]
    count, chunk, _ = mine_ref.shape
    targets = [(theirs_ref, 1, n) for n in range(count)] + [(mine_ref, 0, n) for n in range(count)]
    starts = [chunk_start(shard_ref[0], slot, n) for _, slot, n in targets]
    small = [
        pltpu.make_async_copy(lab_hbm, lab_ref, small_sem.at[0]),
        pltpu.make_async_copy(seg_hbm, seg_ref, small_sem.at[1]),
    ]
    hid_copies = [
        pltpu.make_async_copy(hid_hbm.at[0, :, span], hid_ref.at[:, span], hid_sem.at[n])
        for n, span in enumerate(spans)
    ]
    w_copies = [
        pltpu.make_async_copy(w_hbm.at[0, pl.ds(start, chunk), :], ref.at[n], w_sem.at[m])
        for m, (start, (ref, _, n)) in enumerate(zip(starts, targets))
    ]
    queue = small + hid_copies + w_copies
    for copy in queue[: 2 + IN_FLIGHT]:
        copy.start()
    queue = queue[2 + IN_FLIGHT :]
    for copy in small:
        copy.wait()

    lab = lab_ref[...]
    seg = seg_ref[...]
    rank = ranks_along(lab)
    pick = rank == wanted_ranks(0, rows, own_ref[0], block)
    picker = pick.astype(jnp.float32).astype(jnp.bfloat16)
    for copy, span in zip(hid_copies, spans):
        copy.wait()
        if queue:
            queue.pop(0).start()
        few = jnp.dot(picker, hid_ref[:, span], preferred_element_type=jnp.float32)
        few_ref[:, span] = few.astype(jnp.bfloat16)

    mine = pick[:block, :]
    label = jnp.sum(jnp.where(mine, lab, 0).astype(jnp.float32), axis=1, keepdims=True)
    doc = jnp.sum(jnp.where(mine, seg, 0).astype(jnp.float32), axis=1, keepdims=True)
    same = (lab >= 0) & (seg.astype(jnp.float32) == doc)
    count = jnp.sum(jnp.where(same, 1.0, 0.0), axis=1, keepdims=True)
    weight = float(tokens) / (SEGS * jnp.maximum(count, 1.0))
    lane = lane_ids(block)
    meta_ref[...] = jnp.where(lane == 0, label, jnp.where(lane == 1, weight, 0.0))

    for m, (copy, start, (ref, _, n)) in enumerate(zip(w_copies, starts, targets)):
        copy.wait()
        if queue:
            queue.pop(0).start()
        term = jnp.dot(few_ref[:, pl.ds(start, chunk)], ref[n], preferred_element_type=jnp.float32)
        if m == 0:
            acc_ref[...] = term
        elif m < len(targets) - 1:
            acc_ref[...] += term
        else:
            logits = (acc_ref[...] + term).astype(jnp.bfloat16)
            for k, out_ref in enumerate(out_refs):
                out_ref[...] = logits[k * block : (k + 1) * block, :]


def project(ids, labels, segments, hidden, head_weight, peers, chunk_start, count):
    tokens, depth = hidden.shape[1:]
    width = head_weight.shape[2]
    rows = tokens - IGNORED
    block = rows // peers
    hbm = pl.BlockSpec(memory_space=pltpu.HBM)
    vmem = pl.BlockSpec(memory_space=pltpu.VMEM)
    return pl.pallas_call(
        functools.partial(project_kernel, chunk_start),
        in_specs=[pl.BlockSpec(memory_space=pltpu.SMEM)] * 2 + [hbm] * 4,
        out_specs=[vmem] * (3 + peers),
        out_shape=[jax.ShapeDtypeStruct((count, depth // (2 * count), width), jnp.bfloat16)] * 2
        + [jax.ShapeDtypeStruct((block, LANES), jnp.float32)]
        + [jax.ShapeDtypeStruct((block, width), jnp.bfloat16)] * peers,
        scratch_shapes=[
            pltpu.VMEM((1, tokens), jnp.int32),
            pltpu.VMEM((1, tokens), jnp.int32),
            pltpu.VMEM((tokens, depth), jnp.bfloat16),
            pltpu.VMEM((rows, depth), jnp.bfloat16),
            pltpu.VMEM((rows, width), jnp.float32),
            pltpu.SemaphoreType.DMA((2,)),
            pltpu.SemaphoreType.DMA((4,)),
            pltpu.SemaphoreType.DMA((2 * count,)),
        ],
        compiler_params=LARGE,
        cost_estimate=pl.CostEstimate(
            flops=2 * rows * depth * (width + tokens), bytes_accessed=0, transcendentals=0
        ),
        name="project",
    )(*ids, labels, segments, hidden, head_weight)


def pair_list(peers):
    return [(i, j) for i in range(peers) for j in range(peers) if i != j]


def stat_slots(peers):
    pairs = pair_list(peers)
    return peers, {p: peers + n for n, p in enumerate(pairs)}, peers + len(pairs)


def stats_kernel(own_ref, shard_ref, meta_ref, *refs):
    logit_refs, out_ref = refs[:-1], refs[-1]
    peers = len(logit_refs)
    block, width = logit_refs[0].shape
    _, pair_slot, target_slot = stat_slots(peers)
    span = LANES * GROUP // block
    lane = lane_ids(GROUP)
    sums = jnp.zeros((GROUP, LANES), jnp.float32)
    peaks = jnp.zeros((GROUP, LANES), jnp.float32)
    for g in range(block // GROUP):
        rows = slice(g * GROUP, (g + 1) * GROUP)
        label = meta_ref[rows, 0:1].astype(jnp.int32) - shard_ref[0] * width
        peak = []
        for ref in logit_refs:
            top = ref[rows, 0:LANES].astype(jnp.float32)
            for c in range(LANES, width, LANES):
                top = jnp.maximum(top, ref[rows, c : c + LANES].astype(jnp.float32))
            peak.append(jnp.max(top, axis=1, keepdims=True))
        total = [jnp.zeros((GROUP, LANES), jnp.float32) for _ in range(peers)]
        target = [jnp.zeros((GROUP, LANES), jnp.float32) for _ in range(peers)]
        cross = {p: jnp.zeros((GROUP, LANES), jnp.float32) for p in pair_slot}
        for c in range(0, width, LANES):
            l = [ref[rows, c : c + LANES].astype(jnp.float32) for ref in logit_refs]
            e = [jnp.exp(l[k] - peak[k]) for k in range(peers)]
            hit = (lane + c) == label
            for i in range(peers):
                total[i] += e[i]
                target[i] += jnp.where(hit, l[i], 0.0)
                for j in range(i + 1, peers):
                    gap = l[i] - l[j]
                    cross[i, j] += e[i] * gap
                    cross[j, i] -= e[j] * gap

        def put(slot, vals, top):
            nonlocal sums, peaks
            here = lane == g * span + slot
            sums = jnp.where(here, jnp.sum(vals, axis=1, keepdims=True), sums)
            if top is not None:
                peaks = jnp.where(here, top, peaks)

        for i in range(peers):
            put(i, total[i], peak[i])
            put(target_slot + i, target[i], None)
        for (i, j), slot in pair_slot.items():
            put(slot, cross[i, j], peak[i])
    out_ref[0:GROUP, :] = sums
    out_ref[GROUP : 2 * GROUP, :] = peaks


def stats(ids, meta, logits):
    block, width = logits[0].shape
    peers = len(logits)
    return pl.pallas_call(
        stats_kernel,
        in_specs=[pl.BlockSpec(memory_space=pltpu.SMEM)] * 2 + [pl.BlockSpec(memory_space=pltpu.VMEM)] * (1 + peers),
        out_shape=jax.ShapeDtypeStruct((2 * GROUP, LANES), jnp.float32),
        compiler_params=SMALL,
        cost_estimate=pl.CostEstimate(
            flops=40 * block * width * peers, bytes_accessed=2 * block * width * peers, transcendentals=block * width * peers
        ),
        name="stats",
    )(*ids, meta, *logits)


def merged(parts):
    top = parts[0][GROUP:, :]
    for part in parts[1:]:
        top = jnp.maximum(top, part[GROUP:, :])
    total = jnp.zeros_like(top)
    for part in parts:
        total += part[:GROUP, :] * jnp.exp(part[GROUP:, :] - top)
    return total, top


def merge_kernel(*refs):
    total, top = merged([ref[...] for ref in refs[:-1]])
    refs[-1][:GROUP, :] = total
    refs[-1][GROUP:, :] = top


def merge(parts):
    return pl.pallas_call(
        merge_kernel,
        in_specs=[pl.BlockSpec(memory_space=pltpu.VMEM)] * len(parts),
        out_shape=jax.ShapeDtypeStruct(parts[0].shape, jnp.float32),
        compiler_params=SMALL,
        name="merge",
    )(*parts)


def grad_kernel(count, own_ref, shard_ref, meta_ref, *refs):
    stat_refs, refs = refs[:count], refs[count:]
    peers = len(refs) // 2
    logit_refs, grad_refs = refs[:peers], refs[peers:]
    block, width = logit_refs[0].shape
    _, pair_slot, target_slot = stat_slots(peers)
    span = LANES * GROUP // block
    lane = lane_ids(GROUP)
    total, top = merged([ref[...] for ref in stat_refs])
    norm = top + jnp.log(jnp.maximum(total, 1e-37))
    third = 1.0 / (peers - 1)
    for g in range(block // GROUP):
        rows = slice(g * GROUP, (g + 1) * GROUP)
        at = lambda array, slot: array[:, g * span + slot : g * span + slot + 1]
        label = meta_ref[rows, 0:1].astype(jnp.int32) - shard_ref[0] * width
        weight = meta_ref[rows, 1:2]
        inverse = [1.0 / at(total, i) for i in range(peers)]
        norms = [at(norm, i) for i in range(peers)]
        mean = {p: at(total, slot) * inverse[p[0]] for p, slot in pair_slot.items()}
        shift = []
        for i in range(peers):
            ahead = sum(mean[i, j] for j in range(peers) if j != i)
            back = sum(mean[j, i] for j in range(peers) if j != i)
            loss = norms[i] - at(total, target_slot + i) + (ahead + back) * third
            terms = jnp.zeros((GROUP, LANES), jnp.float32)
            for n in range(LOSS_TERMS):
                term = loss.astype(jnp.bfloat16).astype(jnp.float32)
                loss = loss - term
                terms = jnp.where(lane == n, term, terms)
            grad_refs[i][rows, width:] = terms.astype(jnp.bfloat16)
            shift.append(1.0 + (peers - ahead) * third)
        for c in range(0, width, LANES):
            l = [ref[rows, c : c + LANES].astype(jnp.float32) for ref in logit_refs]
            p = [jnp.exp(l[k] - norms[k]) for k in range(peers)]
            common = sum(l) * third
            rest = sum(p) * third + jnp.where((lane + c) == label, 1.0, 0.0)
            for i in range(peers):
                grad = p[i] * (shift[i] + (l[i] * (peers * third) - common)) - rest
                grad_refs[i][rows, c : c + LANES] = (weight * grad).astype(jnp.bfloat16)


def gradients(ids, meta, parts, logits):
    block, width = logits[0].shape
    peers = len(logits)
    return pl.pallas_call(
        functools.partial(grad_kernel, len(parts)),
        in_specs=[pl.BlockSpec(memory_space=pltpu.SMEM)] * 2
        + [pl.BlockSpec(memory_space=pltpu.VMEM)] * (1 + len(parts) + peers),
        out_shape=[jax.ShapeDtypeStruct((block, width + LANES), jnp.bfloat16)] * peers,
        compiler_params=SMALL,
        cost_estimate=pl.CostEstimate(
            flops=20 * block * width * peers, bytes_accessed=4 * block * width * peers, transcendentals=block * width * peers
        ),
        name="gradients",
    )(*ids, meta, *parts, *logits)


def share_of(w_ref, index, grad):
    return lax.dot_general(w_ref[index], grad, (((1,), (1,)), ((), ())), preferred_element_type=jnp.float32)


def both_shares(mask, shard_ref, refs):
    mine_ref, theirs_ref, own_ref, other_ref = refs
    index = (shard_ref[0] // 2) ^ mask
    return share_of(mine_ref, index, own_ref[...]) + share_of(theirs_ref, index, other_ref[...])


def gather_kernel(peers, own_ref, shard_ref, *refs):
    block_refs, (own_all, other_all, loss_ref) = refs[:-3], refs[-3:]
    block, width = block_refs[0].shape[0], own_all.shape[1]
    for k in range(peers):
        rows = slice(k * block, (k + 1) * block)
        own_all[rows, :] = block_refs[k][:, :width]
        other_all[rows, :] = block_refs[peers + k][:, :width]
        loss_ref[rows, :] = jnp.sum(block_refs[k][:, width:].astype(jnp.float32), axis=1, keepdims=True)


def vmem_call(kernel, outs, cost, name, ids, *arrays):
    return pl.pallas_call(
        kernel,
        in_specs=[pl.BlockSpec(memory_space=pltpu.SMEM)] * 2 + [pl.BlockSpec(memory_space=pltpu.VMEM)] * len(arrays),
        out_specs=[pl.BlockSpec(memory_space=pltpu.VMEM)] * len(outs),
        out_shape=[jax.ShapeDtypeStruct(shape, dtype) for shape, dtype in outs],
        compiler_params=SMALL,
        cost_estimate=cost,
        name=name,
    )(*ids, *arrays)


def coded(value):
    depth, rows = value.shape
    top = jnp.maximum(jnp.max(jnp.abs(value), axis=0, keepdims=True), 1e-30)
    code = jnp.ceil(jnp.log2(top) * CODE_STEPS)
    unit = jnp.exp2(code * (-1.0 / CODE_STEPS)) * CODE_TOP
    whole = jnp.clip(jnp.round(value * unit), -CODE_TOP - 1, CODE_TOP + 1)
    codes = jnp.broadcast_to(code, (CODE_ROWS, rows))
    return whole.astype(jnp.int32).astype(jnp.int16), codes.astype(jnp.int32).astype(jnp.int16)


def put_coded(ref, value):
    depth = value.shape[0]
    ref[:depth, :], ref[depth:, :] = coded(value)


def get_coded(ref):
    depth = ref.shape[0] - CODE_ROWS
    code = ref[depth:, :].astype(jnp.int32).astype(jnp.float32)[0:1, :]
    unit = jnp.exp2(code * (1.0 / CODE_STEPS)) * (1.0 / CODE_TOP)
    return ref[:depth, :].astype(jnp.int32).astype(jnp.float32) * unit


def encode_kernel(mask, own_ref, shard_ref, *refs):
    value = both_shares(mask, shard_ref, refs[:4])
    put_coded(refs[4], value)
    for ref in refs[5:]:
        ref[...] = value


def relay_kernel(own_ref, shard_ref, value_ref, coded_ref, out_ref):
    put_coded(out_ref, value_ref[...] + get_coded(coded_ref))


def keep_kernel(own_ref, shard_ref, *refs):
    refs[-1][...] = both_shares(0, shard_ref, refs[:-1])


def place_kernel(peers, own_ref, shard_ref, row_ref, loss_ref, place_ref, out_ref):
    tokens, rows = place_ref.shape
    block = rows // peers
    rank = ranks_along(row_ref[...])
    here = rank == wanted_ranks(0, rows, own_ref[0], block)
    out_ref[...] = jnp.sum(jnp.where(here, loss_ref[...], 0.0), axis=0, keepdims=True)

    src = lax.broadcasted_iota(jnp.int32, (tokens, tokens), 0)
    dst = lax.broadcasted_iota(jnp.int32, (tokens, tokens), 1)
    flags = (row_ref[...] >= 0).astype(jnp.float32).astype(jnp.bfloat16)
    flags = jnp.broadcast_to(flags, (LANES, tokens))
    turned = lambda keep: lax.dot_general(
        keep.astype(jnp.float32).astype(jnp.bfloat16),
        flags,
        (((1,), (1,)), ((), ())),
        preferred_element_type=jnp.float32,
    )[:, 0:1]
    rank = (turned(dst <= src) * turned(dst == src)).astype(jnp.int32)
    col = lax.broadcasted_iota(jnp.int32, (1, rows), 1)
    wanted = (own_ref[0] ^ (col // block)) * block + col % block + 1
    place_ref[...] = (rank == wanted).astype(jnp.float32).astype(jnp.bfloat16)


def place(ids, labels, losses, peers):
    tokens = labels.shape[1]
    return vmem_call(
        functools.partial(place_kernel, peers),
        [((tokens, tokens - IGNORED), jnp.bfloat16), ((1, tokens), jnp.float32)],
        pl.CostEstimate(flops=4 * tokens * tokens * LANES, bytes_accessed=0, transcendentals=0),
        "place",
        ids,
        labels,
        losses,
    )


def finish_kernel(own_ref, shard_ref, place_ref, sum_ref, *refs):
    value = sum_ref[...]
    for ref in refs[:-1]:
        value += get_coded(ref)
    result = None
    for _ in range(3):
        piece = value.astype(jnp.bfloat16)
        value = value - piece.astype(jnp.float32)
        term = lax.dot_general(
            place_ref[...], piece, (((1,), (1,)), ((), ())), preferred_element_type=jnp.float32
        )
        result = term if result is None else result + term
    refs[-1][0] = result


def swap(array, axis, size, mask):
    return lax.ppermute(array, axis, [(i, i ^ mask) for i in range(size)])


def hop(array, pairs):
    return lax.ppermute(array, "vocab", [(2 * a + c, 2 * b + c) for a, b in pairs for c in range(2)])


def on_device(hidden, head_weight, labels, segments):
    peers = lax.axis_size("peer")
    shards = lax.axis_size("vocab")
    width = head_weight.shape[2]
    depth = head_weight.shape[1] // shards
    tokens = labels.shape[0]
    rows = tokens - IGNORED
    chips = shards // 2
    labels, segments = labels[None, :], segments[None, :]
    ids = [lax.axis_index(name).astype(jnp.int32).reshape(1) for name in ("peer", "vocab")]
    by_core = depth % LANES == 0

    def chunk_start(shard, slot, n):
        if by_core:
            return pl.multiple_of((2 * n + ((shard % 2) ^ slot)) * depth, depth)
        return (n + slot * PLAIN_CHUNKS) * (head_weight.shape[1] // (2 * PLAIN_CHUNKS))

    in_hbm = [pltpu.with_memory_space_constraint(x, pltpu.HBM) for x in (labels, segments, hidden, head_weight)]
    w_mine, w_theirs, meta, *blocks = project(
        ids, *in_hbm, peers, chunk_start, chips if by_core else PLAIN_CHUNKS
    )

    def across(arrays):
        moved = {k: swap(arrays[k], "peer", peers, k) for k in range(peers - 1, 0, -1)}
        return [arrays[0]] + [moved[k] for k in range(1, peers)]

    core_swap = lambda array: swap(array, "vocab", shards, 1)
    logits = across(blocks)
    part = stats(ids, meta, logits)
    part = merge([part, core_swap(part)])
    parts = [part] + [swap(part, "vocab", shards, 2 * mask) for mask in range(1, chips)]
    grads = across(gradients(ids, meta, parts, logits))

    cost = pl.CostEstimate(flops=1000, bytes_accessed=0, transcendentals=0)
    flat = ((rows, width), jnp.bfloat16)
    kernel = functools.partial(gather_kernel, peers)
    outs = [flat, flat, ((rows, 1), jnp.float32)]
    others = [core_swap(grad) for grad in grads]
    own_grad, other_grad, losses = vmem_call(kernel, outs, cost, "gather", ids, *grads, *others)
    placing, token_loss = place(ids, labels, losses, peers)
    if by_core:
        operands = (w_mine, core_swap(w_theirs), own_grad, other_grad)
        coded_shape, full = ((depth + CODE_ROWS, rows), jnp.int16), ((depth, rows), jnp.float32)

        def encode(mask, *more):
            kernel = functools.partial(encode_kernel, mask)
            return vmem_call(kernel, [coded_shape, *more], cost, "encode", ids, *operands)

        if chips == 4:
            (three,) = encode(3)
            far, mid = hop(three, [(0, 1), (3, 2)]), hop(three, [(1, 2), (2, 1)])
            two, two_sum = encode(2, full)
            skip = hop(two, [(0, 2), (3, 1)])
            (one,) = encode(1)
            (relayed,) = vmem_call(relay_kernel, [coded_shape], cost, "relay", ids, two_sum, far)
            relay = hop(relayed, [(1, 3), (2, 0)])
            one = lax.optimization_barrier((one, relayed))[0]
            near = hop(one, [(0, 1), (1, 0), (2, 3), (3, 2)])
            arrived = [mid, skip, relay, near]
        else:
            arrived = [swap(encode(mask)[0], "vocab", shards, 2 * mask) for mask in range(chips - 1, 0, -1)]
        (kept,) = vmem_call(keep_kernel, [((depth, rows), jnp.float32)], cost, "keep", ids, *operands)
    else:
        arrived = []
        share = lax.dot_general(
            head_weight[0], own_grad, (((1,), (1,)), ((), ())), preferred_element_type=jnp.float32
        )
        kept = lax.psum_scatter(share, "vocab", scatter_dimension=0, tiled=True)
    out = ((1, tokens, depth), jnp.float32)
    (grad_hidden,) = vmem_call(finish_kernel, [out], cost, "finish", ids, placing, kept, *arrived)
    return grad_hidden, token_loss


def solution(mesh):
    in_specs = (P("peer", None, None), P("peer", None, "vocab"), P(), P())
    out_specs = (P("peer", None, "vocab"), P("peer", None))
    return jax.shard_map(on_device, mesh=mesh, in_specs=in_specs, out_specs=out_specs, check_vma=False)
```

time: 340 us -> 71.7 us (0.21)
  waiting for transfers between devices: 154 us -> 31.8 us
  blocking collectives: 72.8 us -> 0 us
  matrix products: 58.2 us -> 0 us
  other arithmetic: 38.6 us -> 0 us
  starting transfers between devices: 0.08 us -> 22.3 us
  Pallas kernels: 0 us -> 16.6 us
  between operations: 14.2 us -> 0.77 us
    reduce_scatter x1 -> x0, waiting for transfers between devices: 89.8 us -> none  [on_device(): lax.psum_scatter(projector(head_weight[0], logit_grad), 'vocab', scatter_...]
    all_gather x1 -> x0, waiting for transfers between devices: 64.2 us -> none  [on_device(): lax.all_gather(own_logits[None], 'peer', axis=0, tiled=True)]
    dot_general x3 -> x0, matrix products: 58.2 us -> none  [the longest x1 32.8 us: moments(): jnp.einsum('itv,jtv->ijt', scaled, peer_tiles, precision=lax.Precision.HI...]
    psum x1 -> x0, blocking collectives: 56.2 us -> none  [on_device(): lax.psum((total_part, cross_part, target_part), 'vocab')]
    ppermute x0 -> x20, waiting for transfers between devices: none -> 31.8 us  [the longest x15 22.2 us: swap(): return lax.ppermute(array, axis, [(i, i ^ mask) for i in range(size)])]
    exp x2 -> x0, other arithmetic: 23.5 us -> none  [the longest x1 14.7 us: logit_gradient(): probs = jnp.exp(log_probs)]
    ppermute x0 -> x20, starting transfers between devices: none -> 22.3 us  [the longest x15 13.2 us: swap(): return lax.ppermute(array, axis, [(i, i ^ mask) for i in range(size)])]
    pallas_call x0 -> x12, Pallas kernels: none -> 16.6 us  [the longest x1 7.93 us: project(): pl.pallas_call(functools.partial(project_kernel, chunk_start), in_specs=[...]
  transfers between devices with their start and end apart: 2 -> 20, of which waited for: 2 -> 11; matrix products, arithmetic and copies ran while one was open for 0% -> 0% of each run, Pallas kernels for 0% -> 8%
where the time goes in v2:
time: 71.7 us; the launch traced here: 71.5 us
  waiting for transfers between devices  31.8 us (44%)
  starting transfers between devices  22.3 us (31%)
  Pallas kernels  16.6 us (23%)
  between operations  0.77 us (1%)
    ppermute x15, waiting for transfers between devices, swap(): return lax.ppermute(array, axis, [(i, i ^ mask) for i in range(size)])  22.2 us
    ppermute x15, starting transfers between devices, swap(): return lax.ppermute(array, axis, [(i, i ^ mask) for i in range(size)])  13.2 us
    ppermute x5, waiting for transfers between devices, hop(): lax.ppermute(array, 'vocab', [(2 * a + c, 2 * b + c) for a, b in pairs fo...  9.58 us
    ppermute x5, starting transfers between devices, hop(): lax.ppermute(array, 'vocab', [(2 * a + c, 2 * b + c) for a, b in pairs fo...  9.08 us
    pallas_call x1, Pallas kernels, project(): pl.pallas_call(functools.partial(project_kernel, chunk_start), in_specs=[...  7.93 us
    pallas_call x8, Pallas kernels, vmem_call(): pl.pallas_call(kernel, in_specs=[pl.BlockSpec(memory_space=pltpu.SMEM)] *...  6.89 us
  transfers between devices with their start and end apart: 20, of which 11 were waited for; matrix products, arithmetic and copies ran while one was open for 0% of the time, Pallas kernels for 8%

profile of v2, /device:TPU:0, one launch (start us, length us, event | category | flops | bytes accessed | tf_op | source)
XLA Modules:
  0.0 71.5 jit_solution(4122075619856895636)
XLA Ops:
  0.6 7.9 %project.1 = (bf16[4,512,1280]{2,1,0:T(8,128)(2,1)S(1)}, bf16[4,512,1280]{2,1,0:T(8,128)(2,1)S(1)}, f32[64,128]{1,0:T(8,128)S(1)}, bf16[64,1280]{1,0:T(8,128)(2,...) custom-call(s32[1]{0:T(128)} %bitcast.own_ref, ...), custom_call_target="tpu_custom_call" | custom-call | flops 3758096384 | tf_op jit(solution)/shard_map/project/pallas_call | solution.py:115
  8.6 0.5 collective-permute-start.14
  9.1 2.6 %collective-permute-start = (bf16[64,1280]{1,0:T(8,128)(2,1)S(1)}, bf16[64,1280]{1,0:T(8,128)(2,1)S(1)}, u32[]{:S(2)}, u32[]{:S(2)}) collective-permute-start(bf16[64,1280]{1,0:T(8,128)(2,1)S(1)} %get-tuple-element.23), channel_id=1, source_target_pairs={{0,8},{8,0},{16,24},{24,16},{1,9},{9,1},{17,25},{25,17},{2,10},{10... | collective-permute-start | bytes 491528 | tf_op jit(solution)/shard_map/ppermute | solution.py:417
  11.7 1.5 %collective-permute-start.1 = (bf16[64,1280]{1,0:T(8,128)(2,1)S(1)}, bf16[64,1280]{1,0:T(8,128)(2,1)S(1)}, u32[]{:S(2)}, u32[]{:S(2)}) collective-permute-start(bf16[64,1280]{1,0:T(8,128)(2,1)S(1)} %get-tuple-element.24), channel_id=1, source_target_pairs={{0,16},{8,24},{16,0},{24,8},{1,17},{9,25},{17,1},{25,9},{2,18},{10... | collective-permute-start | bytes 491528 | tf_op jit(solution)/shard_map/ppermute | solution.py:417
  13.2 0.0 collective-permute-start.2
  13.2 3.5 %collective-permute-done.refs_1_.refs_5_ = bf16[64,1280]{1,0:T(8,128)(2,1)S(1)} collective-permute-done((bf16[64,1280]{1,0:T(8,128)(2,1)S(1)}, bf16[64,1280]{1,0:T(8,128)(2,1)S(1)}, u32[]{:S(2)}, u32[]{:S(2)}) %collective-permute-start) | collective-permute-done | bytes 163872 | tf_op jit(solution)/shard_map/ppermute | solution.py:417
  16.7 4.7 %collective-permute-done.1.refs_2_.refs_6_ = bf16[64,1280]{1,0:T(8,128)(2,1)S(1)} collective-permute-done((bf16[64,1280]{1,0:T(8,128)(2,1)S(1)}, bf16[64,1280]{1,0:T(8,128)(2,1)S(1)}, u32[]{:S(2)}, u32[]{:S(2)}) %collective-permute-start.1) | collective-permute-done | bytes 163872 | tf_op jit(solution)/shard_map/ppermute | solution.py:417
  21.4 0.0 collective-permute-done.2.refs_3_.refs_7_
  21.4 0.9 %stats.1.refs_0_ = f32[32,128]{1,0:T(8,128)S(1)} custom-call(s32[1]{0:T(128)} %bitcast.own_ref, s32[1]{0:T(128)} %bitcast.1.shard_ref, f32[64,128]{1,0:T(8,128)S(1)} %get-tuple-element.21.meta_ref, bf16[64,1280]{1,0:T(8,128)(2,1)S(1)} %get-tuple-element.22.refs_0_.refs_4_, bf16[64,1280]{1,0:T(8,128)(2,1)S(1)} %collective-permute-done.refs_1_.refs_5_, ...), custom_call_target="tpu_custom_call" | custom-call | flops 13107200 | bytes 655360 | tf_op jit(solution)/shard_map/stats/pallas_call | solution.py:201
  22.3 0.1 collective-permute-start.3
  22.4 1.2 %collective-permute-done.3.refs_1_ = f32[32,128]{1,0:T(8,128)S(1)} collective-permute-done((f32[32,128]{1,0:T(8,128)S(1)}, f32[32,128]{1,0:T(8,128)S(1)}, u32[]{:S(2)}, u32[]{:S(2)}) %collective-permute-start.3) | collective-permute-done | bytes 16416 | tf_op jit(solution)/shard_map/ppermute | solution.py:417
  23.6 1.6 %collective-permute-start.4 = (f32[32,128]{1,0:T(8,128)S(1)}, f32[32,128]{1,0:T(8,128)S(1)}, u32[]{:S(2)}, u32[]{:S(2)}) collective-permute-start(f32[32,128]{1,0:T(8,128)S(1)} %merge.1.refs_0_), channel_id=1, source_target_pairs={{0,2},{1,3},{2,0},{3,1},{4,6},{5,7},{6,4},{7,5},{8,10},{9,11},{10,... | collective-permute-start | bytes 49160 | tf_op jit(solution)/shard_map/ppermute | solution.py:417
  25.2 2.6 %collective-permute-start.5 = (f32[32,128]{1,0:T(8,128)S(1)}, f32[32,128]{1,0:T(8,128)S(1)}, u32[]{:S(2)}, u32[]{:S(2)}) collective-permute-start(f32[32,128]{1,0:T(8,128)S(1)} %merge.1.refs_0_), channel_id=1, source_target_pairs={{0,4},{1,5},{2,6},{3,7},{4,0},{5,1},{6,2},{7,3},{8,12},{9,13},{10,... | collective-permute-start | bytes 49160 | tf_op jit(solution)/shard_map/ppermute | solution.py:417
  27.8 0.2 collective-permute-start.6
  28.0 0.0 collective-permute-done.4.refs_1_
  28.0 1.9 %collective-permute-done.5.refs_2_ = f32[32,128]{1,0:T(8,128)S(1)} collective-permute-done((f32[32,128]{1,0:T(8,128)S(1)}, f32[32,128]{1,0:T(8,128)S(1)}, u32[]{:S(2)}, u32[]{:S(2)}) %collective-permute-start.5) | collective-permute-done | bytes 16416 | tf_op jit(solution)/shard_map/ppermute | solution.py:417
  29.9 3.4 %collective-permute-done.6.refs_3_ = f32[32,128]{1,0:T(8,128)S(1)} collective-permute-done((f32[32,128]{1,0:T(8,128)S(1)}, f32[32,128]{1,0:T(8,128)S(1)}, u32[]{:S(2)}, u32[]{:S(2)}) %collective-permute-start.6) | collective-permute-done | bytes 16416 | tf_op jit(solution)/shard_map/ppermute | solution.py:417
  33.3 0.9 %gradients.1 = (bf16[64,1408]{1,0:T(8,128)(2,1)S(1)}, bf16[64,1408]{1,0:T(8,128)(2,1)S(1)}, bf16[64,1408]{1,0:T(8,128)(2,1)S(1)}, bf16[64,1408]{1,0:T(8,128)(2,1)S(1)}) custom-call(s32[1]{0:T(128)} %bitcast.own_ref, s32[1]{0:T(128)} %bitcast.1.shard_ref, f32[64,128]{1,0:T(8,128)S(1)} %get-tuple-element.21.meta_ref, f32[32,128]{1,0:T(8,128)S(1)} %merge.1.refs_0_, ...), custom_call_target="tpu_custom_call" | custom-call | flops 6553600 | bytes 1310720 | tf_op jit(solution)/shard_map/gradients/pallas_call | solution.py:283
  34.2 1.3 %collective-permute-start.7 = (bf16[64,1408]{1,0:T(8,128)(2,1)S(1)}, bf16[64,1408]{1,0:T(8,128)(2,1)S(1)}, u32[]{:S(2)}, u32[]{:S(2)}) collective-permute-start(bf16[64,1408]{1,0:T(8,128)(2,1)S(1)} %get-tuple-element.27), channel_id=1, source_target_pairs={{0,8},{8,0},{16,24},{24,16},{1,9},{9,1},{17,25},{25,17},{2,10},{10... | collective-permute-start | bytes 540680 | tf_op jit(solution)/shard_map/ppermute | solution.py:417
  35.5 0.8 %collective-permute-start.8 = (bf16[64,1408]{1,0:T(8,128)(2,1)S(1)}, bf16[64,1408]{1,0:T(8,128)(2,1)S(1)}, u32[]{:S(2)}, u32[]{:S(2)}) collective-permute-start(bf16[64,1408]{1,0:T(8,128)(2,1)S(1)} %get-tuple-element.28), channel_id=1, source_target_pairs={{0,16},{8,24},{16,0},{24,8},{1,17},{9,25},{17,1},{25,9},{2,18},{10... | collective-permute-start | bytes 540680 | tf_op jit(solution)/shard_map/ppermute | solution.py:417
  36.4 1.4 %collective-permute-start.9 = (bf16[64,1408]{1,0:T(8,128)(2,1)S(1)}, bf16[64,1408]{1,0:T(8,128)(2,1)S(1)}, u32[]{:S(2)}, u32[]{:S(2)}) collective-permute-start(bf16[64,1408]{1,0:T(8,128)(2,1)S(1)} %get-tuple-element.29), channel_id=1, source_target_pairs={{0,24},{8,16},{16,8},{24,0},{1,25},{9,17},{17,9},{25,1},{2,26},{10... | collective-permute-start | bytes 540680 | tf_op jit(solution)/shard_map/ppermute | solution.py:417
  37.8 0.0 collective-permute-start.10
  37.8 3.6 %collective-permute-done.7.refs_1_ = bf16[64,1408]{1,0:T(8,128)(2,1)S(1)} collective-permute-done((bf16[64,1408]{1,0:T(8,128)(2,1)S(1)}, bf16[64,1408]{1,0:T(8,128)(2,1)S(1)}, u32[]{:S(2)}, u32[]{:S(2)}) %collective-permute-start.7) | collective-permute-done | bytes 180256 | tf_op jit(solution)/shard_map/ppermute | solution.py:417
  41.4 0.0 collective-permute-start.11
  41.4 2.8 %collective-permute-done.8.refs_2_ = bf16[64,1408]{1,0:T(8,128)(2,1)S(1)} collective-permute-done((bf16[64,1408]{1,0:T(8,128)(2,1)S(1)}, bf16[64,1408]{1,0:T(8,128)(2,1)S(1)}, u32[]{:S(2)}, u32[]{:S(2)}) %collective-permute-start.8) | collective-permute-done | bytes 180256 | tf_op jit(solution)/shard_map/ppermute | solution.py:417
  44.1 0.0 collective-permute-start.12
  44.1 0.0 collective-permute-done.9.refs_3_
  44.1 0.5 collective-permute-start.13
  44.7 0.0 collective-permute-done.10.refs_4_
  44.7 0.0 collective-permute-done.11.refs_5_
  44.7 0.9 %collective-permute-done.12.refs_6_ = bf16[64,1408]{1,0:T(8,128)(2,1)S(1)} collective-permute-done((bf16[64,1408]{1,0:T(8,128)(2,1)S(1)}, bf16[64,1408]{1,0:T(8,128)(2,1)S(1)}, u32[]{:S(2)}, u32[]{:S(2)}) %collective-permute-start.12) | collective-permute-done | bytes 180256 | tf_op jit(solution)/shard_map/ppermute | solution.py:417
  45.6 0.3 collective-permute-done.13.refs_7_
  45.8 0.1 gather.1
  45.9 0.0 collective-permute-done.14.refs_1_
  45.9 1.0 %encode.3 = s16[528,256]{1,0:T(8,128)(2,1)S(1)} custom-call(s32[1]{0:T(128)} %bitcast.own_ref, s32[1]{0:T(128)} %bitcast.1.shard_ref, bf16[4,512,1280]{2,1,0:T(8,128)(2,1)S(1)} %get-tuple-element.32.refs_0_, bf16[4,512,1280]{2,1,0:T(8,128)(2,1)S(1)} %collective-permute-done.14.refs_1_, bf16[256,1280]{1,0:T(8,128)(2,1)S(1)} %get-tuple-element.34.refs_2_, ...), custom_call_target="tpu_custom_call" | custom-call | flops 1000 | tf_op jit(solution)/shard_map/encode/pallas_call | solution.py:317
  46.9 1.3 %collective-permute-start.17 = (s16[528,256]{1,0:T(8,128)(2,1)S(1)}, s16[528,256]{1,0:T(8,128)(2,1)S(1)}, u32[]{:S(2)}, u32[]{:S(2)}) collective-permute-start(s16[528,256]{1,0:T(8,128)(2,1)S(1)} %encode.3), channel_id=1, source_target_pairs={{0,2},{1,3},{6,4},{7,5},{8,10},{9,11},{14,12},{15,13},{16,18},{17,... | collective-permute-start | bytes 811016 | tf_op jit(solution)/shard_map/ppermute | solution.py:421
  48.2 0.7 collective-permute-start.15
  48.9 1.0 %encode.4 = (s16[528,256]{1,0:T(8,128)(2,1)S(1)}, f32[512,256]{1,0:T(8,128)S(1)}) custom-call(s32[1]{0:T(128)} %bitcast.own_ref, s32[1]{0:T(128)} %bitcast.1.shard_ref, bf16[4,512,1280]{2,1,0:T(8,128)(2,1)S(1)} %get-tuple-element.32.refs_0_, bf16[4,512,1280]{2,1,0:T(8,128)(2,1)S(1)} %collective-permute-done.14.refs_1_, ...), custom_call_target="tpu_custom_call" | custom-call | flops 1000 | tf_op jit(solution)/shard_map/encode/pallas_call | solution.py:317
  49.9 0.0 copy-start
  49.9 3.3 %collective-permute-start.16 = (s16[528,256]{1,0:T(8,128)(2,1)S(1)}, s16[528,256]{1,0:T(8,128)(2,1)S(1)}, u32[]{:S(2)}, u32[]{:S(2)}) collective-permute-start(s16[528,256]{1,0:T(8,128)(2,1)S(1)} %get-tuple-element.36), channel_id=1, source_target_pairs={{0,4},{1,5},{6,2},{7,3},{8,12},{9,13},{14,10},{15,11},{16,20},{17,... | collective-permute-start | bytes 811016 | tf_op jit(solution)/shard_map/ppermute | solution.py:421
  53.2 1.0 %encode.5 = s16[528,256]{1,0:T(8,128)(2,1)S(1)} custom-call(s32[1]{0:T(128)} %bitcast.own_ref, s32[1]{0:T(128)} %bitcast.1.shard_ref, bf16[4,512,1280]{2,1,0:T(8,128)(2,1)S(1)} %get-tuple-element.32.refs_0_, bf16[4,512,1280]{2,1,0:T(8,128)(2,1)S(1)} %collective-permute-done.14.refs_1_, bf16[256,1280]{1,0:T(8,128)(2,1)S(1)} %get-tuple-element.34.refs_2_, ...), custom_call_target="tpu_custom_call" | custom-call | flops 1000 | tf_op jit(solution)/shard_map/encode/pallas_call | solution.py:317
  54.2 0.8 %collective-permute-done.17.coded_ref = s16[528,256]{1,0:T(8,128)(2,1)S(1)} collective-permute-done((s16[528,256]{1,0:T(8,128)(2,1)S(1)}, s16[528,256]{1,0:T(8,128)(2,1)S(1)}, u32[]{:S(2)}, u32[]{:S(2)}) %collective-permute-start.17) | collective-permute-done | bytes 270368 | tf_op jit(solution)/shard_map/ppermute | solution.py:421
  55.0 0.2 relay.1
  55.2 2.5 %collective-permute-start.19 = (s16[528,256]{1,0:T(8,128)(2,1)S(1)}, s16[528,256]{1,0:T(8,128)(2,1)S(1)}, u32[]{:S(2)}, u32[]{:S(2)}) collective-permute-start(s16[528,256]{1,0:T(8,128)(2,1)S(1)} %encode.5), channel_id=1, source_target_pairs={{0,2},{1,3},{2,0},{3,1},{4,6},{5,7},{6,4},{7,5},{8,10},{9,11},{10,... | collective-permute-start | bytes 811016 | tf_op jit(solution)/shard_map/ppermute | solution.py:421
  57.7 1.3 %collective-permute-start.18 = (s16[528,256]{1,0:T(8,128)(2,1)S(1)}, s16[528,256]{1,0:T(8,128)(2,1)S(1)}, u32[]{:S(2)}, u32[]{:S(2)}) collective-permute-start(s16[528,256]{1,0:T(8,128)(2,1)S(1)} %relay.1), channel_id=1, source_target_pairs={{2,6},{3,7},{4,0},{5,1},{10,14},{11,15},{12,8},{13,9},{18,22},{19,... | collective-permute-start | bytes 811016 | tf_op jit(solution)/shard_map/ppermute | solution.py:421
  59.0 0.0 copy-done
  59.0 0.9 %place.1 = (bf16[512,256]{1,0:T(8,128)(2,1)S(1)}, f32[1,512]{1,0:T(1,128)}) custom-call(s32[1]{0:T(128)} %bitcast.own_ref, s32[1]{0:T(128)} %bitcast.1.shard_ref, s32[1,512]{1,0:T(1,128)S(1)} %bitcast.5, f32[256,1]{1,0:T(8,128)S(1)} %get-tuple-element.30.loss_ref), custom_call_target="tpu_custom_call" | custom-call | flops 134217728 | tf_op jit(solution)/shard_map/place/pallas_call | solution.py:317
  59.9 0.9 %keep.1.sum_ref = f32[512,256]{1,0:T(8,128)S(1)} custom-call(s32[1]{0:T(128)} %bitcast.own_ref, s32[1]{0:T(128)} %bitcast.1.shard_ref, bf16[4,512,1280]{2,1,0:T(8,128)(2,1)S(1)} %get-tuple-element.32.refs_0_, bf16[4,512,1280]{2,1,0:T(8,128)(2,1)S(1)} %collective-permute-done.14.refs_1_, bf16[256,1280]{1,0:T(8,128)(2,1)S(1)} %get-tuple-element.34.refs_2_, ...), custom_call_target="tpu_custom_call" | custom-call | flops 1000 | tf_op jit(solution)/shard_map/keep/pallas_call | solution.py:317
  60.8 0.0 collective-permute-done.16.refs_1_
  60.8 0.0 collective-permute-done.15.refs_0_
  60.8 8.8 %collective-permute-done.19.refs_3_ = s16[528,256]{1,0:T(8,128)(2,1)S(1)} collective-permute-done((s16[528,256]{1,0:T(8,128)(2,1)S(1)}, s16[528,256]{1,0:T(8,128)(2,1)S(1)}, u32[]{:S(2)}, u32[]{:S(2)}) %collective-permute-start.19) | collective-permute-done | bytes 270368 | tf_op jit(solution)/shard_map/ppermute | solution.py:421
  69.6 0.0 collective-permute-done.18.refs_2_
  69.6 1.9 %finish.1 = f32[1,512,512]{2,1,0:T(8,128)} custom-call(s32[1]{0:T(128)} %bitcast.own_ref, s32[1]{0:T(128)} %bitcast.1.shard_ref, bf16[512,256]{1,0:T(8,128)(2,1)S(1)} %get-tuple-element.31.place_ref, f32[512,256]{1,0:T(8,128)S(1)} %keep.1.sum_ref, s16[528,256]{1,0:T(8,128)(2,1)S(1)} %collective-permute-done.15.refs_0_, ...), custom_call_target="tpu_custom_call" | custom-call | flops 1000 | tf_op jit(solution)/shard_map/finish/pallas_call | solution.py:317
  (1 shorter events, 0.0 us)
Async XLA Ops:
  8.6 37.4 %collective-permute-start.14 = (bf16[4,512,1280]{2,1,0:T(8,128)(2,1)S(1)}, bf16[4,512,1280]{2,1,0:T(8,128)(2,1)S(1)}, u32[]{:S(2)}, u32[]{:S(2)}) collective-permute-start(bf16[4,512,1280]{2,1,0:T(8,128)(2,1)S(1)} %get-tuple-element.33), channel_id=1, source_target_pairs={{0,1},{1,0},{2,3},{3,2},{4,5},{5,4},{6,7},{7,6},{8,9},{9,8},{10,11... | collective-permute-start | bytes 15728648 | tf_op jit(solution)/shard_map/ppermute | solution.py:417
  9.1 7.6 %collective-permute-start = (bf16[64,1280]{1,0:T(8,128)(2,1)S(1)}, bf16[64,1280]{1,0:T(8,128)(2,1)S(1)}, u32[]{:S(2)}, u32[]{:S(2)}) collective-permute-start(bf16[64,1280]{1,0:T(8,128)(2,1)S(1)} %get-tuple-element.23), channel_id=1, source_target_pairs={{0,8},{8,0},{16,24},{24,16},{1,9},{9,1},{17,25},{25,17},{2,10},{10... | collective-permute-start | bytes 491528 | tf_op jit(solution)/shard_map/ppermute | solution.py:417
  11.7 9.8 %collective-permute-start.1 = (bf16[64,1280]{1,0:T(8,128)(2,1)S(1)}, bf16[64,1280]{1,0:T(8,128)(2,1)S(1)}, u32[]{:S(2)}, u32[]{:S(2)}) collective-permute-start(bf16[64,1280]{1,0:T(8,128)(2,1)S(1)} %get-tuple-element.24), channel_id=1, source_target_pairs={{0,16},{8,24},{16,0},{24,8},{1,17},{9,25},{17,1},{25,9},{2,18},{10... | collective-permute-start | bytes 491528 | tf_op jit(solution)/shard_map/ppermute | solution.py:417
  13.2 8.3 %collective-permute-start.2 = (bf16[64,1280]{1,0:T(8,128)(2,1)S(1)}, bf16[64,1280]{1,0:T(8,128)(2,1)S(1)}, u32[]{:S(2)}, u32[]{:S(2)}) collective-permute-start(bf16[64,1280]{1,0:T(8,128)(2,1)S(1)} %get-tuple-element.25), channel_id=1, source_target_pairs={{0,24},{8,16},{16,8},{24,0},{1,25},{9,17},{17,9},{25,1},{2,26},{10... | collective-permute-start | bytes 491528 | tf_op jit(solution)/shard_map/ppermute | solution.py:417
  22.3 1.2 %collective-permute-start.3 = (f32[32,128]{1,0:T(8,128)S(1)}, f32[32,128]{1,0:T(8,128)S(1)}, u32[]{:S(2)}, u32[]{:S(2)}) collective-permute-start(f32[32,128]{1,0:T(8,128)S(1)} %stats.1.refs_0_), channel_id=1, source_target_pairs={{0,1},{1,0},{2,3},{3,2},{4,5},{5,4},{6,7},{7,6},{8,9},{9,8},{10,11... | collective-permute-start | bytes 49160 | tf_op jit(solution)/shard_map/ppermute | solution.py:417
  23.6 4.5 %collective-permute-start.4 = (f32[32,128]{1,0:T(8,128)S(1)}, f32[32,128]{1,0:T(8,128)S(1)}, u32[]{:S(2)}, u32[]{:S(2)}) collective-permute-start(f32[32,128]{1,0:T(8,128)S(1)} %merge.1.refs_0_), channel_id=1, source_target_pairs={{0,2},{1,3},{2,0},{3,1},{4,6},{5,7},{6,4},{7,5},{8,10},{9,11},{10,... | collective-permute-start | bytes 49160 | tf_op jit(solution)/shard_map/ppermute | solution.py:417
  25.2 4.7 %collective-permute-start.5 = (f32[32,128]{1,0:T(8,128)S(1)}, f32[32,128]{1,0:T(8,128)S(1)}, u32[]{:S(2)}, u32[]{:S(2)}) collective-permute-start(f32[32,128]{1,0:T(8,128)S(1)} %merge.1.refs_0_), channel_id=1, source_target_pairs={{0,4},{1,5},{2,6},{3,7},{4,0},{5,1},{6,2},{7,3},{8,12},{9,13},{10,... | collective-permute-start | bytes 49160 | tf_op jit(solution)/shard_map/ppermute | solution.py:417
  27.8 5.5 %collective-permute-start.6 = (f32[32,128]{1,0:T(8,128)S(1)}, f32[32,128]{1,0:T(8,128)S(1)}, u32[]{:S(2)}, u32[]{:S(2)}) collective-permute-start(f32[32,128]{1,0:T(8,128)S(1)} %merge.1.refs_0_), channel_id=1, source_target_pairs={{0,6},{1,7},{2,4},{3,5},{4,2},{5,3},{6,0},{7,1},{8,14},{9,15},{10,... | collective-permute-start | bytes 49160 | tf_op jit(solution)/shard_map/ppermute | solution.py:417
  34.2 7.1 %collective-permute-start.7 = (bf16[64,1408]{1,0:T(8,128)(2,1)S(1)}, bf16[64,1408]{1,0:T(8,128)(2,1)S(1)}, u32[]{:S(2)}, u32[]{:S(2)}) collective-permute-start(bf16[64,1408]{1,0:T(8,128)(2,1)S(1)} %get-tuple-element.27), channel_id=1, source_target_pairs={{0,8},{8,0},{16,24},{24,16},{1,9},{9,1},{17,25},{25,17},{2,10},{10... | collective-permute-start | bytes 540680 | tf_op jit(solution)/shard_map/ppermute | solution.py:417
  35.5 8.6 %collective-permute-start.8 = (bf16[64,1408]{1,0:T(8,128)(2,1)S(1)}, bf16[64,1408]{1,0:T(8,128)(2,1)S(1)}, u32[]{:S(2)}, u32[]{:S(2)}) collective-permute-start(bf16[64,1408]{1,0:T(8,128)(2,1)S(1)} %get-tuple-element.28), channel_id=1, source_target_pairs={{0,16},{8,24},{16,0},{24,8},{1,17},{9,25},{17,1},{25,9},{2,18},{10... | collective-permute-start | bytes 540680 | tf_op jit(solution)/shard_map/ppermute | solution.py:417
  36.4 7.8 %collective-permute-start.9 = (bf16[64,1408]{1,0:T(8,128)(2,1)S(1)}, bf16[64,1408]{1,0:T(8,128)(2,1)S(1)}, u32[]{:S(2)}, u32[]{:S(2)}) collective-permute-start(bf16[64,1408]{1,0:T(8,128)(2,1)S(1)} %get-tuple-element.29), channel_id=1, source_target_pairs={{0,24},{8,16},{16,8},{24,0},{1,25},{9,17},{17,9},{25,1},{2,26},{10... | collective-permute-start | bytes 540680 | tf_op jit(solution)/shard_map/ppermute | solution.py:417
  37.8 6.9 %collective-permute-start.10 = (bf16[64,1408]{1,0:T(8,128)(2,1)S(1)}, bf16[64,1408]{1,0:T(8,128)(2,1)S(1)}, u32[]{:S(2)}, u32[]{:S(2)}) collective-permute-start(bf16[64,1408]{1,0:T(8,128)(2,1)S(1)} %get-tuple-element.26.refs_0_), channel_id=1, source_target_pairs={{0,1},{1,0},{2,3},{3,2},{4,5},{5,4},{6,7},{7,6},{8,9},{9,8},{10,11... | collective-permute-start | bytes 540680 | tf_op jit(solution)/shard_map/ppermute | solution.py:417
  41.4 3.3 %collective-permute-start.11 = (bf16[64,1408]{1,0:T(8,128)(2,1)S(1)}, bf16[64,1408]{1,0:T(8,128)(2,1)S(1)}, u32[]{:S(2)}, u32[]{:S(2)}) collective-permute-start(bf16[64,1408]{1,0:T(8,128)(2,1)S(1)} %collective-permute-done.7.refs_1_), channel_id=1, source_target_pairs={{0,1},{1,0},{2,3},{3,2},{4,5},{5,4},{6,7},{7,6},{8,9},{9,8},{10,11... | collective-permute-start | bytes 540680 | tf_op jit(solution)/shard_map/ppermute | solution.py:417
  44.1 1.4 %collective-permute-start.12 = (bf16[64,1408]{1,0:T(8,128)(2,1)S(1)}, bf16[64,1408]{1,0:T(8,128)(2,1)S(1)}, u32[]{:S(2)}, u32[]{:S(2)}) collective-permute-start(bf16[64,1408]{1,0:T(8,128)(2,1)S(1)} %collective-permute-done.8.refs_2_), channel_id=1, source_target_pairs={{0,1},{1,0},{2,3},{3,2},{4,5},{5,4},{6,7},{7,6},{8,9},{9,8},{10,11... | collective-permute-start | bytes 540680 | tf_op jit(solution)/shard_map/ppermute | solution.py:417
  44.1 1.7 %collective-permute-start.13 = (bf16[64,1408]{1,0:T(8,128)(2,1)S(1)}, bf16[64,1408]{1,0:T(8,128)(2,1)S(1)}, u32[]{:S(2)}, u32[]{:S(2)}) collective-permute-start(bf16[64,1408]{1,0:T(8,128)(2,1)S(1)} %collective-permute-done.9.refs_3_), channel_id=1, source_target_pairs={{0,1},{1,0},{2,3},{3,2},{4,5},{5,4},{6,7},{7,6},{8,9},{9,8},{10,11... | collective-permute-start | bytes 540680 | tf_op jit(solution)/shard_map/ppermute | solution.py:417
  46.9 8.1 %collective-permute-start.17 = (s16[528,256]{1,0:T(8,128)(2,1)S(1)}, s16[528,256]{1,0:T(8,128)(2,1)S(1)}, u32[]{:S(2)}, u32[]{:S(2)}) collective-permute-start(s16[528,256]{1,0:T(8,128)(2,1)S(1)} %encode.3), channel_id=1, source_target_pairs={{0,2},{1,3},{6,4},{7,5},{8,10},{9,11},{14,12},{15,13},{16,18},{17,... | collective-permute-start | bytes 811016 | tf_op jit(solution)/shard_map/ppermute | solution.py:421
  48.2 12.6 %collective-permute-start.15 = (s16[528,256]{1,0:T(8,128)(2,1)S(1)}, s16[528,256]{1,0:T(8,128)(2,1)S(1)}, u32[]{:S(2)}, u32[]{:S(2)}) collective-permute-start(s16[528,256]{1,0:T(8,128)(2,1)S(1)} %encode.3), channel_id=1, source_target_pairs={{2,4},{3,5},{4,2},{5,3},{10,12},{11,13},{12,10},{13,11},{18,20},{1... | collective-permute-start | bytes 811016 | tf_op jit(solution)/shard_map/ppermute | solution.py:421
  49.9 9.1 %copy-start = (s32[512]{0:T(512)S(1)}, s32[512]{0:T(512)}, u32[]{:S(2)}) copy-start(s32[512]{0:T(512)} %param.6) | copy-start | bytes 6148
  49.9 10.9 %collective-permute-start.16 = (s16[528,256]{1,0:T(8,128)(2,1)S(1)}, s16[528,256]{1,0:T(8,128)(2,1)S(1)}, u32[]{:S(2)}, u32[]{:S(2)}) collective-permute-start(s16[528,256]{1,0:T(8,128)(2,1)S(1)} %get-tuple-element.36), channel_id=1, source_target_pairs={{0,4},{1,5},{6,2},{7,3},{8,12},{9,13},{14,10},{15,11},{16,20},{17,... | collective-permute-start | bytes 811016 | tf_op jit(solution)/shard_map/ppermute | solution.py:421
  55.2 14.4 %collective-permute-start.19 = (s16[528,256]{1,0:T(8,128)(2,1)S(1)}, s16[528,256]{1,0:T(8,128)(2,1)S(1)}, u32[]{:S(2)}, u32[]{:S(2)}) collective-permute-start(s16[528,256]{1,0:T(8,128)(2,1)S(1)} %encode.5), channel_id=1, source_target_pairs={{0,2},{1,3},{2,0},{3,1},{4,6},{5,7},{6,4},{7,5},{8,10},{9,11},{10,... | collective-permute-start | bytes 811016 | tf_op jit(solution)/shard_map/ppermute | solution.py:421
  57.7 11.9 %collective-permute-start.18 = (s16[528,256]{1,0:T(8,128)(2,1)S(1)}, s16[528,256]{1,0:T(8,128)(2,1)S(1)}, u32[]{:S(2)}, u32[]{:S(2)}) collective-permute-start(s16[528,256]{1,0:T(8,128)(2,1)S(1)} %relay.1), channel_id=1, source_target_pairs={{2,6},{3,7},{4,0},{5,1},{10,14},{11,15},{12,8},{13,9},{18,22},{19,... | collective-permute-start | bytes 811016 | tf_op jit(solution)/shard_map/ppermute | solution.py:421

commit v3 on v2

--- a/solution.py
+++ b/solution.py
@@ -126,7 +126,7 @@
             pltpu.VMEM((rows, depth), jnp.bfloat16),
             pltpu.VMEM((rows, width), jnp.float32),
             pltpu.SemaphoreType.DMA((2,)),
-            pltpu.SemaphoreType.DMA((4,)),
+            pltpu.SemaphoreType.DMA((2,)),
             pltpu.SemaphoreType.DMA((2 * count,)),
         ],
         compiler_params=LARGE,
@@ -359,7 +359,10 @@
 
 
 def keep_kernel(own_ref, shard_ref, *refs):
-    refs[-1][...] = both_shares(0, shard_ref, refs[:-1])
+    value = both_shares(0, shard_ref, refs[:4])
+    for ref in refs[4:-1]:
+        value += get_coded(ref)
+    refs[-1][...] = value
 
 
 def place_kernel(peers, own_ref, shard_ref, row_ref, loss_ref, place_ref, out_ref):
@@ -398,19 +401,41 @@
     )
 
 
-def finish_kernel(own_ref, shard_ref, place_ref, sum_ref, *refs):
+def finish_kernel(place_ref, sum_ref, *refs):
+    coded_refs, (out_hbm, out_ref, sems) = refs[:-3], refs[-3:]
     value = sum_ref[...]
-    for ref in refs[:-1]:
+    for ref in coded_refs:
         value += get_coded(ref)
-    result = None
-    for _ in range(3):
-        piece = value.astype(jnp.bfloat16)
-        value = value - piece.astype(jnp.float32)
-        term = lax.dot_general(
-            place_ref[...], piece, (((1,), (1,)), ((), ())), preferred_element_type=jnp.float32
-        )
-        result = term if result is None else result + term
-    refs[-1][0] = result
+    high = value.astype(jnp.bfloat16)
+    low = (value - high.astype(jnp.float32)).astype(jnp.bfloat16)
+    turned = lambda place, piece: lax.dot_general(
+        place, piece, (((1,), (1,)), ((), ())), preferred_element_type=jnp.float32
+    )
+    part = out_ref.shape[0] // sems.shape[0]
+    copies = []
+    for n in range(sems.shape[0]):
+        span = pl.ds(n * part, part)
+        place = place_ref[span, :]
+        out_ref[span, :] = turned(place, high) + turned(place, low)
+        copies.append(pltpu.make_async_copy(out_ref.at[span, :], out_hbm.at[0, span, :], sems.at[n]))
+        copies[-1].start()
+    for copy in copies:
+        copy.wait()
+
+
+def finish(placing, kept, arrived):
+    tokens, rows = placing.shape
+    depth = kept.shape[0]
+    return pl.pallas_call(
+        finish_kernel,
+        in_specs=[pl.BlockSpec(memory_space=pltpu.VMEM)] * (2 + len(arrived)),
+        out_specs=pl.BlockSpec(memory_space=pltpu.HBM),
+        out_shape=jax.ShapeDtypeStruct((1, tokens, depth), jnp.float32),
+        scratch_shapes=[pltpu.VMEM((tokens, depth), jnp.float32), pltpu.SemaphoreType.DMA((4,))],
+        compiler_params=SMALL,
+        cost_estimate=pl.CostEstimate(flops=1000, bytes_accessed=0, transcendentals=0),
+        name="finish",
+    )(placing, kept, *arrived)
 
 
 def swap(array, axis, size, mask):
@@ -451,7 +476,9 @@
     logits = across(blocks)
     part = stats(ids, meta, logits)
     part = merge([part, core_swap(part)])
-    parts = [part] + [swap(part, "vocab", shards, 2 * mask) for mask in range(1, chips)]
+    after = lambda array, *before: lax.optimization_barrier((array,) + before)[0]
+    w_given = core_swap(after(w_theirs, part)) if by_core else None
+    parts = [part] + [swap(part, "vocab", shards, 2 * mask) for mask in range(chips - 1, 0, -1)]
     grads = across(gradients(ids, meta, parts, logits))
 
     cost = pl.CostEstimate(flops=1000, bytes_accessed=0, transcendentals=0)
@@ -462,7 +489,7 @@
     own_grad, other_grad, losses = vmem_call(kernel, outs, cost, "gather", ids, *grads, *others)
     placing, token_loss = place(ids, labels, losses, peers)
     if by_core:
-        operands = (w_mine, core_swap(w_theirs), own_grad, other_grad)
+        operands = (w_mine, w_given, own_grad, other_grad)
         coded_shape, full = ((depth + CODE_ROWS, rows), jnp.int16), ((depth, rows), jnp.float32)
 
         def encode(mask, *more):
@@ -479,18 +506,18 @@
             relay = hop(relayed, [(1, 3), (2, 0)])
             one = lax.optimization_barrier((one, relayed))[0]
             near = hop(one, [(0, 1), (1, 0), (2, 3), (3, 2)])
-            arrived = [mid, skip, relay, near]
+            early, arrived = [mid, skip], [relay, near]
         else:
+            early = []
             arrived = [swap(encode(mask)[0], "vocab", shards, 2 * mask) for mask in range(chips - 1, 0, -1)]
-        (kept,) = vmem_call(keep_kernel, [((depth, rows), jnp.float32)], cost, "keep", ids, *operands)
+        (kept,) = vmem_call(keep_kernel, [((depth, rows), jnp.float32)], cost, "keep", ids, *operands, *early)
     else:
         arrived = []
         share = lax.dot_general(
             head_weight[0], own_grad, (((1,), (1,)), ((), ())), preferred_element_type=jnp.float32
         )
         kept = lax.psum_scatter(share, "vocab", scatter_dimension=0, tiled=True)
-    out = ((1, tokens, depth), jnp.float32)
-    (grad_hidden,) = vmem_call(finish_kernel, [out], cost, "finish", ids, placing, kept, *arrived)
+    grad_hidden = finish(placing, kept, arrived)
     return grad_hidden, token_loss
 
 

time: 71.7 us -> 70.1 us (0.978)
  waiting for transfers between devices: 31.8 us -> 30.5 us
  Pallas kernels: 16.6 us -> 15.8 us
    pallas_call x8 -> x7, Pallas kernels: 6.89 us -> 5.02 us  [vmem_call(): pl.pallas_call(kernel, in_specs=[pl.BlockSpec(memory_space=pltpu.SMEM)] *...]
    pallas_call x0 -> x1, Pallas kernels: none -> 1.69 us  [finish(): pl.pallas_call(finish_kernel, in_specs=[pl.BlockSpec(memory_space=pltpu.V...]
    ppermute x15, waiting for transfers between devices: 22.2 us -> 20.8 us  [swap(): return lax.ppermute(array, axis, [(i, i ^ mask) for i in range(size)])]
  transfers between devices with their start and end apart: 20 -> 20, of which waited for: 11 -> 12; matrix products, arithmetic and copies ran while one was open for 0% -> 0% of each run, Pallas kernels for 8% -> 7%
where the time goes in v3:
time: 70.1 us; the launch traced here: 69.8 us
  waiting for transfers between devices  30.5 us (44%)
  starting transfers between devices  22.8 us (33%)
  Pallas kernels  15.8 us (23%)
  between operations  0.78 us (1%)
    ppermute x15, waiting for transfers between devices, swap(): return lax.ppermute(array, axis, [(i, i ^ mask) for i in range(size)])  20.8 us
    ppermute x15, starting transfers between devices, swap(): return lax.ppermute(array, axis, [(i, i ^ mask) for i in range(size)])  13.3 us
    ppermute x5, waiting for transfers between devices, hop(): lax.ppermute(array, 'vocab', [(2 * a + c, 2 * b + c) for a, b in pairs fo...  9.68 us
    ppermute x5, starting transfers between devices, hop(): lax.ppermute(array, 'vocab', [(2 * a + c, 2 * b + c) for a, b in pairs fo...  9.52 us
    pallas_call x1, Pallas kernels, project(): pl.pallas_call(functools.partial(project_kernel, chunk_start), in_specs=[...  7.28 us
    pallas_call x7, Pallas kernels, vmem_call(): pl.pallas_call(kernel, in_specs=[pl.BlockSpec(memory_space=pltpu.SMEM)] *...  5.02 us
    pallas_call x1, Pallas kernels, finish(): pl.pallas_call(finish_kernel, in_specs=[pl.BlockSpec(memory_space=pltpu.V...  1.69 us
  transfers between devices with their start and end apart: 20, of which 12 were waited for; matrix products, arithmetic and copies ran while one was open for 0% of the time, Pallas kernels for 7%

profile of v3, /device:TPU:0, one launch (start us, length us, event | category | flops | bytes accessed | tf_op | source)
XLA Modules:
  0.0 69.8 jit_solution(2533105317662236330)
XLA Ops:
  0.6 7.3 %project.1 = (bf16[4,512,1280]{2,1,0:T(8,128)(2,1)S(1)}, bf16[4,512,1280]{2,1,0:T(8,128)(2,1)S(1)}, f32[64,128]{1,0:T(8,128)S(1)}, bf16[64,1280]{1,0:T(8,128)(2,...) custom-call(s32[1]{0:T(128)} %bitcast.own_ref, ...), custom_call_target="tpu_custom_call" | custom-call | flops 3758096384 | tf_op jit(solution)/shard_map/project/pallas_call | solution.py:115
  7.9 3.0 %collective-permute-start = (bf16[64,1280]{1,0:T(8,128)(2,1)S(1)}, bf16[64,1280]{1,0:T(8,128)(2,1)S(1)}, u32[]{:S(2)}, u32[]{:S(2)}) collective-permute-start(bf16[64,1280]{1,0:T(8,128)(2,1)S(1)} %get-tuple-element.24), channel_id=1, source_target_pairs={{0,8},{8,0},{16,24},{24,16},{1,9},{9,1},{17,25},{25,17},{2,10},{10... | collective-permute-start | bytes 491528 | tf_op jit(solution)/shard_map/ppermute | solution.py:442
  10.9 1.5 %collective-permute-start.1 = (bf16[64,1280]{1,0:T(8,128)(2,1)S(1)}, bf16[64,1280]{1,0:T(8,128)(2,1)S(1)}, u32[]{:S(2)}, u32[]{:S(2)}) collective-permute-start(bf16[64,1280]{1,0:T(8,128)(2,1)S(1)} %get-tuple-element.25), channel_id=1, source_target_pairs={{0,16},{8,24},{16,0},{24,8},{1,17},{9,25},{17,1},{25,9},{2,18},{10... | collective-permute-start | bytes 491528 | tf_op jit(solution)/shard_map/ppermute | solution.py:442
  12.5 0.0 collective-permute-start.2
  12.5 3.5 %collective-permute-done.refs_1_.refs_5_ = bf16[64,1280]{1,0:T(8,128)(2,1)S(1)} collective-permute-done((bf16[64,1280]{1,0:T(8,128)(2,1)S(1)}, bf16[64,1280]{1,0:T(8,128)(2,1)S(1)}, u32[]{:S(2)}, u32[]{:S(2)}) %collective-permute-start) | collective-permute-done | bytes 163872 | tf_op jit(solution)/shard_map/ppermute | solution.py:442
  16.0 4.1 %collective-permute-done.1.refs_2_.refs_6_ = bf16[64,1280]{1,0:T(8,128)(2,1)S(1)} collective-permute-done((bf16[64,1280]{1,0:T(8,128)(2,1)S(1)}, bf16[64,1280]{1,0:T(8,128)(2,1)S(1)}, u32[]{:S(2)}, u32[]{:S(2)}) %collective-permute-start.1) | collective-permute-done | bytes 163872 | tf_op jit(solution)/shard_map/ppermute | solution.py:442
  20.1 0.0 collective-permute-done.2.refs_3_.refs_7_
  20.1 0.9 %stats.1.refs_0_ = f32[32,128]{1,0:T(8,128)S(1)} custom-call(s32[1]{0:T(128)} %bitcast.own_ref, s32[1]{0:T(128)} %bitcast.1.shard_ref, f32[64,128]{1,0:T(8,128)S(1)} %get-tuple-element.22.meta_ref, bf16[64,1280]{1,0:T(8,128)(2,1)S(1)} %get-tuple-element.23.refs_0_.refs_4_, bf16[64,1280]{1,0:T(8,128)(2,1)S(1)} %collective-permute-done.refs_1_.refs_5_, ...), custom_call_target="tpu_custom_call" | custom-call | flops 13107200 | bytes 655360 | tf_op jit(solution)/shard_map/stats/pallas_call | solution.py:201
  21.0 0.1 collective-permute-start.3
  21.1 1.2 %collective-permute-done.3.refs_1_ = f32[32,128]{1,0:T(8,128)S(1)} collective-permute-done((f32[32,128]{1,0:T(8,128)S(1)}, f32[32,128]{1,0:T(8,128)S(1)}, u32[]{:S(2)}, u32[]{:S(2)}) %collective-permute-start.3) | collective-permute-done | bytes 16416 | tf_op jit(solution)/shard_map/ppermute | solution.py:442
  22.2 0.2 collective-permute-start.14
  22.5 3.6 %collective-permute-start.4 = (f32[32,128]{1,0:T(8,128)S(1)}, f32[32,128]{1,0:T(8,128)S(1)}, u32[]{:S(2)}, u32[]{:S(2)}) collective-permute-start(f32[32,128]{1,0:T(8,128)S(1)} %merge.1.refs_0_), channel_id=1, source_target_pairs={{0,6},{1,7},{2,4},{3,5},{4,2},{5,3},{6,0},{7,1},{8,14},{9,15},{10,... | collective-permute-start | bytes 49160 | tf_op jit(solution)/shard_map/ppermute | solution.py:442
  26.1 0.0 collective-permute-start.5
  26.1 0.8 %collective-permute-start.6 = (f32[32,128]{1,0:T(8,128)S(1)}, f32[32,128]{1,0:T(8,128)S(1)}, u32[]{:S(2)}, u32[]{:S(2)}) collective-permute-start(f32[32,128]{1,0:T(8,128)S(1)} %merge.1.refs_0_), channel_id=1, source_target_pairs={{0,2},{1,3},{2,0},{3,1},{4,6},{5,7},{6,4},{7,5},{8,10},{9,11},{10,... | collective-permute-start | bytes 49160 | tf_op jit(solution)/shard_map/ppermute | solution.py:442
  26.9 1.1 %collective-permute-done.4.refs_1_ = f32[32,128]{1,0:T(8,128)S(1)} collective-permute-done((f32[32,128]{1,0:T(8,128)S(1)}, f32[32,128]{1,0:T(8,128)S(1)}, u32[]{:S(2)}, u32[]{:S(2)}) %collective-permute-start.4) | collective-permute-done | bytes 16416 | tf_op jit(solution)/shard_map/ppermute | solution.py:442
  28.0 2.7 %collective-permute-done.5.refs_2_ = f32[32,128]{1,0:T(8,128)S(1)} collective-permute-done((f32[32,128]{1,0:T(8,128)S(1)}, f32[32,128]{1,0:T(8,128)S(1)}, u32[]{:S(2)}, u32[]{:S(2)}) %collective-permute-start.5) | collective-permute-done | bytes 16416 | tf_op jit(solution)/shard_map/ppermute | solution.py:442
  30.7 0.0 collective-permute-done.6.refs_3_
  30.7 0.9 %gradients.1 = (bf16[64,1408]{1,0:T(8,128)(2,1)S(1)}, bf16[64,1408]{1,0:T(8,128)(2,1)S(1)}, bf16[64,1408]{1,0:T(8,128)(2,1)S(1)}, bf16[64,1408]{1,0:T(8,128)(2,1)S(1)}) custom-call(s32[1]{0:T(128)} %bitcast.own_ref, s32[1]{0:T(128)} %bitcast.1.shard_ref, f32[64,128]{1,0:T(8,128)S(1)} %get-tuple-element.22.meta_ref, f32[32,128]{1,0:T(8,128)S(1)} %merge.1.refs_0_, ...), custom_call_target="tpu_custom_call" | custom-call | flops 6553600 | bytes 1310720 | tf_op jit(solution)/shard_map/gradients/pallas_call | solution.py:283
  31.6 1.3 %collective-permute-start.7 = (bf16[64,1408]{1,0:T(8,128)(2,1)S(1)}, bf16[64,1408]{1,0:T(8,128)(2,1)S(1)}, u32[]{:S(2)}, u32[]{:S(2)}) collective-permute-start(bf16[64,1408]{1,0:T(8,128)(2,1)S(1)} %get-tuple-element.28), channel_id=1, source_target_pairs={{0,8},{8,0},{16,24},{24,16},{1,9},{9,1},{17,25},{25,17},{2,10},{10... | collective-permute-start | bytes 540680 | tf_op jit(solution)/shard_map/ppermute | solution.py:442
  32.9 0.8 %collective-permute-start.8 = (bf16[64,1408]{1,0:T(8,128)(2,1)S(1)}, bf16[64,1408]{1,0:T(8,128)(2,1)S(1)}, u32[]{:S(2)}, u32[]{:S(2)}) collective-permute-start(bf16[64,1408]{1,0:T(8,128)(2,1)S(1)} %get-tuple-element.29), channel_id=1, source_target_pairs={{0,16},{8,24},{16,0},{24,8},{1,17},{9,25},{17,1},{25,9},{2,18},{10... | collective-permute-start | bytes 540680 | tf_op jit(solution)/shard_map/ppermute | solution.py:442
  33.7 1.4 %collective-permute-start.9 = (bf16[64,1408]{1,0:T(8,128)(2,1)S(1)}, bf16[64,1408]{1,0:T(8,128)(2,1)S(1)}, u32[]{:S(2)}, u32[]{:S(2)}) collective-permute-start(bf16[64,1408]{1,0:T(8,128)(2,1)S(1)} %get-tuple-element.30), channel_id=1, source_target_pairs={{0,24},{8,16},{16,8},{24,0},{1,25},{9,17},{17,9},{25,1},{2,26},{10... | collective-permute-start | bytes 540680 | tf_op jit(solution)/shard_map/ppermute | solution.py:442
  35.2 0.0 collective-permute-start.10
  35.2 3.8 %collective-permute-done.7.refs_1_ = bf16[64,1408]{1,0:T(8,128)(2,1)S(1)} collective-permute-done((bf16[64,1408]{1,0:T(8,128)(2,1)S(1)}, bf16[64,1408]{1,0:T(8,128)(2,1)S(1)}, u32[]{:S(2)}, u32[]{:S(2)}) %collective-permute-start.7) | collective-permute-done | bytes 180256 | tf_op jit(solution)/shard_map/ppermute | solution.py:442
  39.0 0.0 collective-permute-start.11
  39.0 3.2 %collective-permute-done.8.refs_2_ = bf16[64,1408]{1,0:T(8,128)(2,1)S(1)} collective-permute-done((bf16[64,1408]{1,0:T(8,128)(2,1)S(1)}, bf16[64,1408]{1,0:T(8,128)(2,1)S(1)}, u32[]{:S(2)}, u32[]{:S(2)}) %collective-permute-start.8) | collective-permute-done | bytes 180256 | tf_op jit(solution)/shard_map/ppermute | solution.py:442
  42.1 0.0 collective-permute-start.12
  42.2 0.0 collective-permute-done.9.refs_3_
  42.2 0.5 collective-permute-start.13
  42.7 0.0 collective-permute-done.10.refs_4_
  42.7 0.0 collective-permute-done.11.refs_5_
  42.7 0.9 %collective-permute-done.12.refs_6_ = bf16[64,1408]{1,0:T(8,128)(2,1)S(1)} collective-permute-done((bf16[64,1408]{1,0:T(8,128)(2,1)S(1)}, bf16[64,1408]{1,0:T(8,128)(2,1)S(1)}, u32[]{:S(2)}, u32[]{:S(2)}) %collective-permute-start.12) | collective-permute-done | bytes 180256 | tf_op jit(solution)/shard_map/ppermute | solution.py:442
  43.6 0.3 collective-permute-done.13.refs_7_
  43.8 0.1 gather.1
  44.0 0.0 collective-permute-done.14.refs_1_
  44.0 1.0 %encode.3 = s16[528,256]{1,0:T(8,128)(2,1)S(1)} custom-call(s32[1]{0:T(128)} %bitcast.own_ref, s32[1]{0:T(128)} %bitcast.1.shard_ref, bf16[4,512,1280]{2,1,0:T(8,128)(2,1)S(1)} %get-tuple-element.33.refs_0_, bf16[4,512,1280]{2,1,0:T(8,128)(2,1)S(1)} %collective-permute-done.14.refs_1_, bf16[256,1280]{1,0:T(8,128)(2,1)S(1)} %get-tuple-element.36.refs_2_, ...), custom_call_target="tpu_custom_call" | custom-call | flops 1000 | tf_op jit(solution)/shard_map/encode/pallas_call | solution.py:317
  44.9 1.5 %collective-permute-start.17 = (s16[528,256]{1,0:T(8,128)(2,1)S(1)}, s16[528,256]{1,0:T(8,128)(2,1)S(1)}, u32[]{:S(2)}, u32[]{:S(2)}) collective-permute-start(s16[528,256]{1,0:T(8,128)(2,1)S(1)} %encode.3), channel_id=1, source_target_pairs={{0,2},{1,3},{6,4},{7,5},{8,10},{9,11},{14,12},{15,13},{16,18},{17,... | collective-permute-start | bytes 811016 | tf_op jit(solution)/shard_map/ppermute | solution.py:446
  46.4 0.7 collective-permute-start.15
  47.1 1.0 %encode.4 = (s16[528,256]{1,0:T(8,128)(2,1)S(1)}, f32[512,256]{1,0:T(8,128)S(1)}) custom-call(s32[1]{0:T(128)} %bitcast.own_ref, s32[1]{0:T(128)} %bitcast.1.shard_ref, bf16[4,512,1280]{2,1,0:T(8,128)(2,1)S(1)} %get-tuple-element.33.refs_0_, bf16[4,512,1280]{2,1,0:T(8,128)(2,1)S(1)} %collective-permute-done.14.refs_1_, ...), custom_call_target="tpu_custom_call" | custom-call | flops 1000 | tf_op jit(solution)/shard_map/encode/pallas_call | solution.py:317
  48.1 0.0 copy-start
  48.1 4.5 %collective-permute-start.16 = (s16[528,256]{1,0:T(8,128)(2,1)S(1)}, s16[528,256]{1,0:T(8,128)(2,1)S(1)}, u32[]{:S(2)}, u32[]{:S(2)}) collective-permute-start(s16[528,256]{1,0:T(8,128)(2,1)S(1)} %get-tuple-element.38), channel_id=1, source_target_pairs={{0,4},{1,5},{6,2},{7,3},{8,12},{9,13},{14,10},{15,11},{16,20},{17,... | collective-permute-start | bytes 811016 | tf_op jit(solution)/shard_map/ppermute | solution.py:446
  52.7 1.0 %encode.5 = s16[528,256]{1,0:T(8,128)(2,1)S(1)} custom-call(s32[1]{0:T(128)} %bitcast.own_ref, s32[1]{0:T(128)} %bitcast.1.shard_ref, bf16[4,512,1280]{2,1,0:T(8,128)(2,1)S(1)} %get-tuple-element.33.refs_0_, bf16[4,512,1280]{2,1,0:T(8,128)(2,1)S(1)} %collective-permute-done.14.refs_1_, bf16[256,1280]{1,0:T(8,128)(2,1)S(1)} %get-tuple-element.36.refs_2_, ...), custom_call_target="tpu_custom_call" | custom-call | flops 1000 | tf_op jit(solution)/shard_map/encode/pallas_call | solution.py:317
  53.7 0.0 collective-permute-done.17.coded_ref
  53.7 0.2 relay.1
  53.9 1.5 %collective-permute-start.19 = (s16[528,256]{1,0:T(8,128)(2,1)S(1)}, s16[528,256]{1,0:T(8,128)(2,1)S(1)}, u32[]{:S(2)}, u32[]{:S(2)}) collective-permute-start(s16[528,256]{1,0:T(8,128)(2,1)S(1)} %encode.5), channel_id=1, source_target_pairs={{0,2},{1,3},{2,0},{3,1},{4,6},{5,7},{6,4},{7,5},{8,10},{9,11},{10,... | collective-permute-start | bytes 811016 | tf_op jit(solution)/shard_map/ppermute | solution.py:446
  55.4 1.3 %collective-permute-start.18 = (s16[528,256]{1,0:T(8,128)(2,1)S(1)}, s16[528,256]{1,0:T(8,128)(2,1)S(1)}, u32[]{:S(2)}, u32[]{:S(2)}) collective-permute-start(s16[528,256]{1,0:T(8,128)(2,1)S(1)} %relay.1), channel_id=1, source_target_pairs={{2,6},{3,7},{4,0},{5,1},{10,14},{11,15},{12,8},{13,9},{18,22},{19,... | collective-permute-start | bytes 811016 | tf_op jit(solution)/shard_map/ppermute | solution.py:446
  56.7 0.0 copy-done
  56.7 0.9 %place.1 = (bf16[512,256]{1,0:T(8,128)(2,1)S(1)}, f32[1,512]{1,0:T(1,128)}) custom-call(s32[1]{0:T(128)} %bitcast.own_ref, s32[1]{0:T(128)} %bitcast.1.shard_ref, s32[1,512]{1,0:T(1,128)S(1)} %bitcast.5, f32[256,1]{1,0:T(8,128)S(1)} %get-tuple-element.31.loss_ref), custom_call_target="tpu_custom_call" | custom-call | flops 134217728 | tf_op jit(solution)/shard_map/place/pallas_call | solution.py:317
  57.6 1.9 %collective-permute-done.16.refs_5_ = s16[528,256]{1,0:T(8,128)(2,1)S(1)} collective-permute-done((s16[528,256]{1,0:T(8,128)(2,1)S(1)}, s16[528,256]{1,0:T(8,128)(2,1)S(1)}, u32[]{:S(2)}, u32[]{:S(2)}) %collective-permute-start.16) | collective-permute-done | bytes 270368 | tf_op jit(solution)/shard_map/ppermute | solution.py:446
  59.5 0.0 collective-permute-done.15.refs_4_
  59.5 0.9 %keep.1.sum_ref = f32[512,256]{1,0:T(8,128)S(1)} custom-call(s32[1]{0:T(128)} %bitcast.own_ref, s32[1]{0:T(128)} %bitcast.1.shard_ref, bf16[4,512,1280]{2,1,0:T(8,128)(2,1)S(1)} %get-tuple-element.33.refs_0_, bf16[4,512,1280]{2,1,0:T(8,128)(2,1)S(1)} %collective-permute-done.14.refs_1_, bf16[256,1280]{1,0:T(8,128)(2,1)S(1)} %get-tuple-element.36.refs_2_, ...), custom_call_target="tpu_custom_call" | custom-call | flops 1000 | tf_op jit(solution)/shard_map/keep/pallas_call | solution.py:317
  60.4 4.2 %collective-permute-done.19.refs_1_ = s16[528,256]{1,0:T(8,128)(2,1)S(1)} collective-permute-done((s16[528,256]{1,0:T(8,128)(2,1)S(1)}, s16[528,256]{1,0:T(8,128)(2,1)S(1)}, u32[]{:S(2)}, u32[]{:S(2)}) %collective-permute-start.19) | collective-permute-done | bytes 270368 | tf_op jit(solution)/shard_map/ppermute | solution.py:446
  64.6 3.5 %collective-permute-done.18.refs_0_ = s16[528,256]{1,0:T(8,128)(2,1)S(1)} collective-permute-done((s16[528,256]{1,0:T(8,128)(2,1)S(1)}, s16[528,256]{1,0:T(8,128)(2,1)S(1)}, u32[]{:S(2)}, u32[]{:S(2)}) %collective-permute-start.18) | collective-permute-done | bytes 270368 | tf_op jit(solution)/shard_map/ppermute | solution.py:446
  68.2 1.7 %finish.1 = f32[1,512,512]{2,1,0:T(8,128)} custom-call(bf16[512,256]{1,0:T(8,128)(2,1)S(1)} %get-tuple-element.32.place_ref, f32[512,256]{1,0:T(8,128)S(1)} %keep.1.sum_ref, s16[528,256]{1,0:T(8,128)(2,1)S(1)} %collective-permute-done.18.refs_0_, s16[528,256]{1,0:T(8,128)(2,1)S(1)} %collective-permute-done.19.refs_1_), custom_call_target="tpu_custom_call" | custom-call | flops 1000 | tf_op jit(solution)/shard_map/finish/pallas_call | solution.py:429
  (1 shorter events, 0.0 us)
Async XLA Ops:
  7.9 8.0 %collective-permute-start = (bf16[64,1280]{1,0:T(8,128)(2,1)S(1)}, bf16[64,1280]{1,0:T(8,128)(2,1)S(1)}, u32[]{:S(2)}, u32[]{:S(2)}) collective-permute-start(bf16[64,1280]{1,0:T(8,128)(2,1)S(1)} %get-tuple-element.24), channel_id=1, source_target_pairs={{0,8},{8,0},{16,24},{24,16},{1,9},{9,1},{17,25},{25,17},{2,10},{10... | collective-permute-start | bytes 491528 | tf_op jit(solution)/shard_map/ppermute | solution.py:442
  10.9 9.2 %collective-permute-start.1 = (bf16[64,1280]{1,0:T(8,128)(2,1)S(1)}, bf16[64,1280]{1,0:T(8,128)(2,1)S(1)}, u32[]{:S(2)}, u32[]{:S(2)}) collective-permute-start(bf16[64,1280]{1,0:T(8,128)(2,1)S(1)} %get-tuple-element.25), channel_id=1, source_target_pairs={{0,16},{8,24},{16,0},{24,8},{1,17},{9,25},{17,1},{25,9},{2,18},{10... | collective-permute-start | bytes 491528 | tf_op jit(solution)/shard_map/ppermute | solution.py:442
  12.5 7.7 %collective-permute-start.2 = (bf16[64,1280]{1,0:T(8,128)(2,1)S(1)}, bf16[64,1280]{1,0:T(8,128)(2,1)S(1)}, u32[]{:S(2)}, u32[]{:S(2)}) collective-permute-start(bf16[64,1280]{1,0:T(8,128)(2,1)S(1)} %get-tuple-element.26), channel_id=1, source_target_pairs={{0,24},{8,16},{16,8},{24,0},{1,25},{9,17},{17,9},{25,1},{2,26},{10... | collective-permute-start | bytes 491528 | tf_op jit(solution)/shard_map/ppermute | solution.py:442
  21.0 1.2 %collective-permute-start.3 = (f32[32,128]{1,0:T(8,128)S(1)}, f32[32,128]{1,0:T(8,128)S(1)}, u32[]{:S(2)}, u32[]{:S(2)}) collective-permute-start(f32[32,128]{1,0:T(8,128)S(1)} %stats.1.refs_0_), channel_id=1, source_target_pairs={{0,1},{1,0},{2,3},{3,2},{4,5},{5,4},{6,7},{7,6},{8,9},{9,8},{10,11... | collective-permute-start | bytes 49160 | tf_op jit(solution)/shard_map/ppermute | solution.py:442
  22.2 21.7 %collective-permute-start.14 = (bf16[4,512,1280]{2,1,0:T(8,128)(2,1)S(1)}, bf16[4,512,1280]{2,1,0:T(8,128)(2,1)S(1)}, u32[]{:S(2)}, u32[]{:S(2)}) collective-permute-start(bf16[4,512,1280]{2,1,0:T(8,128)(2,1)S(1)} %get-tuple-element.35), channel_id=1, source_target_pairs={{0,1},{1,0},{2,3},{3,2},{4,5},{5,4},{6,7},{7,6},{8,9},{9,8},{10,11... | collective-permute-start | bytes 15728648 | tf_op jit(solution)/shard_map/ppermute | solution.py:442
  22.5 5.5 %collective-permute-start.4 = (f32[32,128]{1,0:T(8,128)S(1)}, f32[32,128]{1,0:T(8,128)S(1)}, u32[]{:S(2)}, u32[]{:S(2)}) collective-permute-start(f32[32,128]{1,0:T(8,128)S(1)} %merge.1.refs_0_), channel_id=1, source_target_pairs={{0,6},{1,7},{2,4},{3,5},{4,2},{5,3},{6,0},{7,1},{8,14},{9,15},{10,... | collective-permute-start | bytes 49160 | tf_op jit(solution)/shard_map/ppermute | solution.py:442
  26.1 4.6 %collective-permute-start.5 = (f32[32,128]{1,0:T(8,128)S(1)}, f32[32,128]{1,0:T(8,128)S(1)}, u32[]{:S(2)}, u32[]{:S(2)}) collective-permute-start(f32[32,128]{1,0:T(8,128)S(1)} %merge.1.refs_0_), channel_id=1, source_target_pairs={{0,4},{1,5},{2,6},{3,7},{4,0},{5,1},{6,2},{7,3},{8,12},{9,13},{10,... | collective-permute-start | bytes 49160 | tf_op jit(solution)/shard_map/ppermute | solution.py:442
  26.1 4.6 %collective-permute-start.6 = (f32[32,128]{1,0:T(8,128)S(1)}, f32[32,128]{1,0:T(8,128)S(1)}, u32[]{:S(2)}, u32[]{:S(2)}) collective-permute-start(f32[32,128]{1,0:T(8,128)S(1)} %merge.1.refs_0_), channel_id=1, source_target_pairs={{0,2},{1,3},{2,0},{3,1},{4,6},{5,7},{6,4},{7,5},{8,10},{9,11},{10,... | collective-permute-start | bytes 49160 | tf_op jit(solution)/shard_map/ppermute | solution.py:442
  31.6 7.3 %collective-permute-start.7 = (bf16[64,1408]{1,0:T(8,128)(2,1)S(1)}, bf16[64,1408]{1,0:T(8,128)(2,1)S(1)}, u32[]{:S(2)}, u32[]{:S(2)}) collective-permute-start(bf16[64,1408]{1,0:T(8,128)(2,1)S(1)} %get-tuple-element.28), channel_id=1, source_target_pairs={{0,8},{8,0},{16,24},{24,16},{1,9},{9,1},{17,25},{25,17},{2,10},{10... | collective-permute-start | bytes 540680 | tf_op jit(solution)/shard_map/ppermute | solution.py:442
  32.9 9.2 %collective-permute-start.8 = (bf16[64,1408]{1,0:T(8,128)(2,1)S(1)}, bf16[64,1408]{1,0:T(8,128)(2,1)S(1)}, u32[]{:S(2)}, u32[]{:S(2)}) collective-permute-start(bf16[64,1408]{1,0:T(8,128)(2,1)S(1)} %get-tuple-element.29), channel_id=1, source_target_pairs={{0,16},{8,24},{16,0},{24,8},{1,17},{9,25},{17,1},{25,9},{2,18},{10... | collective-permute-start | bytes 540680 | tf_op jit(solution)/shard_map/ppermute | solution.py:442
  33.7 8.4 %collective-permute-start.9 = (bf16[64,1408]{1,0:T(8,128)(2,1)S(1)}, bf16[64,1408]{1,0:T(8,128)(2,1)S(1)}, u32[]{:S(2)}, u32[]{:S(2)}) collective-permute-start(bf16[64,1408]{1,0:T(8,128)(2,1)S(1)} %get-tuple-element.30), channel_id=1, source_target_pairs={{0,24},{8,16},{16,8},{24,0},{1,25},{9,17},{17,9},{25,1},{2,26},{10... | collective-permute-start | bytes 540680 | tf_op jit(solution)/shard_map/ppermute | solution.py:442
  35.2 7.5 %collective-permute-start.10 = (bf16[64,1408]{1,0:T(8,128)(2,1)S(1)}, bf16[64,1408]{1,0:T(8,128)(2,1)S(1)}, u32[]{:S(2)}, u32[]{:S(2)}) collective-permute-start(bf16[64,1408]{1,0:T(8,128)(2,1)S(1)} %get-tuple-element.27.refs_0_), channel_id=1, source_target_pairs={{0,1},{1,0},{2,3},{3,2},{4,5},{5,4},{6,7},{7,6},{8,9},{9,8},{10,11... | collective-permute-start | bytes 540680 | tf_op jit(solution)/shard_map/ppermute | solution.py:442
  39.0 3.7 %collective-permute-start.11 = (bf16[64,1408]{1,0:T(8,128)(2,1)S(1)}, bf16[64,1408]{1,0:T(8,128)(2,1)S(1)}, u32[]{:S(2)}, u32[]{:S(2)}) collective-permute-start(bf16[64,1408]{1,0:T(8,128)(2,1)S(1)} %collective-permute-done.7.refs_1_), channel_id=1, source_target_pairs={{0,1},{1,0},{2,3},{3,2},{4,5},{5,4},{6,7},{7,6},{8,9},{9,8},{10,11... | collective-permute-start | bytes 540680 | tf_op jit(solution)/shard_map/ppermute | solution.py:442
  42.1 1.4 %collective-permute-start.12 = (bf16[64,1408]{1,0:T(8,128)(2,1)S(1)}, bf16[64,1408]{1,0:T(8,128)(2,1)S(1)}, u32[]{:S(2)}, u32[]{:S(2)}) collective-permute-start(bf16[64,1408]{1,0:T(8,128)(2,1)S(1)} %collective-permute-done.8.refs_2_), channel_id=1, source_target_pairs={{0,1},{1,0},{2,3},{3,2},{4,5},{5,4},{6,7},{7,6},{8,9},{9,8},{10,11... | collective-permute-start | bytes 540680 | tf_op jit(solution)/shard_map/ppermute | solution.py:442
  42.2 1.7 %collective-permute-start.13 = (bf16[64,1408]{1,0:T(8,128)(2,1)S(1)}, bf16[64,1408]{1,0:T(8,128)(2,1)S(1)}, u32[]{:S(2)}, u32[]{:S(2)}) collective-permute-start(bf16[64,1408]{1,0:T(8,128)(2,1)S(1)} %collective-permute-done.9.refs_3_), channel_id=1, source_target_pairs={{0,1},{1,0},{2,3},{3,2},{4,5},{5,4},{6,7},{7,6},{8,9},{9,8},{10,11... | collective-permute-start | bytes 540680 | tf_op jit(solution)/shard_map/ppermute | solution.py:442
  44.9 8.7 %collective-permute-start.17 = (s16[528,256]{1,0:T(8,128)(2,1)S(1)}, s16[528,256]{1,0:T(8,128)(2,1)S(1)}, u32[]{:S(2)}, u32[]{:S(2)}) collective-permute-start(s16[528,256]{1,0:T(8,128)(2,1)S(1)} %encode.3), channel_id=1, source_target_pairs={{0,2},{1,3},{6,4},{7,5},{8,10},{9,11},{14,12},{15,13},{16,18},{17,... | collective-permute-start | bytes 811016 | tf_op jit(solution)/shard_map/ppermute | solution.py:446
  46.4 13.1 %collective-permute-start.15 = (s16[528,256]{1,0:T(8,128)(2,1)S(1)}, s16[528,256]{1,0:T(8,128)(2,1)S(1)}, u32[]{:S(2)}, u32[]{:S(2)}) collective-permute-start(s16[528,256]{1,0:T(8,128)(2,1)S(1)} %encode.3), channel_id=1, source_target_pairs={{2,4},{3,5},{4,2},{5,3},{10,12},{11,13},{12,10},{13,11},{18,20},{1... | collective-permute-start | bytes 811016 | tf_op jit(solution)/shard_map/ppermute | solution.py:446
  48.1 8.6 %copy-start = (s32[512]{0:T(512)S(1)}, s32[512]{0:T(512)}, u32[]{:S(2)}) copy-start(s32[512]{0:T(512)} %param.6) | copy-start | bytes 6148
  48.1 11.4 %collective-permute-start.16 = (s16[528,256]{1,0:T(8,128)(2,1)S(1)}, s16[528,256]{1,0:T(8,128)(2,1)S(1)}, u32[]{:S(2)}, u32[]{:S(2)}) collective-permute-start(s16[528,256]{1,0:T(8,128)(2,1)S(1)} %get-tuple-element.38), channel_id=1, source_target_pairs={{0,4},{1,5},{6,2},{7,3},{8,12},{9,13},{14,10},{15,11},{16,20},{17,... | collective-permute-start | bytes 811016 | tf_op jit(solution)/shard_map/ppermute | solution.py:446
  53.9 10.8 %collective-permute-start.19 = (s16[528,256]{1,0:T(8,128)(2,1)S(1)}, s16[528,256]{1,0:T(8,128)(2,1)S(1)}, u32[]{:S(2)}, u32[]{:S(2)}) collective-permute-start(s16[528,256]{1,0:T(8,128)(2,1)S(1)} %encode.5), channel_id=1, source_target_pairs={{0,2},{1,3},{2,0},{3,1},{4,6},{5,7},{6,4},{7,5},{8,10},{9,11},{10,... | collective-permute-start | bytes 811016 | tf_op jit(solution)/shard_map/ppermute | solution.py:446
  55.4 12.8 %collective-permute-start.18 = (s16[528,256]{1,0:T(8,128)(2,1)S(1)}, s16[528,256]{1,0:T(8,128)(2,1)S(1)}, u32[]{:S(2)}, u32[]{:S(2)}) collective-permute-start(s16[528,256]{1,0:T(8,128)(2,1)S(1)} %relay.1), channel_id=1, source_target_pairs={{2,6},{3,7},{4,0},{5,1},{10,14},{11,15},{12,8},{13,9},{18,22},{19,... | collective-permute-start | bytes 811016 | tf_op jit(solution)/shard_map/ppermute | solution.py:446

commit v4 on v3

--- a/solution.py
+++ b/solution.py
@@ -348,20 +348,26 @@
 
 
 def encode_kernel(mask, own_ref, shard_ref, *refs):
-    value = both_shares(mask, shard_ref, refs[:4])
-    put_coded(refs[4], value)
-    for ref in refs[5:]:
-        ref[...] = value
+    put_coded(refs[4], both_shares(mask, shard_ref, refs[:4]))
+
+
+def is_middle(shard_ref):
+    chip = shard_ref[0] // 2
+    return (chip == 1) | (chip == 2)
 
 
 def relay_kernel(own_ref, shard_ref, value_ref, coded_ref, out_ref):
-    put_coded(out_ref, value_ref[...] + get_coded(coded_ref))
+    put_coded(out_ref, value_ref[...] + jnp.where(is_middle(shard_ref), get_coded(coded_ref), 0.0))
+
+
+def sum_kernel(mask, own_ref, shard_ref, *refs):
+    refs[-1][...] = both_shares(mask, shard_ref, refs[:4])
 
 
 def keep_kernel(own_ref, shard_ref, *refs):
     value = both_shares(0, shard_ref, refs[:4])
     for ref in refs[4:-1]:
-        value += get_coded(ref)
+        value += jnp.where(is_middle(shard_ref), 0.0, get_coded(ref))
     refs[-1][...] = value
 
 
@@ -497,16 +503,15 @@
             return vmem_call(kernel, [coded_shape, *more], cost, "encode", ids, *operands)
 
         if chips == 4:
-            (three,) = encode(3)
-            far, mid = hop(three, [(0, 1), (3, 2)]), hop(three, [(1, 2), (2, 1)])
-            two, two_sum = encode(2, full)
-            skip = hop(two, [(0, 2), (3, 1)])
+            (two,) = encode(2)
+            first = hop(two, [(0, 1), (3, 2), (1, 3), (2, 0)])
+            kernel = functools.partial(sum_kernel, 3)
+            (three,) = vmem_call(kernel, [full], cost, "share", ids, *operands)
             (one,) = encode(1)
-            (relayed,) = vmem_call(relay_kernel, [coded_shape], cost, "relay", ids, two_sum, far)
-            relay = hop(relayed, [(1, 3), (2, 0)])
-            one = lax.optimization_barrier((one, relayed))[0]
-            near = hop(one, [(0, 1), (1, 0), (2, 3), (3, 2)])
-            early, arrived = [mid, skip], [relay, near]
+            (relayed,) = vmem_call(relay_kernel, [coded_shape], cost, "relay", ids, three, first)
+            cross = swap(relayed, "vocab", shards, 6)
+            near = swap(one, "vocab", shards, 2)
+            early, arrived = [first], [cross, near]
         else:
             early = []
             arrived = [swap(encode(mask)[0], "vocab", shards, 2 * mask) for mask in range(chips - 1, 0, -1)]

time: 70.1 us -> 68.2 us (0.973)
  starting transfers between devices: 22.8 us -> 16.6 us
  waiting for transfers between devices: 30.5 us -> 35 us
    ppermute x5 -> x1, starting transfers between devices: 9.52 us -> 0.06 us  [hop(): lax.ppermute(array, 'vocab', [(2 * a + c, 2 * b + c) for a, b in pairs fo...]
    ppermute x15 -> x17, waiting for transfers between devices: 20.8 us -> 29.2 us  [swap(): return lax.ppermute(array, axis, [(i, i ^ mask) for i in range(size)])]
    ppermute x5 -> x1, waiting for transfers between devices: 9.68 us -> 5.81 us  [hop(): lax.ppermute(array, 'vocab', [(2 * a + c, 2 * b + c) for a, b in pairs fo...]
    ppermute x15 -> x17, starting transfers between devices: 13.3 us -> 16.5 us  [swap(): return lax.ppermute(array, axis, [(i, i ^ mask) for i in range(size)])]
  transfers between devices with their start and end apart: 20 -> 18, of which waited for: 12 -> 12; matrix products, arithmetic and copies ran while one was open for 0% -> 0% of each run, Pallas kernels for 7% -> 7%
where the time goes in v4:
time: 68.2 us; the launch traced here: 68 us
  waiting for transfers between devices  35 us (51%)
  starting transfers between devices  16.6 us (24%)
  Pallas kernels  15.7 us (23%)
  between operations  0.74 us (1%)
    ppermute x17, waiting for transfers between devices, swap(): return lax.ppermute(array, axis, [(i, i ^ mask) for i in range(size)])  29.2 us
    ppermute x17, starting transfers between devices, swap(): return lax.ppermute(array, axis, [(i, i ^ mask) for i in range(size)])  16.5 us
    pallas_call x1, Pallas kernels, project(): pl.pallas_call(functools.partial(project_kernel, chunk_start), in_specs=[...  7.28 us
    ppermute x1, waiting for transfers between devices, hop(): lax.ppermute(array, 'vocab', [(2 * a + c, 2 * b + c) for a, b in pairs fo...  5.81 us
    pallas_call x7, Pallas kernels, vmem_call(): pl.pallas_call(kernel, in_specs=[pl.BlockSpec(memory_space=pltpu.SMEM)] *...  4.92 us
    pallas_call x1, Pallas kernels, finish(): pl.pallas_call(finish_kernel, in_specs=[pl.BlockSpec(memory_space=pltpu.V...  1.68 us
  transfers between devices with their start and end apart: 18, of which 12 were waited for; matrix products, arithmetic and copies ran while one was open for 0% of the time, Pallas kernels for 7%

profile of v4, /device:TPU:0, one launch (start us, length us, event | category | flops | bytes accessed | tf_op | source)
XLA Modules:
  0.0 68.0 jit_solution(15418082575007795142)
XLA Ops:
  0.6 7.3 %project.1 = (bf16[4,512,1280]{2,1,0:T(8,128)(2,1)S(1)}, bf16[4,512,1280]{2,1,0:T(8,128)(2,1)S(1)}, f32[64,128]{1,0:T(8,128)S(1)}, bf16[64,1280]{1,0:T(8,128)(2,...) custom-call(s32[1]{0:T(128)} %bitcast.own_ref, ...), custom_call_target="tpu_custom_call" | custom-call | flops 3758096384 | tf_op jit(solution)/shard_map/project/pallas_call | solution.py:115
  7.9 3.0 %collective-permute-start = (bf16[64,1280]{1,0:T(8,128)(2,1)S(1)}, bf16[64,1280]{1,0:T(8,128)(2,1)S(1)}, u32[]{:S(2)}, u32[]{:S(2)}) collective-permute-start(bf16[64,1280]{1,0:T(8,128)(2,1)S(1)} %get-tuple-element.21), channel_id=1, source_target_pairs={{0,8},{8,0},{16,24},{24,16},{1,9},{9,1},{17,25},{25,17},{2,10},{10... | collective-permute-start | bytes 491528 | tf_op jit(solution)/shard_map/ppermute | solution.py:448
  10.9 1.5 %collective-permute-start.1 = (bf16[64,1280]{1,0:T(8,128)(2,1)S(1)}, bf16[64,1280]{1,0:T(8,128)(2,1)S(1)}, u32[]{:S(2)}, u32[]{:S(2)}) collective-permute-start(bf16[64,1280]{1,0:T(8,128)(2,1)S(1)} %get-tuple-element.22), channel_id=1, source_target_pairs={{0,16},{8,24},{16,0},{24,8},{1,17},{9,25},{17,1},{25,9},{2,18},{10... | collective-permute-start | bytes 491528 | tf_op jit(solution)/shard_map/ppermute | solution.py:448
  12.5 0.0 collective-permute-start.2
  12.5 3.5 %collective-permute-done.refs_1_.refs_5_ = bf16[64,1280]{1,0:T(8,128)(2,1)S(1)} collective-permute-done((bf16[64,1280]{1,0:T(8,128)(2,1)S(1)}, bf16[64,1280]{1,0:T(8,128)(2,1)S(1)}, u32[]{:S(2)}, u32[]{:S(2)}) %collective-permute-start) | collective-permute-done | bytes 163872 | tf_op jit(solution)/shard_map/ppermute | solution.py:448
  16.0 4.1 %collective-permute-done.1.refs_2_.refs_6_ = bf16[64,1280]{1,0:T(8,128)(2,1)S(1)} collective-permute-done((bf16[64,1280]{1,0:T(8,128)(2,1)S(1)}, bf16[64,1280]{1,0:T(8,128)(2,1)S(1)}, u32[]{:S(2)}, u32[]{:S(2)}) %collective-permute-start.1) | collective-permute-done | bytes 163872 | tf_op jit(solution)/shard_map/ppermute | solution.py:448
  20.1 0.0 collective-permute-done.2.refs_3_.refs_7_
  20.1 0.9 %stats.1.refs_0_ = f32[32,128]{1,0:T(8,128)S(1)} custom-call(s32[1]{0:T(128)} %bitcast.own_ref, s32[1]{0:T(128)} %bitcast.1.shard_ref, f32[64,128]{1,0:T(8,128)S(1)} %get-tuple-element.19.meta_ref, bf16[64,1280]{1,0:T(8,128)(2,1)S(1)} %get-tuple-element.20.refs_0_.refs_4_, bf16[64,1280]{1,0:T(8,128)(2,1)S(1)} %collective-permute-done.refs_1_.refs_5_, ...), custom_call_target="tpu_custom_call" | custom-call | flops 13107200 | bytes 655360 | tf_op jit(solution)/shard_map/stats/pallas_call | solution.py:201
  21.0 0.1 collective-permute-start.3
  21.1 1.2 %collective-permute-done.3.refs_1_ = f32[32,128]{1,0:T(8,128)S(1)} collective-permute-done((f32[32,128]{1,0:T(8,128)S(1)}, f32[32,128]{1,0:T(8,128)S(1)}, u32[]{:S(2)}, u32[]{:S(2)}) %collective-permute-start.3) | collective-permute-done | bytes 16416 | tf_op jit(solution)/shard_map/ppermute | solution.py:448
  22.2 0.2 collective-permute-start.14
  22.5 3.6 %collective-permute-start.4 = (f32[32,128]{1,0:T(8,128)S(1)}, f32[32,128]{1,0:T(8,128)S(1)}, u32[]{:S(2)}, u32[]{:S(2)}) collective-permute-start(f32[32,128]{1,0:T(8,128)S(1)} %merge.1.refs_0_), channel_id=1, source_target_pairs={{0,6},{1,7},{2,4},{3,5},{4,2},{5,3},{6,0},{7,1},{8,14},{9,15},{10,... | collective-permute-start | bytes 49160 | tf_op jit(solution)/shard_map/ppermute | solution.py:448
  26.1 0.0 collective-permute-start.5
  26.1 0.8 %collective-permute-start.6 = (f32[32,128]{1,0:T(8,128)S(1)}, f32[32,128]{1,0:T(8,128)S(1)}, u32[]{:S(2)}, u32[]{:S(2)}) collective-permute-start(f32[32,128]{1,0:T(8,128)S(1)} %merge.1.refs_0_), channel_id=1, source_target_pairs={{0,2},{1,3},{2,0},{3,1},{4,6},{5,7},{6,4},{7,5},{8,10},{9,11},{10,... | collective-permute-start | bytes 49160 | tf_op jit(solution)/shard_map/ppermute | solution.py:448
  26.9 1.1 %collective-permute-done.4.refs_1_ = f32[32,128]{1,0:T(8,128)S(1)} collective-permute-done((f32[32,128]{1,0:T(8,128)S(1)}, f32[32,128]{1,0:T(8,128)S(1)}, u32[]{:S(2)}, u32[]{:S(2)}) %collective-permute-start.4) | collective-permute-done | bytes 16416 | tf_op jit(solution)/shard_map/ppermute | solution.py:448
  28.0 2.7 %collective-permute-done.5.refs_2_ = f32[32,128]{1,0:T(8,128)S(1)} collective-permute-done((f32[32,128]{1,0:T(8,128)S(1)}, f32[32,128]{1,0:T(8,128)S(1)}, u32[]{:S(2)}, u32[]{:S(2)}) %collective-permute-start.5) | collective-permute-done | bytes 16416 | tf_op jit(solution)/shard_map/ppermute | solution.py:448
  30.7 0.0 collective-permute-done.6.refs_3_
  30.7 0.9 %gradients.1 = (bf16[64,1408]{1,0:T(8,128)(2,1)S(1)}, bf16[64,1408]{1,0:T(8,128)(2,1)S(1)}, bf16[64,1408]{1,0:T(8,128)(2,1)S(1)}, bf16[64,1408]{1,0:T(8,128)(2,1)S(1)}) custom-call(s32[1]{0:T(128)} %bitcast.own_ref, s32[1]{0:T(128)} %bitcast.1.shard_ref, f32[64,128]{1,0:T(8,128)S(1)} %get-tuple-element.19.meta_ref, f32[32,128]{1,0:T(8,128)S(1)} %merge.1.refs_0_, ...), custom_call_target="tpu_custom_call" | custom-call | flops 6553600 | bytes 1310720 | tf_op jit(solution)/shard_map/gradients/pallas_call | solution.py:283
  31.6 1.3 %collective-permute-start.7 = (bf16[64,1408]{1,0:T(8,128)(2,1)S(1)}, bf16[64,1408]{1,0:T(8,128)(2,1)S(1)}, u32[]{:S(2)}, u32[]{:S(2)}) collective-permute-start(bf16[64,1408]{1,0:T(8,128)(2,1)S(1)} %get-tuple-element.25), channel_id=1, source_target_pairs={{0,8},{8,0},{16,24},{24,16},{1,9},{9,1},{17,25},{25,17},{2,10},{10... | collective-permute-start | bytes 540680 | tf_op jit(solution)/shard_map/ppermute | solution.py:448
  32.9 0.8 %collective-permute-start.8 = (bf16[64,1408]{1,0:T(8,128)(2,1)S(1)}, bf16[64,1408]{1,0:T(8,128)(2,1)S(1)}, u32[]{:S(2)}, u32[]{:S(2)}) collective-permute-start(bf16[64,1408]{1,0:T(8,128)(2,1)S(1)} %get-tuple-element.26), channel_id=1, source_target_pairs={{0,16},{8,24},{16,0},{24,8},{1,17},{9,25},{17,1},{25,9},{2,18},{10... | collective-permute-start | bytes 540680 | tf_op jit(solution)/shard_map/ppermute | solution.py:448
  33.7 1.4 %collective-permute-start.9 = (bf16[64,1408]{1,0:T(8,128)(2,1)S(1)}, bf16[64,1408]{1,0:T(8,128)(2,1)S(1)}, u32[]{:S(2)}, u32[]{:S(2)}) collective-permute-start(bf16[64,1408]{1,0:T(8,128)(2,1)S(1)} %get-tuple-element.27), channel_id=1, source_target_pairs={{0,24},{8,16},{16,8},{24,0},{1,25},{9,17},{17,9},{25,1},{2,26},{10... | collective-permute-start | bytes 540680 | tf_op jit(solution)/shard_map/ppermute | solution.py:448
  35.2 0.0 collective-permute-start.10
  35.2 3.8 %collective-permute-done.7.refs_1_ = bf16[64,1408]{1,0:T(8,128)(2,1)S(1)} collective-permute-done((bf16[64,1408]{1,0:T(8,128)(2,1)S(1)}, bf16[64,1408]{1,0:T(8,128)(2,1)S(1)}, u32[]{:S(2)}, u32[]{:S(2)}) %collective-permute-start.7) | collective-permute-done | bytes 180256 | tf_op jit(solution)/shard_map/ppermute | solution.py:448
  39.0 0.0 collective-permute-start.11
  39.0 3.2 %collective-permute-done.8.refs_2_ = bf16[64,1408]{1,0:T(8,128)(2,1)S(1)} collective-permute-done((bf16[64,1408]{1,0:T(8,128)(2,1)S(1)}, bf16[64,1408]{1,0:T(8,128)(2,1)S(1)}, u32[]{:S(2)}, u32[]{:S(2)}) %collective-permute-start.8) | collective-permute-done | bytes 180256 | tf_op jit(solution)/shard_map/ppermute | solution.py:448
  42.1 0.0 collective-permute-start.12
  42.2 0.0 collective-permute-done.9.refs_3_
  42.2 0.5 collective-permute-start.13
  42.7 0.0 collective-permute-done.10.refs_4_
  42.7 0.0 collective-permute-done.11.refs_5_
  42.7 0.9 %collective-permute-done.12.refs_6_ = bf16[64,1408]{1,0:T(8,128)(2,1)S(1)} collective-permute-done((bf16[64,1408]{1,0:T(8,128)(2,1)S(1)}, bf16[64,1408]{1,0:T(8,128)(2,1)S(1)}, u32[]{:S(2)}, u32[]{:S(2)}) %collective-permute-start.12) | collective-permute-done | bytes 180256 | tf_op jit(solution)/shard_map/ppermute | solution.py:448
  43.6 0.3 collective-permute-done.13.refs_7_
  43.8 0.1 gather.1
  44.0 0.0 collective-permute-done.14.refs_1_
  44.0 1.0 %encode.2 = s16[528,256]{1,0:T(8,128)(2,1)S(1)} custom-call(s32[1]{0:T(128)} %bitcast.own_ref, s32[1]{0:T(128)} %bitcast.1.shard_ref, bf16[4,512,1280]{2,1,0:T(8,128)(2,1)S(1)} %get-tuple-element.30.refs_0_, bf16[4,512,1280]{2,1,0:T(8,128)(2,1)S(1)} %collective-permute-done.14.refs_1_, bf16[256,1280]{1,0:T(8,128)(2,1)S(1)} %get-tuple-element.33.refs_2_, ...), custom_call_target="tpu_custom_call" | custom-call | flops 1000 | tf_op jit(solution)/shard_map/encode/pallas_call | solution.py:317
  44.9 0.1 collective-permute-start.15
  45.0 1.0 %encode.3 = s16[528,256]{1,0:T(8,128)(2,1)S(1)} custom-call(s32[1]{0:T(128)} %bitcast.own_ref, s32[1]{0:T(128)} %bitcast.1.shard_ref, bf16[4,512,1280]{2,1,0:T(8,128)(2,1)S(1)} %get-tuple-element.30.refs_0_, bf16[4,512,1280]{2,1,0:T(8,128)(2,1)S(1)} %collective-permute-done.14.refs_1_, bf16[256,1280]{1,0:T(8,128)(2,1)S(1)} %get-tuple-element.33.refs_2_, ...), custom_call_target="tpu_custom_call" | custom-call | flops 1000 | tf_op jit(solution)/shard_map/encode/pallas_call | solution.py:317
  46.0 0.0 copy-start
  46.0 1.9 %collective-permute-start.17 = (s16[528,256]{1,0:T(8,128)(2,1)S(1)}, s16[528,256]{1,0:T(8,128)(2,1)S(1)}, u32[]{:S(2)}, u32[]{:S(2)}) collective-permute-start(s16[528,256]{1,0:T(8,128)(2,1)S(1)} %encode.3), channel_id=1, source_target_pairs={{0,2},{1,3},{2,0},{3,1},{4,6},{5,7},{6,4},{7,5},{8,10},{9,11},{10,... | collective-permute-start | bytes 811016 | tf_op jit(solution)/shard_map/ppermute | solution.py:448
  48.0 0.9 %share.1.value_ref = f32[512,256]{1,0:T(8,128)S(1)} custom-call(s32[1]{0:T(128)} %bitcast.own_ref, s32[1]{0:T(128)} %bitcast.1.shard_ref, bf16[4,512,1280]{2,1,0:T(8,128)(2,1)S(1)} %get-tuple-element.30.refs_0_, bf16[4,512,1280]{2,1,0:T(8,128)(2,1)S(1)} %collective-permute-done.14.refs_1_, bf16[256,1280]{1,0:T(8,128)(2,1)S(1)} %get-tuple-element.33.refs_2_, ...), custom_call_target="tpu_custom_call" | custom-call | flops 1000 | tf_op jit(solution)/shard_map/share/pallas_call | solution.py:317
  48.8 5.8 %collective-permute-done.15.refs_4_.coded_ref = s16[528,256]{1,0:T(8,128)(2,1)S(1)} collective-permute-done((s16[528,256]{1,0:T(8,128)(2,1)S(1)}, s16[528,256]{1,0:T(8,128)(2,1)S(1)}, u32[]{:S(2)}, u32[]{:S(2)}) %collective-permute-start.15) | collective-permute-done | bytes 270368 | tf_op jit(solution)/shard_map/ppermute | solution.py:452
  54.6 0.2 relay.1
  54.8 1.3 %collective-permute-start.16 = (s16[528,256]{1,0:T(8,128)(2,1)S(1)}, s16[528,256]{1,0:T(8,128)(2,1)S(1)}, u32[]{:S(2)}, u32[]{:S(2)}) collective-permute-start(s16[528,256]{1,0:T(8,128)(2,1)S(1)} %relay.1), channel_id=1, source_target_pairs={{0,6},{1,7},{2,4},{3,5},{4,2},{5,3},{6,0},{7,1},{8,14},{9,15},{10,... | collective-permute-start | bytes 811016 | tf_op jit(solution)/shard_map/ppermute | solution.py:448
  56.1 0.0 copy-done
  56.1 0.9 %place.1 = (bf16[512,256]{1,0:T(8,128)(2,1)S(1)}, f32[1,512]{1,0:T(1,128)}) custom-call(s32[1]{0:T(128)} %bitcast.own_ref, s32[1]{0:T(128)} %bitcast.1.shard_ref, s32[1,512]{1,0:T(1,128)S(1)} %bitcast.5, f32[256,1]{1,0:T(8,128)S(1)} %get-tuple-element.28.loss_ref), custom_call_target="tpu_custom_call" | custom-call | flops 134217728 | tf_op jit(solution)/shard_map/place/pallas_call | solution.py:317
  57.0 0.9 %keep.1.sum_ref = f32[512,256]{1,0:T(8,128)S(1)} custom-call(s32[1]{0:T(128)} %bitcast.own_ref, s32[1]{0:T(128)} %bitcast.1.shard_ref, bf16[4,512,1280]{2,1,0:T(8,128)(2,1)S(1)} %get-tuple-element.30.refs_0_, bf16[4,512,1280]{2,1,0:T(8,128)(2,1)S(1)} %collective-permute-done.14.refs_1_, bf16[256,1280]{1,0:T(8,128)(2,1)S(1)} %get-tuple-element.33.refs_2_, ...), custom_call_target="tpu_custom_call" | custom-call | flops 1000 | tf_op jit(solution)/shard_map/keep/pallas_call | solution.py:317
  57.9 3.0 %collective-permute-done.17.refs_1_ = s16[528,256]{1,0:T(8,128)(2,1)S(1)} collective-permute-done((s16[528,256]{1,0:T(8,128)(2,1)S(1)}, s16[528,256]{1,0:T(8,128)(2,1)S(1)}, u32[]{:S(2)}, u32[]{:S(2)}) %collective-permute-start.17) | collective-permute-done | bytes 270368 | tf_op jit(solution)/shard_map/ppermute | solution.py:448
  60.9 5.4 %collective-permute-done.16.refs_0_ = s16[528,256]{1,0:T(8,128)(2,1)S(1)} collective-permute-done((s16[528,256]{1,0:T(8,128)(2,1)S(1)}, s16[528,256]{1,0:T(8,128)(2,1)S(1)}, u32[]{:S(2)}, u32[]{:S(2)}) %collective-permute-start.16) | collective-permute-done | bytes 270368 | tf_op jit(solution)/shard_map/ppermute | solution.py:448
  66.3 1.7 %finish.1 = f32[1,512,512]{2,1,0:T(8,128)} custom-call(bf16[512,256]{1,0:T(8,128)(2,1)S(1)} %get-tuple-element.29.place_ref, f32[512,256]{1,0:T(8,128)S(1)} %keep.1.sum_ref, s16[528,256]{1,0:T(8,128)(2,1)S(1)} %collective-permute-done.16.refs_0_, s16[528,256]{1,0:T(8,128)(2,1)S(1)} %collective-permute-done.17.refs_1_), custom_call_target="tpu_custom_call" | custom-call | flops 1000 | tf_op jit(solution)/shard_map/finish/pallas_call | solution.py:435
  (1 shorter events, 0.0 us)
Async XLA Ops:
  7.9 8.0 %collective-permute-start = (bf16[64,1280]{1,0:T(8,128)(2,1)S(1)}, bf16[64,1280]{1,0:T(8,128)(2,1)S(1)}, u32[]{:S(2)}, u32[]{:S(2)}) collective-permute-start(bf16[64,1280]{1,0:T(8,128)(2,1)S(1)} %get-tuple-element.21), channel_id=1, source_target_pairs={{0,8},{8,0},{16,24},{24,16},{1,9},{9,1},{17,25},{25,17},{2,10},{10... | collective-permute-start | bytes 491528 | tf_op jit(solution)/shard_map/ppermute | solution.py:448
  10.9 9.2 %collective-permute-start.1 = (bf16[64,1280]{1,0:T(8,128)(2,1)S(1)}, bf16[64,1280]{1,0:T(8,128)(2,1)S(1)}, u32[]{:S(2)}, u32[]{:S(2)}) collective-permute-start(bf16[64,1280]{1,0:T(8,128)(2,1)S(1)} %get-tuple-element.22), channel_id=1, source_target_pairs={{0,16},{8,24},{16,0},{24,8},{1,17},{9,25},{17,1},{25,9},{2,18},{10... | collective-permute-start | bytes 491528 | tf_op jit(solution)/shard_map/ppermute | solution.py:448
  12.5 7.7 %collective-permute-start.2 = (bf16[64,1280]{1,0:T(8,128)(2,1)S(1)}, bf16[64,1280]{1,0:T(8,128)(2,1)S(1)}, u32[]{:S(2)}, u32[]{:S(2)}) collective-permute-start(bf16[64,1280]{1,0:T(8,128)(2,1)S(1)} %get-tuple-element.23), channel_id=1, source_target_pairs={{0,24},{8,16},{16,8},{24,0},{1,25},{9,17},{17,9},{25,1},{2,26},{10... | collective-permute-start | bytes 491528 | tf_op jit(solution)/shard_map/ppermute | solution.py:448
  21.0 1.2 %collective-permute-start.3 = (f32[32,128]{1,0:T(8,128)S(1)}, f32[32,128]{1,0:T(8,128)S(1)}, u32[]{:S(2)}, u32[]{:S(2)}) collective-permute-start(f32[32,128]{1,0:T(8,128)S(1)} %stats.1.refs_0_), channel_id=1, source_target_pairs={{0,1},{1,0},{2,3},{3,2},{4,5},{5,4},{6,7},{7,6},{8,9},{9,8},{10,11... | collective-permute-start | bytes 49160 | tf_op jit(solution)/shard_map/ppermute | solution.py:448
  22.2 21.7 %collective-permute-start.14 = (bf16[4,512,1280]{2,1,0:T(8,128)(2,1)S(1)}, bf16[4,512,1280]{2,1,0:T(8,128)(2,1)S(1)}, u32[]{:S(2)}, u32[]{:S(2)}) collective-permute-start(bf16[4,512,1280]{2,1,0:T(8,128)(2,1)S(1)} %get-tuple-element.32), channel_id=1, source_target_pairs={{0,1},{1,0},{2,3},{3,2},{4,5},{5,4},{6,7},{7,6},{8,9},{9,8},{10,11... | collective-permute-start | bytes 15728648 | tf_op jit(solution)/shard_map/ppermute | solution.py:448
  22.5 5.5 %collective-permute-start.4 = (f32[32,128]{1,0:T(8,128)S(1)}, f32[32,128]{1,0:T(8,128)S(1)}, u32[]{:S(2)}, u32[]{:S(2)}) collective-permute-start(f32[32,128]{1,0:T(8,128)S(1)} %merge.1.refs_0_), channel_id=1, source_target_pairs={{0,6},{1,7},{2,4},{3,5},{4,2},{5,3},{6,0},{7,1},{8,14},{9,15},{10,... | collective-permute-start | bytes 49160 | tf_op jit(solution)/shard_map/ppermute | solution.py:448
  26.1 4.6 %collective-permute-start.5 = (f32[32,128]{1,0:T(8,128)S(1)}, f32[32,128]{1,0:T(8,128)S(1)}, u32[]{:S(2)}, u32[]{:S(2)}) collective-permute-start(f32[32,128]{1,0:T(8,128)S(1)} %merge.1.refs_0_), channel_id=1, source_target_pairs={{0,4},{1,5},{2,6},{3,7},{4,0},{5,1},{6,2},{7,3},{8,12},{9,13},{10,... | collective-permute-start | bytes 49160 | tf_op jit(solution)/shard_map/ppermute | solution.py:448
  26.1 4.6 %collective-permute-start.6 = (f32[32,128]{1,0:T(8,128)S(1)}, f32[32,128]{1,0:T(8,128)S(1)}, u32[]{:S(2)}, u32[]{:S(2)}) collective-permute-start(f32[32,128]{1,0:T(8,128)S(1)} %merge.1.refs_0_), channel_id=1, source_target_pairs={{0,2},{1,3},{2,0},{3,1},{4,6},{5,7},{6,4},{7,5},{8,10},{9,11},{10,... | collective-permute-start | bytes 49160 | tf_op jit(solution)/shard_map/ppermute | solution.py:448
  31.6 7.3 %collective-permute-start.7 = (bf16[64,1408]{1,0:T(8,128)(2,1)S(1)}, bf16[64,1408]{1,0:T(8,128)(2,1)S(1)}, u32[]{:S(2)}, u32[]{:S(2)}) collective-permute-start(bf16[64,1408]{1,0:T(8,128)(2,1)S(1)} %get-tuple-element.25), channel_id=1, source_target_pairs={{0,8},{8,0},{16,24},{24,16},{1,9},{9,1},{17,25},{25,17},{2,10},{10... | collective-permute-start | bytes 540680 | tf_op jit(solution)/shard_map/ppermute | solution.py:448
  32.9 9.2 %collective-permute-start.8 = (bf16[64,1408]{1,0:T(8,128)(2,1)S(1)}, bf16[64,1408]{1,0:T(8,128)(2,1)S(1)}, u32[]{:S(2)}, u32[]{:S(2)}) collective-permute-start(bf16[64,1408]{1,0:T(8,128)(2,1)S(1)} %get-tuple-element.26), channel_id=1, source_target_pairs={{0,16},{8,24},{16,0},{24,8},{1,17},{9,25},{17,1},{25,9},{2,18},{10... | collective-permute-start | bytes 540680 | tf_op jit(solution)/shard_map/ppermute | solution.py:448
  33.7 8.4 %collective-permute-start.9 = (bf16[64,1408]{1,0:T(8,128)(2,1)S(1)}, bf16[64,1408]{1,0:T(8,128)(2,1)S(1)}, u32[]{:S(2)}, u32[]{:S(2)}) collective-permute-start(bf16[64,1408]{1,0:T(8,128)(2,1)S(1)} %get-tuple-element.27), channel_id=1, source_target_pairs={{0,24},{8,16},{16,8},{24,0},{1,25},{9,17},{17,9},{25,1},{2,26},{10... | collective-permute-start | bytes 540680 | tf_op jit(solution)/shard_map/ppermute | solution.py:448
  35.2 7.5 %collective-permute-start.10 = (bf16[64,1408]{1,0:T(8,128)(2,1)S(1)}, bf16[64,1408]{1,0:T(8,128)(2,1)S(1)}, u32[]{:S(2)}, u32[]{:S(2)}) collective-permute-start(bf16[64,1408]{1,0:T(8,128)(2,1)S(1)} %get-tuple-element.24.refs_0_), channel_id=1, source_target_pairs={{0,1},{1,0},{2,3},{3,2},{4,5},{5,4},{6,7},{7,6},{8,9},{9,8},{10,11... | collective-permute-start | bytes 540680 | tf_op jit(solution)/shard_map/ppermute | solution.py:448
  39.0 3.7 %collective-permute-start.11 = (bf16[64,1408]{1,0:T(8,128)(2,1)S(1)}, bf16[64,1408]{1,0:T(8,128)(2,1)S(1)}, u32[]{:S(2)}, u32[]{:S(2)}) collective-permute-start(bf16[64,1408]{1,0:T(8,128)(2,1)S(1)} %collective-permute-done.7.refs_1_), channel_id=1, source_target_pairs={{0,1},{1,0},{2,3},{3,2},{4,5},{5,4},{6,7},{7,6},{8,9},{9,8},{10,11... | collective-permute-start | bytes 540680 | tf_op jit(solution)/shard_map/ppermute | solution.py:448
  42.1 1.4 %collective-permute-start.12 = (bf16[64,1408]{1,0:T(8,128)(2,1)S(1)}, bf16[64,1408]{1,0:T(8,128)(2,1)S(1)}, u32[]{:S(2)}, u32[]{:S(2)}) collective-permute-start(bf16[64,1408]{1,0:T(8,128)(2,1)S(1)} %collective-permute-done.8.refs_2_), channel_id=1, source_target_pairs={{0,1},{1,0},{2,3},{3,2},{4,5},{5,4},{6,7},{7,6},{8,9},{9,8},{10,11... | collective-permute-start | bytes 540680 | tf_op jit(solution)/shard_map/ppermute | solution.py:448
  42.2 1.7 %collective-permute-start.13 = (bf16[64,1408]{1,0:T(8,128)(2,1)S(1)}, bf16[64,1408]{1,0:T(8,128)(2,1)S(1)}, u32[]{:S(2)}, u32[]{:S(2)}) collective-permute-start(bf16[64,1408]{1,0:T(8,128)(2,1)S(1)} %collective-permute-done.9.refs_3_), channel_id=1, source_target_pairs={{0,1},{1,0},{2,3},{3,2},{4,5},{5,4},{6,7},{7,6},{8,9},{9,8},{10,11... | collective-permute-start | bytes 540680 | tf_op jit(solution)/shard_map/ppermute | solution.py:448
  44.9 9.7 %collective-permute-start.15 = (s16[528,256]{1,0:T(8,128)(2,1)S(1)}, s16[528,256]{1,0:T(8,128)(2,1)S(1)}, u32[]{:S(2)}, u32[]{:S(2)}) collective-permute-start(s16[528,256]{1,0:T(8,128)(2,1)S(1)} %encode.2), channel_id=1, source_target_pairs={{0,2},{1,3},{6,4},{7,5},{2,6},{3,7},{4,0},{5,1},{8,10},{9,11},{14,... | collective-permute-start | bytes 811016 | tf_op jit(solution)/shard_map/ppermute | solution.py:452
  46.0 10.1 %copy-start = (s32[512]{0:T(512)S(1)}, s32[512]{0:T(512)}, u32[]{:S(2)}) copy-start(s32[512]{0:T(512)} %param.6) | copy-start | bytes 6148
  46.0 14.9 %collective-permute-start.17 = (s16[528,256]{1,0:T(8,128)(2,1)S(1)}, s16[528,256]{1,0:T(8,128)(2,1)S(1)}, u32[]{:S(2)}, u32[]{:S(2)}) collective-permute-start(s16[528,256]{1,0:T(8,128)(2,1)S(1)} %encode.3), channel_id=1, source_target_pairs={{0,2},{1,3},{2,0},{3,1},{4,6},{5,7},{6,4},{7,5},{8,10},{9,11},{10,... | collective-permute-start | bytes 811016 | tf_op jit(solution)/shard_map/ppermute | solution.py:448
  54.8 11.5 %collective-permute-start.16 = (s16[528,256]{1,0:T(8,128)(2,1)S(1)}, s16[528,256]{1,0:T(8,128)(2,1)S(1)}, u32[]{:S(2)}, u32[]{:S(2)}) collective-permute-start(s16[528,256]{1,0:T(8,128)(2,1)S(1)} %relay.1), channel_id=1, source_target_pairs={{0,6},{1,7},{2,4},{3,5},{4,2},{5,3},{6,0},{7,1},{8,14},{9,15},{10,... | collective-permute-start | bytes 811016 | tf_op jit(solution)/shard_map/ppermute | solution.py:448

commit v5 on v4

--- a/solution.py
+++ b/solution.py
@@ -238,8 +238,8 @@
 
 def grad_kernel(count, own_ref, shard_ref, meta_ref, *refs):
     stat_refs, refs = refs[:count], refs[count:]
-    peers = len(refs) // 2
-    logit_refs, grad_refs = refs[:peers], refs[peers:]
+    peers = len(refs) // 3
+    logit_refs, grad_refs, loss_refs = refs[:peers], refs[peers : 2 * peers], refs[2 * peers :]
     block, width = logit_refs[0].shape
     _, pair_slot, target_slot = stat_slots(peers)
     span = LANES * GROUP // block
@@ -260,12 +260,7 @@
             ahead = sum(mean[i, j] for j in range(peers) if j != i)
             back = sum(mean[j, i] for j in range(peers) if j != i)
             loss = norms[i] - at(total, target_slot + i) + (ahead + back) * third
-            terms = jnp.zeros((GROUP, LANES), jnp.float32)
-            for n in range(LOSS_TERMS):
-                term = loss.astype(jnp.bfloat16).astype(jnp.float32)
-                loss = loss - term
-                terms = jnp.where(lane == n, term, terms)
-            grad_refs[i][rows, width:] = terms.astype(jnp.bfloat16)
+            loss_refs[i][rows, :] = jnp.broadcast_to(loss, (GROUP, LANES))
             shift.append(1.0 + (peers - ahead) * third)
         for c in range(0, width, LANES):
             l = [ref[rows, c : c + LANES].astype(jnp.float32) for ref in logit_refs]
@@ -284,7 +279,8 @@
         functools.partial(grad_kernel, len(parts)),
         in_specs=[pl.BlockSpec(memory_space=pltpu.SMEM)] * 2
         + [pl.BlockSpec(memory_space=pltpu.VMEM)] * (1 + len(parts) + peers),
-        out_shape=[jax.ShapeDtypeStruct((block, width + LANES), jnp.bfloat16)] * peers,
+        out_shape=[jax.ShapeDtypeStruct((block, width), jnp.bfloat16)] * peers
+        + [jax.ShapeDtypeStruct((block, LANES), jnp.float32)] * peers,
         compiler_params=SMALL,
         cost_estimate=pl.CostEstimate(
             flops=20 * block * width * peers, bytes_accessed=4 * block * width * peers, transcendentals=block * width * peers
@@ -304,13 +300,12 @@
 
 
 def gather_kernel(peers, own_ref, shard_ref, *refs):
-    block_refs, (own_all, other_all, loss_ref) = refs[:-3], refs[-3:]
+    block_refs, (own_all, other_all) = refs[:-2], refs[-2:]
     block, width = block_refs[0].shape[0], own_all.shape[1]
     for k in range(peers):
         rows = slice(k * block, (k + 1) * block)
         own_all[rows, :] = block_refs[k][:, :width]
         other_all[rows, :] = block_refs[peers + k][:, :width]
-        loss_ref[rows, :] = jnp.sum(block_refs[k][:, width:].astype(jnp.float32), axis=1, keepdims=True)
 
 
 def vmem_call(kernel, outs, cost, name, ids, *arrays):
@@ -371,12 +366,13 @@
     refs[-1][...] = value
 
 
-def place_kernel(peers, own_ref, shard_ref, row_ref, loss_ref, place_ref, out_ref):
+def place_kernel(peers, own_ref, shard_ref, row_ref, *refs):
+    loss_refs, (place_ref, out_ref) = refs[:peers], refs[peers:]
     tokens, rows = place_ref.shape
     block = rows // peers
     rank = ranks_along(row_ref[...])
     here = rank == wanted_ranks(0, rows, own_ref[0], block)
-    out_ref[...] = jnp.sum(jnp.where(here, loss_ref[...], 0.0), axis=0, keepdims=True)
+    out_ref[...] = jnp.sum(jnp.where(here, jnp.concatenate([ref[:, 0:1] for ref in loss_refs], axis=0), 0.0), axis=0, keepdims=True)
 
     src = lax.broadcasted_iota(jnp.int32, (tokens, tokens), 0)
     dst = lax.broadcasted_iota(jnp.int32, (tokens, tokens), 1)
@@ -403,7 +399,7 @@
         "place",
         ids,
         labels,
-        losses,
+        *losses,
     )
 
 
@@ -485,15 +481,15 @@
     after = lambda array, *before: lax.optimization_barrier((array,) + before)[0]
     w_given = core_swap(after(w_theirs, part)) if by_core else None
     parts = [part] + [swap(part, "vocab", shards, 2 * mask) for mask in range(chips - 1, 0, -1)]
-    grads = across(gradients(ids, meta, parts, logits))
+    outs = gradients(ids, meta, parts, logits)
+    grads, losses = across(outs[:peers]), outs[peers:]
 
     cost = pl.CostEstimate(flops=1000, bytes_accessed=0, transcendentals=0)
     flat = ((rows, width), jnp.bfloat16)
     kernel = functools.partial(gather_kernel, peers)
-    outs = [flat, flat, ((rows, 1), jnp.float32)]
+    outs = [flat, flat]
     others = [core_swap(grad) for grad in grads]
-    own_grad, other_grad, losses = vmem_call(kernel, outs, cost, "gather", ids, *grads, *others)
-    placing, token_loss = place(ids, labels, losses, peers)
+    own_grad, other_grad = vmem_call(kernel, outs, cost, "gather", ids, *grads, *others)
     if by_core:
         operands = (w_mine, w_given, own_grad, other_grad)
         coded_shape, full = ((depth + CODE_ROWS, rows), jnp.int16), ((depth, rows), jnp.float32)
@@ -522,6 +518,8 @@
             head_weight[0], own_grad, (((1,), (1,)), ((), ())), preferred_element_type=jnp.float32
         )
         kept = lax.psum_scatter(share, "vocab", scatter_dimension=0, tiled=True)
+    losses = across([after(loss, kept) for loss in losses])
+    placing, token_loss = place(ids, labels, losses, peers)
     grad_hidden = finish(placing, kept, arrived)
     return grad_hidden, token_loss
 

time: 68.2 us -> 67.4 us (0.988)
  waiting for transfers between devices: 35 us -> 30.1 us
  starting transfers between devices: 16.6 us -> 20.8 us
    ppermute x17 -> x20, waiting for transfers between devices: 29.2 us -> 24.5 us  [swap(): return lax.ppermute(array, axis, [(i, i ^ mask) for i in range(size)])]
    ppermute x17 -> x20, starting transfers between devices: 16.5 us -> 20.7 us  [swap(): return lax.ppermute(array, axis, [(i, i ^ mask) for i in range(size)])]
  transfers between devices with their start and end apart: 18 -> 21, of which waited for: 12 -> 14; matrix products, arithmetic and copies ran while one was open for 0% -> 0% of each run, Pallas kernels for 7% -> 7%
where the time goes in v5:
time: 67.4 us; the launch traced here: 67.3 us
  waiting for transfers between devices  30.1 us (45%)
  starting transfers between devices  20.8 us (31%)
  Pallas kernels  15.6 us (23%)
  between operations  0.75 us (1%)
    ppermute x20, waiting for transfers between devices, swap(): return lax.ppermute(array, axis, [(i, i ^ mask) for i in range(size)])  24.5 us
    ppermute x20, starting transfers between devices, swap(): return lax.ppermute(array, axis, [(i, i ^ mask) for i in range(size)])  20.7 us
    pallas_call x1, Pallas kernels, project(): pl.pallas_call(functools.partial(project_kernel, chunk_start), in_specs=[...  7.28 us
    ppermute x1, waiting for transfers between devices, hop(): lax.ppermute(array, 'vocab', [(2 * a + c, 2 * b + c) for a, b in pairs fo...  5.58 us
    pallas_call x7, Pallas kernels, vmem_call(): pl.pallas_call(kernel, in_specs=[pl.BlockSpec(memory_space=pltpu.SMEM)] *...  4.89 us
    pallas_call x1, Pallas kernels, finish(): pl.pallas_call(finish_kernel, in_specs=[pl.BlockSpec(memory_space=pltpu.V...  1.68 us
  transfers between devices with their start and end apart: 21, of which 14 were waited for; matrix products, arithmetic and copies ran while one was open for 0% of the time, Pallas kernels for 7%

profile of v5, /device:TPU:0, one launch (start us, length us, event | category | flops | bytes accessed | tf_op | source)
XLA Modules:
  0.0 67.3 jit_solution(4289567947936317304)
XLA Ops:
  0.6 7.3 %project.1 = (bf16[4,512,1280]{2,1,0:T(8,128)(2,1)S(1)}, bf16[4,512,1280]{2,1,0:T(8,128)(2,1)S(1)}, f32[64,128]{1,0:T(8,128)S(1)}, bf16[64,1280]{1,0:T(8,128)(2,...) custom-call(s32[1]{0:T(128)} %bitcast.own_ref, ...), custom_call_target="tpu_custom_call" | custom-call | flops 3758096384 | tf_op jit(solution)/shard_map/project/pallas_call | solution.py:115
  7.9 3.0 %collective-permute-start = (bf16[64,1280]{1,0:T(8,128)(2,1)S(1)}, bf16[64,1280]{1,0:T(8,128)(2,1)S(1)}, u32[]{:S(2)}, u32[]{:S(2)}) collective-permute-start(bf16[64,1280]{1,0:T(8,128)(2,1)S(1)} %get-tuple-element.28), channel_id=1, source_target_pairs={{0,8},{8,0},{16,24},{24,16},{1,9},{9,1},{17,25},{25,17},{2,10},{10... | collective-permute-start | bytes 491528 | tf_op jit(solution)/shard_map/ppermute | solution.py:444
  10.9 1.5 %collective-permute-start.1 = (bf16[64,1280]{1,0:T(8,128)(2,1)S(1)}, bf16[64,1280]{1,0:T(8,128)(2,1)S(1)}, u32[]{:S(2)}, u32[]{:S(2)}) collective-permute-start(bf16[64,1280]{1,0:T(8,128)(2,1)S(1)} %get-tuple-element.29), channel_id=1, source_target_pairs={{0,16},{8,24},{16,0},{24,8},{1,17},{9,25},{17,1},{25,9},{2,18},{10... | collective-permute-start | bytes 491528 | tf_op jit(solution)/shard_map/ppermute | solution.py:444
  12.5 0.0 collective-permute-start.2
  12.5 3.5 %collective-permute-done.refs_1_.refs_5_ = bf16[64,1280]{1,0:T(8,128)(2,1)S(1)} collective-permute-done((bf16[64,1280]{1,0:T(8,128)(2,1)S(1)}, bf16[64,1280]{1,0:T(8,128)(2,1)S(1)}, u32[]{:S(2)}, u32[]{:S(2)}) %collective-permute-start) | collective-permute-done | bytes 163872 | tf_op jit(solution)/shard_map/ppermute | solution.py:444
  16.0 4.1 %collective-permute-done.1.refs_2_.refs_6_ = bf16[64,1280]{1,0:T(8,128)(2,1)S(1)} collective-permute-done((bf16[64,1280]{1,0:T(8,128)(2,1)S(1)}, bf16[64,1280]{1,0:T(8,128)(2,1)S(1)}, u32[]{:S(2)}, u32[]{:S(2)}) %collective-permute-start.1) | collective-permute-done | bytes 163872 | tf_op jit(solution)/shard_map/ppermute | solution.py:444
  20.1 0.0 collective-permute-done.2.refs_3_.refs_7_
  20.1 0.9 %stats.1.refs_0_ = f32[32,128]{1,0:T(8,128)S(1)} custom-call(s32[1]{0:T(128)} %bitcast.own_ref, s32[1]{0:T(128)} %bitcast.1.shard_ref, f32[64,128]{1,0:T(8,128)S(1)} %get-tuple-element.26.meta_ref, bf16[64,1280]{1,0:T(8,128)(2,1)S(1)} %get-tuple-element.27.refs_0_.refs_4_, bf16[64,1280]{1,0:T(8,128)(2,1)S(1)} %collective-permute-done.refs_1_.refs_5_, ...), custom_call_target="tpu_custom_call" | custom-call | flops 13107200 | bytes 655360 | tf_op jit(solution)/shard_map/stats/pallas_call | solution.py:201
  21.0 0.1 collective-permute-start.3
  21.1 1.2 %collective-permute-done.3.refs_1_ = f32[32,128]{1,0:T(8,128)S(1)} collective-permute-done((f32[32,128]{1,0:T(8,128)S(1)}, f32[32,128]{1,0:T(8,128)S(1)}, u32[]{:S(2)}, u32[]{:S(2)}) %collective-permute-start.3) | collective-permute-done | bytes 16416 | tf_op jit(solution)/shard_map/ppermute | solution.py:444
  22.2 0.2 collective-permute-start.7
  22.5 3.6 %collective-permute-start.4 = (f32[32,128]{1,0:T(8,128)S(1)}, f32[32,128]{1,0:T(8,128)S(1)}, u32[]{:S(2)}, u32[]{:S(2)}) collective-permute-start(f32[32,128]{1,0:T(8,128)S(1)} %merge.1.refs_0_), channel_id=1, source_target_pairs={{0,6},{1,7},{2,4},{3,5},{4,2},{5,3},{6,0},{7,1},{8,14},{9,15},{10,... | collective-permute-start | bytes 49160 | tf_op jit(solution)/shard_map/ppermute | solution.py:444
  26.1 0.0 collective-permute-start.5
  26.1 0.8 %collective-permute-start.6 = (f32[32,128]{1,0:T(8,128)S(1)}, f32[32,128]{1,0:T(8,128)S(1)}, u32[]{:S(2)}, u32[]{:S(2)}) collective-permute-start(f32[32,128]{1,0:T(8,128)S(1)} %merge.1.refs_0_), channel_id=1, source_target_pairs={{0,2},{1,3},{2,0},{3,1},{4,6},{5,7},{6,4},{7,5},{8,10},{9,11},{10,... | collective-permute-start | bytes 49160 | tf_op jit(solution)/shard_map/ppermute | solution.py:444
  26.9 1.1 %collective-permute-done.4.refs_1_ = f32[32,128]{1,0:T(8,128)S(1)} collective-permute-done((f32[32,128]{1,0:T(8,128)S(1)}, f32[32,128]{1,0:T(8,128)S(1)}, u32[]{:S(2)}, u32[]{:S(2)}) %collective-permute-start.4) | collective-permute-done | bytes 16416 | tf_op jit(solution)/shard_map/ppermute | solution.py:444
  28.0 2.7 %collective-permute-done.5.refs_2_ = f32[32,128]{1,0:T(8,128)S(1)} collective-permute-done((f32[32,128]{1,0:T(8,128)S(1)}, f32[32,128]{1,0:T(8,128)S(1)}, u32[]{:S(2)}, u32[]{:S(2)}) %collective-permute-start.5) | collective-permute-done | bytes 16416 | tf_op jit(solution)/shard_map/ppermute | solution.py:444
  30.7 0.0 collective-permute-done.6.refs_3_
  30.7 0.9 %gradients.1 = (bf16[64,1280]{1,0:T(8,128)(2,1)S(1)}, bf16[64,1280]{1,0:T(8,128)(2,1)S(1)}, bf16[64,1280]{1,0:T(8,128)(2,1)S(1)}, bf16[64,1280]{1,0:T(8,128)(2,1...) custom-call(s32[1]{0:T(128)} %bitcast.own_ref, ...), custom_call_target="tpu_custom_call" | custom-call | flops 6553600 | bytes 1310720 | tf_op jit(solution)/shard_map/gradients/pallas_call | solution.py:278
  31.6 1.3 %collective-permute-start.8 = (bf16[64,1280]{1,0:T(8,128)(2,1)S(1)}, bf16[64,1280]{1,0:T(8,128)(2,1)S(1)}, u32[]{:S(2)}, u32[]{:S(2)}) collective-permute-start(bf16[64,1280]{1,0:T(8,128)(2,1)S(1)} %get-tuple-element.36), channel_id=1, source_target_pairs={{0,8},{8,0},{16,24},{24,16},{1,9},{9,1},{17,25},{25,17},{2,10},{10... | collective-permute-start | bytes 491528 | tf_op jit(solution)/shard_map/ppermute | solution.py:444
  32.9 0.8 %collective-permute-start.9 = (bf16[64,1280]{1,0:T(8,128)(2,1)S(1)}, bf16[64,1280]{1,0:T(8,128)(2,1)S(1)}, u32[]{:S(2)}, u32[]{:S(2)}) collective-permute-start(bf16[64,1280]{1,0:T(8,128)(2,1)S(1)} %get-tuple-element.37), channel_id=1, source_target_pairs={{0,16},{8,24},{16,0},{24,8},{1,17},{9,25},{17,1},{25,9},{2,18},{10... | collective-permute-start | bytes 491528 | tf_op jit(solution)/shard_map/ppermute | solution.py:444
  33.7 1.4 %collective-permute-start.10 = (bf16[64,1280]{1,0:T(8,128)(2,1)S(1)}, bf16[64,1280]{1,0:T(8,128)(2,1)S(1)}, u32[]{:S(2)}, u32[]{:S(2)}) collective-permute-start(bf16[64,1280]{1,0:T(8,128)(2,1)S(1)} %get-tuple-element.38), channel_id=1, source_target_pairs={{0,24},{8,16},{16,8},{24,0},{1,25},{9,17},{17,9},{25,1},{2,26},{10... | collective-permute-start | bytes 491528 | tf_op jit(solution)/shard_map/ppermute | solution.py:444
  35.2 0.0 collective-permute-start.11
  35.2 3.3 %collective-permute-done.8.refs_1_ = bf16[64,1280]{1,0:T(8,128)(2,1)S(1)} collective-permute-done((bf16[64,1280]{1,0:T(8,128)(2,1)S(1)}, bf16[64,1280]{1,0:T(8,128)(2,1)S(1)}, u32[]{:S(2)}, u32[]{:S(2)}) %collective-permute-start.8) | collective-permute-done | bytes 163872 | tf_op jit(solution)/shard_map/ppermute | solution.py:444
  38.5 0.0 collective-permute-start.12
  38.5 2.9 %collective-permute-done.9.refs_2_ = bf16[64,1280]{1,0:T(8,128)(2,1)S(1)} collective-permute-done((bf16[64,1280]{1,0:T(8,128)(2,1)S(1)}, bf16[64,1280]{1,0:T(8,128)(2,1)S(1)}, u32[]{:S(2)}, u32[]{:S(2)}) %collective-permute-start.9) | collective-permute-done | bytes 163872 | tf_op jit(solution)/shard_map/ppermute | solution.py:444
  41.4 0.0 collective-permute-start.13
  41.4 0.0 collective-permute-done.10.refs_3_
  41.5 0.5 collective-permute-start.14
  42.0 0.0 collective-permute-done.11.refs_4_
  42.0 0.0 collective-permute-done.12.refs_5_
  42.0 0.9 %collective-permute-done.13.refs_6_ = bf16[64,1280]{1,0:T(8,128)(2,1)S(1)} collective-permute-done((bf16[64,1280]{1,0:T(8,128)(2,1)S(1)}, bf16[64,1280]{1,0:T(8,128)(2,1)S(1)}, u32[]{:S(2)}, u32[]{:S(2)}) %collective-permute-start.13) | collective-permute-done | bytes 163872 | tf_op jit(solution)/shard_map/ppermute | solution.py:444
  42.8 0.2 collective-permute-done.14.refs_7_
  43.1 0.1 gather.1
  43.2 0.0 collective-permute-done.7.refs_1_
  43.2 1.0 %encode.2 = s16[528,256]{1,0:T(8,128)(2,1)S(1)} custom-call(s32[1]{0:T(128)} %bitcast.own_ref, s32[1]{0:T(128)} %bitcast.1.shard_ref, bf16[4,512,1280]{2,1,0:T(8,128)(2,1)S(1)} %get-tuple-element.32.refs_0_, bf16[4,512,1280]{2,1,0:T(8,128)(2,1)S(1)} %collective-permute-done.7.refs_1_, bf16[256,1280]{1,0:T(8,128)(2,1)S(1)} %get-tuple-element.39.refs_2_, ...), custom_call_target="tpu_custom_call" | custom-call | flops 1000 | tf_op jit(solution)/shard_map/encode/pallas_call | solution.py:312
  44.2 0.1 collective-permute-start.15
  44.2 1.0 %encode.3 = s16[528,256]{1,0:T(8,128)(2,1)S(1)} custom-call(s32[1]{0:T(128)} %bitcast.own_ref, s32[1]{0:T(128)} %bitcast.1.shard_ref, bf16[4,512,1280]{2,1,0:T(8,128)(2,1)S(1)} %get-tuple-element.32.refs_0_, bf16[4,512,1280]{2,1,0:T(8,128)(2,1)S(1)} %collective-permute-done.7.refs_1_, bf16[256,1280]{1,0:T(8,128)(2,1)S(1)} %get-tuple-element.39.refs_2_, ...), custom_call_target="tpu_custom_call" | custom-call | flops 1000 | tf_op jit(solution)/shard_map/encode/pallas_call | solution.py:312
  45.2 2.2 %collective-permute-start.20 = (s16[528,256]{1,0:T(8,128)(2,1)S(1)}, s16[528,256]{1,0:T(8,128)(2,1)S(1)}, u32[]{:S(2)}, u32[]{:S(2)}) collective-permute-start(s16[528,256]{1,0:T(8,128)(2,1)S(1)} %encode.3), channel_id=1, source_target_pairs={{0,2},{1,3},{2,0},{3,1},{4,6},{5,7},{6,4},{7,5},{8,10},{9,11},{10,... | collective-permute-start | bytes 811016 | tf_op jit(solution)/shard_map/ppermute | solution.py:444
  47.4 0.9 %share.1.value_ref = f32[512,256]{1,0:T(8,128)S(1)} custom-call(s32[1]{0:T(128)} %bitcast.own_ref, s32[1]{0:T(128)} %bitcast.1.shard_ref, bf16[4,512,1280]{2,1,0:T(8,128)(2,1)S(1)} %get-tuple-element.32.refs_0_, bf16[4,512,1280]{2,1,0:T(8,128)(2,1)S(1)} %collective-permute-done.7.refs_1_, bf16[256,1280]{1,0:T(8,128)(2,1)S(1)} %get-tuple-element.39.refs_2_, ...), custom_call_target="tpu_custom_call" | custom-call | flops 1000 | tf_op jit(solution)/shard_map/share/pallas_call | solution.py:312
  48.3 5.6 %collective-permute-done.15.refs_4_.coded_ref = s16[528,256]{1,0:T(8,128)(2,1)S(1)} collective-permute-done((s16[528,256]{1,0:T(8,128)(2,1)S(1)}, s16[528,256]{1,0:T(8,128)(2,1)S(1)}, u32[]{:S(2)}, u32[]{:S(2)}) %collective-permute-start.15) | collective-permute-done | bytes 270368 | tf_op jit(solution)/shard_map/ppermute | solution.py:448
  53.9 0.2 relay.1
  54.1 0.0 copy-start
  54.1 1.7 %collective-permute-start.19 = (s16[528,256]{1,0:T(8,128)(2,1)S(1)}, s16[528,256]{1,0:T(8,128)(2,1)S(1)}, u32[]{:S(2)}, u32[]{:S(2)}) collective-permute-start(s16[528,256]{1,0:T(8,128)(2,1)S(1)} %relay.1), channel_id=1, source_target_pairs={{0,6},{1,7},{2,4},{3,5},{4,2},{5,3},{6,0},{7,1},{8,14},{9,15},{10,... | collective-permute-start | bytes 811016 | tf_op jit(solution)/shard_map/ppermute | solution.py:444
  55.8 0.9 %keep.1.sum_ref = f32[512,256]{1,0:T(8,128)S(1)} custom-call(s32[1]{0:T(128)} %bitcast.own_ref, s32[1]{0:T(128)} %bitcast.1.shard_ref, bf16[4,512,1280]{2,1,0:T(8,128)(2,1)S(1)} %get-tuple-element.32.refs_0_, bf16[4,512,1280]{2,1,0:T(8,128)(2,1)S(1)} %collective-permute-done.7.refs_1_, bf16[256,1280]{1,0:T(8,128)(2,1)S(1)} %get-tuple-element.39.refs_2_, ...), custom_call_target="tpu_custom_call" | custom-call | flops 1000 | tf_op jit(solution)/shard_map/keep/pallas_call | solution.py:312
  56.6 1.0 %collective-permute-start.16 = (f32[64,128]{1,0:T(8,128)S(1)}, f32[64,128]{1,0:T(8,128)S(1)}, u32[]{:S(2)}, u32[]{:S(2)}) collective-permute-start(f32[64,128]{1,0:T(8,128)S(1)} %get-tuple-element.43), channel_id=1, source_target_pairs={{0,8},{8,0},{16,24},{24,16},{1,9},{9,1},{17,25},{25,17},{2,10},{10... | collective-permute-start | bytes 98312 | tf_op jit(solution)/shard_map/ppermute | solution.py:444
  57.7 1.2 %collective-permute-start.17 = (f32[64,128]{1,0:T(8,128)S(1)}, f32[64,128]{1,0:T(8,128)S(1)}, u32[]{:S(2)}, u32[]{:S(2)}) collective-permute-start(f32[64,128]{1,0:T(8,128)S(1)} %get-tuple-element.45), channel_id=1, source_target_pairs={{0,16},{8,24},{16,0},{24,8},{1,17},{9,25},{17,1},{25,9},{2,18},{10... | collective-permute-start | bytes 98312 | tf_op jit(solution)/shard_map/ppermute | solution.py:444
  58.9 1.3 %collective-permute-start.18 = (f32[64,128]{1,0:T(8,128)S(1)}, f32[64,128]{1,0:T(8,128)S(1)}, u32[]{:S(2)}, u32[]{:S(2)}) collective-permute-start(f32[64,128]{1,0:T(8,128)S(1)} %get-tuple-element.47), channel_id=1, source_target_pairs={{0,24},{8,16},{16,8},{24,0},{1,25},{9,17},{17,9},{25,1},{2,26},{10... | collective-permute-start | bytes 98312 | tf_op jit(solution)/shard_map/ppermute | solution.py:444
  60.2 0.7 %collective-permute-done.16.refs_1_ = f32[64,128]{1,0:T(8,128)S(1)} collective-permute-done((f32[64,128]{1,0:T(8,128)S(1)}, f32[64,128]{1,0:T(8,128)S(1)}, u32[]{:S(2)}, u32[]{:S(2)}) %collective-permute-start.16) | collective-permute-done | bytes 32800 | tf_op jit(solution)/shard_map/ppermute | solution.py:444
  60.9 0.7 %collective-permute-done.17.refs_2_ = f32[64,128]{1,0:T(8,128)S(1)} collective-permute-done((f32[64,128]{1,0:T(8,128)S(1)}, f32[64,128]{1,0:T(8,128)S(1)}, u32[]{:S(2)}, u32[]{:S(2)}) %collective-permute-start.17) | collective-permute-done | bytes 32800 | tf_op jit(solution)/shard_map/ppermute | solution.py:444
  61.7 2.0 %collective-permute-done.18.refs_3_ = f32[64,128]{1,0:T(8,128)S(1)} collective-permute-done((f32[64,128]{1,0:T(8,128)S(1)}, f32[64,128]{1,0:T(8,128)S(1)}, u32[]{:S(2)}, u32[]{:S(2)}) %collective-permute-start.18) | collective-permute-done | bytes 32800 | tf_op jit(solution)/shard_map/ppermute | solution.py:444
  63.7 0.0 copy-done
  63.7 0.9 %place.1 = (bf16[512,256]{1,0:T(8,128)(2,1)S(1)}, f32[1,512]{1,0:T(1,128)}) custom-call(s32[1]{0:T(128)} %bitcast.own_ref, s32[1]{0:T(128)} %bitcast.1.shard_ref, s32[1,512]{1,0:T(1,128)S(1)} %bitcast.5, f32[64,128]{1,0:T(8,128)S(1)} %get-tuple-element.41.refs_0_, f32[64,128]{1,0:T(8,128)S(1)} %collective-permute-done.16.refs_1_, ...), custom_call_target="tpu_custom_call" | custom-call | flops 134217728 | tf_op jit(solution)/shard_map/place/pallas_call | solution.py:312
  64.6 0.0 collective-permute-done.20.refs_1_
  64.6 0.9 %collective-permute-done.19.refs_0_ = s16[528,256]{1,0:T(8,128)(2,1)S(1)} collective-permute-done((s16[528,256]{1,0:T(8,128)(2,1)S(1)}, s16[528,256]{1,0:T(8,128)(2,1)S(1)}, u32[]{:S(2)}, u32[]{:S(2)}) %collective-permute-start.19) | collective-permute-done | bytes 270368 | tf_op jit(solution)/shard_map/ppermute | solution.py:444
  65.6 1.7 %finish.1 = f32[1,512,512]{2,1,0:T(8,128)} custom-call(bf16[512,256]{1,0:T(8,128)(2,1)S(1)} %get-tuple-element.48.place_ref, f32[512,256]{1,0:T(8,128)S(1)} %keep.1.sum_ref, s16[528,256]{1,0:T(8,128)(2,1)S(1)} %collective-permute-done.19.refs_0_, s16[528,256]{1,0:T(8,128)(2,1)S(1)} %collective-permute-done.20.refs_1_), custom_call_target="tpu_custom_call" | custom-call | flops 1000 | tf_op jit(solution)/shard_map/finish/pallas_call | solution.py:431
  (1 shorter events, 0.0 us)
Async XLA Ops:
  7.9 8.0 %collective-permute-start = (bf16[64,1280]{1,0:T(8,128)(2,1)S(1)}, bf16[64,1280]{1,0:T(8,128)(2,1)S(1)}, u32[]{:S(2)}, u32[]{:S(2)}) collective-permute-start(bf16[64,1280]{1,0:T(8,128)(2,1)S(1)} %get-tuple-element.28), channel_id=1, source_target_pairs={{0,8},{8,0},{16,24},{24,16},{1,9},{9,1},{17,25},{25,17},{2,10},{10... | collective-permute-start | bytes 491528 | tf_op jit(solution)/shard_map/ppermute | solution.py:444
  10.9 9.2 %collective-permute-start.1 = (bf16[64,1280]{1,0:T(8,128)(2,1)S(1)}, bf16[64,1280]{1,0:T(8,128)(2,1)S(1)}, u32[]{:S(2)}, u32[]{:S(2)}) collective-permute-start(bf16[64,1280]{1,0:T(8,128)(2,1)S(1)} %get-tuple-element.29), channel_id=1, source_target_pairs={{0,16},{8,24},{16,0},{24,8},{1,17},{9,25},{17,1},{25,9},{2,18},{10... | collective-permute-start | bytes 491528 | tf_op jit(solution)/shard_map/ppermute | solution.py:444
  12.5 7.7 %collective-permute-start.2 = (bf16[64,1280]{1,0:T(8,128)(2,1)S(1)}, bf16[64,1280]{1,0:T(8,128)(2,1)S(1)}, u32[]{:S(2)}, u32[]{:S(2)}) collective-permute-start(bf16[64,1280]{1,0:T(8,128)(2,1)S(1)} %get-tuple-element.30), channel_id=1, source_target_pairs={{0,24},{8,16},{16,8},{24,0},{1,25},{9,17},{17,9},{25,1},{2,26},{10... | collective-permute-start | bytes 491528 | tf_op jit(solution)/shard_map/ppermute | solution.py:444
  21.0 1.2 %collective-permute-start.3 = (f32[32,128]{1,0:T(8,128)S(1)}, f32[32,128]{1,0:T(8,128)S(1)}, u32[]{:S(2)}, u32[]{:S(2)}) collective-permute-start(f32[32,128]{1,0:T(8,128)S(1)} %stats.1.refs_0_), channel_id=1, source_target_pairs={{0,1},{1,0},{2,3},{3,2},{4,5},{5,4},{6,7},{7,6},{8,9},{9,8},{10,11... | collective-permute-start | bytes 49160 | tf_op jit(solution)/shard_map/ppermute | solution.py:444
  22.2 20.9 %collective-permute-start.7 = (bf16[4,512,1280]{2,1,0:T(8,128)(2,1)S(1)}, bf16[4,512,1280]{2,1,0:T(8,128)(2,1)S(1)}, u32[]{:S(2)}, u32[]{:S(2)}) collective-permute-start(bf16[4,512,1280]{2,1,0:T(8,128)(2,1)S(1)} %get-tuple-element.34), channel_id=1, source_target_pairs={{0,1},{1,0},{2,3},{3,2},{4,5},{5,4},{6,7},{7,6},{8,9},{9,8},{10,11... | collective-permute-start | bytes 15728648 | tf_op jit(solution)/shard_map/ppermute | solution.py:444
  22.5 5.5 %collective-permute-start.4 = (f32[32,128]{1,0:T(8,128)S(1)}, f32[32,128]{1,0:T(8,128)S(1)}, u32[]{:S(2)}, u32[]{:S(2)}) collective-permute-start(f32[32,128]{1,0:T(8,128)S(1)} %merge.1.refs_0_), channel_id=1, source_target_pairs={{0,6},{1,7},{2,4},{3,5},{4,2},{5,3},{6,0},{7,1},{8,14},{9,15},{10,... | collective-permute-start | bytes 49160 | tf_op jit(solution)/shard_map/ppermute | solution.py:444
  26.1 4.6 %collective-permute-start.5 = (f32[32,128]{1,0:T(8,128)S(1)}, f32[32,128]{1,0:T(8,128)S(1)}, u32[]{:S(2)}, u32[]{:S(2)}) collective-permute-start(f32[32,128]{1,0:T(8,128)S(1)} %merge.1.refs_0_), channel_id=1, source_target_pairs={{0,4},{1,5},{2,6},{3,7},{4,0},{5,1},{6,2},{7,3},{8,12},{9,13},{10,... | collective-permute-start | bytes 49160 | tf_op jit(solution)/shard_map/ppermute | solution.py:444
  26.1 4.6 %collective-permute-start.6 = (f32[32,128]{1,0:T(8,128)S(1)}, f32[32,128]{1,0:T(8,128)S(1)}, u32[]{:S(2)}, u32[]{:S(2)}) collective-permute-start(f32[32,128]{1,0:T(8,128)S(1)} %merge.1.refs_0_), channel_id=1, source_target_pairs={{0,2},{1,3},{2,0},{3,1},{4,6},{5,7},{6,4},{7,5},{8,10},{9,11},{10,... | collective-permute-start | bytes 49160 | tf_op jit(solution)/shard_map/ppermute | solution.py:444
  31.6 6.9 %collective-permute-start.8 = (bf16[64,1280]{1,0:T(8,128)(2,1)S(1)}, bf16[64,1280]{1,0:T(8,128)(2,1)S(1)}, u32[]{:S(2)}, u32[]{:S(2)}) collective-permute-start(bf16[64,1280]{1,0:T(8,128)(2,1)S(1)} %get-tuple-element.36), channel_id=1, source_target_pairs={{0,8},{8,0},{16,24},{24,16},{1,9},{9,1},{17,25},{25,17},{2,10},{10... | collective-permute-start | bytes 491528 | tf_op jit(solution)/shard_map/ppermute | solution.py:444
  32.9 8.5 %collective-permute-start.9 = (bf16[64,1280]{1,0:T(8,128)(2,1)S(1)}, bf16[64,1280]{1,0:T(8,128)(2,1)S(1)}, u32[]{:S(2)}, u32[]{:S(2)}) collective-permute-start(bf16[64,1280]{1,0:T(8,128)(2,1)S(1)} %get-tuple-element.37), channel_id=1, source_target_pairs={{0,16},{8,24},{16,0},{24,8},{1,17},{9,25},{17,1},{25,9},{2,18},{10... | collective-permute-start | bytes 491528 | tf_op jit(solution)/shard_map/ppermute | solution.py:444
  33.7 7.7 %collective-permute-start.10 = (bf16[64,1280]{1,0:T(8,128)(2,1)S(1)}, bf16[64,1280]{1,0:T(8,128)(2,1)S(1)}, u32[]{:S(2)}, u32[]{:S(2)}) collective-permute-start(bf16[64,1280]{1,0:T(8,128)(2,1)S(1)} %get-tuple-element.38), channel_id=1, source_target_pairs={{0,24},{8,16},{16,8},{24,0},{1,25},{9,17},{17,9},{25,1},{2,26},{10... | collective-permute-start | bytes 491528 | tf_op jit(solution)/shard_map/ppermute | solution.py:444
  35.2 6.8 %collective-permute-start.11 = (bf16[64,1280]{1,0:T(8,128)(2,1)S(1)}, bf16[64,1280]{1,0:T(8,128)(2,1)S(1)}, u32[]{:S(2)}, u32[]{:S(2)}) collective-permute-start(bf16[64,1280]{1,0:T(8,128)(2,1)S(1)} %get-tuple-element.35.refs_0_), channel_id=1, source_target_pairs={{0,1},{1,0},{2,3},{3,2},{4,5},{5,4},{6,7},{7,6},{8,9},{9,8},{10,11... | collective-permute-start | bytes 491528 | tf_op jit(solution)/shard_map/ppermute | solution.py:444
  38.5 3.5 %collective-permute-start.12 = (bf16[64,1280]{1,0:T(8,128)(2,1)S(1)}, bf16[64,1280]{1,0:T(8,128)(2,1)S(1)}, u32[]{:S(2)}, u32[]{:S(2)}) collective-permute-start(bf16[64,1280]{1,0:T(8,128)(2,1)S(1)} %collective-permute-done.8.refs_1_), channel_id=1, source_target_pairs={{0,1},{1,0},{2,3},{3,2},{4,5},{5,4},{6,7},{7,6},{8,9},{9,8},{10,11... | collective-permute-start | bytes 491528 | tf_op jit(solution)/shard_map/ppermute | solution.py:444
  41.4 1.4 %collective-permute-start.13 = (bf16[64,1280]{1,0:T(8,128)(2,1)S(1)}, bf16[64,1280]{1,0:T(8,128)(2,1)S(1)}, u32[]{:S(2)}, u32[]{:S(2)}) collective-permute-start(bf16[64,1280]{1,0:T(8,128)(2,1)S(1)} %collective-permute-done.9.refs_2_), channel_id=1, source_target_pairs={{0,1},{1,0},{2,3},{3,2},{4,5},{5,4},{6,7},{7,6},{8,9},{9,8},{10,11... | collective-permute-start | bytes 491528 | tf_op jit(solution)/shard_map/ppermute | solution.py:444
  41.5 1.6 %collective-permute-start.14 = (bf16[64,1280]{1,0:T(8,128)(2,1)S(1)}, bf16[64,1280]{1,0:T(8,128)(2,1)S(1)}, u32[]{:S(2)}, u32[]{:S(2)}) collective-permute-start(bf16[64,1280]{1,0:T(8,128)(2,1)S(1)} %collective-permute-done.10.refs_3_), channel_id=1, source_target_pairs={{0,1},{1,0},{2,3},{3,2},{4,5},{5,4},{6,7},{7,6},{8,9},{9,8},{10,11... | collective-permute-start | bytes 491528 | tf_op jit(solution)/shard_map/ppermute | solution.py:444
  44.2 9.7 %collective-permute-start.15 = (s16[528,256]{1,0:T(8,128)(2,1)S(1)}, s16[528,256]{1,0:T(8,128)(2,1)S(1)}, u32[]{:S(2)}, u32[]{:S(2)}) collective-permute-start(s16[528,256]{1,0:T(8,128)(2,1)S(1)} %encode.2), channel_id=1, source_target_pairs={{0,2},{1,3},{6,4},{7,5},{2,6},{3,7},{4,0},{5,1},{8,10},{9,11},{14,... | collective-permute-start | bytes 811016 | tf_op jit(solution)/shard_map/ppermute | solution.py:448
  45.2 19.4 %collective-permute-start.20 = (s16[528,256]{1,0:T(8,128)(2,1)S(1)}, s16[528,256]{1,0:T(8,128)(2,1)S(1)}, u32[]{:S(2)}, u32[]{:S(2)}) collective-permute-start(s16[528,256]{1,0:T(8,128)(2,1)S(1)} %encode.3), channel_id=1, source_target_pairs={{0,2},{1,3},{2,0},{3,1},{4,6},{5,7},{6,4},{7,5},{8,10},{9,11},{10,... | collective-permute-start | bytes 811016 | tf_op jit(solution)/shard_map/ppermute | solution.py:444
  54.1 9.6 %copy-start = (s32[512]{0:T(512)S(1)}, s32[512]{0:T(512)}, u32[]{:S(2)}) copy-start(s32[512]{0:T(512)} %param.6) | copy-start | bytes 6148
  54.1 11.5 %collective-permute-start.19 = (s16[528,256]{1,0:T(8,128)(2,1)S(1)}, s16[528,256]{1,0:T(8,128)(2,1)S(1)}, u32[]{:S(2)}, u32[]{:S(2)}) collective-permute-start(s16[528,256]{1,0:T(8,128)(2,1)S(1)} %relay.1), channel_id=1, source_target_pairs={{0,6},{1,7},{2,4},{3,5},{4,2},{5,3},{6,0},{7,1},{8,14},{9,15},{10,... | collective-permute-start | bytes 811016 | tf_op jit(solution)/shard_map/ppermute | solution.py:444
  56.6 4.3 %collective-permute-start.16 = (f32[64,128]{1,0:T(8,128)S(1)}, f32[64,128]{1,0:T(8,128)S(1)}, u32[]{:S(2)}, u32[]{:S(2)}) collective-permute-start(f32[64,128]{1,0:T(8,128)S(1)} %get-tuple-element.43), channel_id=1, source_target_pairs={{0,8},{8,0},{16,24},{24,16},{1,9},{9,1},{17,25},{25,17},{2,10},{10... | collective-permute-start | bytes 98312 | tf_op jit(solution)/shard_map/ppermute | solution.py:444
  57.7 4.0 %collective-permute-start.17 = (f32[64,128]{1,0:T(8,128)S(1)}, f32[64,128]{1,0:T(8,128)S(1)}, u32[]{:S(2)}, u32[]{:S(2)}) collective-permute-start(f32[64,128]{1,0:T(8,128)S(1)} %get-tuple-element.45), channel_id=1, source_target_pairs={{0,16},{8,24},{16,0},{24,8},{1,17},{9,25},{17,1},{25,9},{2,18},{10... | collective-permute-start | bytes 98312 | tf_op jit(solution)/shard_map/ppermute | solution.py:444
  58.9 4.8 %collective-permute-start.18 = (f32[64,128]{1,0:T(8,128)S(1)}, f32[64,128]{1,0:T(8,128)S(1)}, u32[]{:S(2)}, u32[]{:S(2)}) collective-permute-start(f32[64,128]{1,0:T(8,128)S(1)} %get-tuple-element.47), channel_id=1, source_target_pairs={{0,24},{8,16},{16,8},{24,0},{1,25},{9,17},{17,9},{25,1},{2,26},{10... | collective-permute-start | bytes 98312 | tf_op jit(solution)/shard_map/ppermute | solution.py:444

commit v6 on v5

--- a/solution.py
+++ b/solution.py
@@ -299,13 +299,10 @@
     return share_of(mine_ref, index, own_ref[...]) + share_of(theirs_ref, index, other_ref[...])
 
 
-def gather_kernel(peers, own_ref, shard_ref, *refs):
-    block_refs, (own_all, other_all) = refs[:-2], refs[-2:]
-    block, width = block_refs[0].shape[0], own_all.shape[1]
-    for k in range(peers):
-        rows = slice(k * block, (k + 1) * block)
-        own_all[rows, :] = block_refs[k][:, :width]
-        other_all[rows, :] = block_refs[peers + k][:, :width]
+def gather_kernel(own_ref, shard_ref, *refs):
+    block = refs[0].shape[0]
+    for k, ref in enumerate(refs[:-1]):
+        refs[-1][k * block : (k + 1) * block, :] = ref[...]
 
 
 def vmem_call(kernel, outs, cost, name, ids, *arrays):
@@ -353,6 +350,14 @@
 
 def relay_kernel(own_ref, shard_ref, value_ref, coded_ref, out_ref):
     put_coded(out_ref, value_ref[...] + jnp.where(is_middle(shard_ref), get_coded(coded_ref), 0.0))
+
+
+def own_sum_kernel(mask, own_ref, shard_ref, mine_ref, grad_ref, out_ref):
+    out_ref[...] = share_of(mine_ref, (shard_ref[0] // 2) ^ mask, grad_ref[...])
+
+
+def add_kernel(mask, own_ref, shard_ref, theirs_ref, grad_ref, part_ref, out_ref):
+    put_coded(out_ref, part_ref[...] + share_of(theirs_ref, (shard_ref[0] // 2) ^ mask, grad_ref[...]))
 
 
 def sum_kernel(mask, own_ref, shard_ref, *refs):
@@ -486,10 +491,9 @@
 
     cost = pl.CostEstimate(flops=1000, bytes_accessed=0, transcendentals=0)
     flat = ((rows, width), jnp.bfloat16)
-    kernel = functools.partial(gather_kernel, peers)
-    outs = [flat, flat]
     others = [core_swap(grad) for grad in grads]
-    own_grad, other_grad = vmem_call(kernel, outs, cost, "gather", ids, *grads, *others)
+    (own_grad,) = vmem_call(gather_kernel, [flat], cost, "gather", ids, *grads)
+    (other_grad,) = vmem_call(gather_kernel, [flat], cost, "gather", ids, *others)
     if by_core:
         operands = (w_mine, w_given, own_grad, other_grad)
         coded_shape, full = ((depth + CODE_ROWS, rows), jnp.int16), ((depth, rows), jnp.float32)
@@ -499,7 +503,11 @@
             return vmem_call(kernel, [coded_shape, *more], cost, "encode", ids, *operands)
 
         if chips == 4:
-            (two,) = encode(2)
+            full = ((depth, rows), jnp.float32)
+            kernel = functools.partial(own_sum_kernel, 2)
+            (part,) = vmem_call(kernel, [full], cost, "share", ids, w_mine, own_grad)
+            kernel = functools.partial(add_kernel, 2)
+            (two,) = vmem_call(kernel, [coded_shape], cost, "encode", ids, w_given, other_grad, part)
             first = hop(two, [(0, 1), (3, 2), (1, 3), (2, 0)])
             kernel = functools.partial(sum_kernel, 3)
             (three,) = vmem_call(kernel, [full], cost, "share", ids, *operands)

time: 67.4 us -> 67.1 us (level)
    pallas_call x7 -> x9, Pallas kernels: 4.89 us -> 5.1 us  [vmem_call(): pl.pallas_call(kernel, in_specs=[pl.BlockSpec(memory_space=pltpu.SMEM)] *...]
  transfers between devices with their start and end apart: 21 -> 21, of which waited for: 14 -> 14; matrix products, arithmetic and copies ran while one was open for 0% -> 0% of each run, Pallas kernels for 7% -> 8%
where the time goes in v6:
time: 67.1 us; the launch traced here: 66.9 us
  waiting for transfers between devices  29.5 us (44%)
  starting transfers between devices  20.8 us (31%)
  Pallas kernels  15.9 us (24%)
  between operations  0.77 us (1%)
    ppermute x20, waiting for transfers between devices, swap(): return lax.ppermute(array, axis, [(i, i ^ mask) for i in range(size)])  23.9 us
    ppermute x20, starting transfers between devices, swap(): return lax.ppermute(array, axis, [(i, i ^ mask) for i in range(size)])  20.7 us
    pallas_call x1, Pallas kernels, project(): pl.pallas_call(functools.partial(project_kernel, chunk_start), in_specs=[...  7.28 us
    ppermute x1, waiting for transfers between devices, hop(): lax.ppermute(array, 'vocab', [(2 * a + c, 2 * b + c) for a, b in pairs fo...  5.59 us
    pallas_call x9, Pallas kernels, vmem_call(): pl.pallas_call(kernel, in_specs=[pl.BlockSpec(memory_space=pltpu.SMEM)] *...  5.1 us
    pallas_call x1, Pallas kernels, finish(): pl.pallas_call(finish_kernel, in_specs=[pl.BlockSpec(memory_space=pltpu.V...  1.68 us
  transfers between devices with their start and end apart: 21, of which 14 were waited for; matrix products, arithmetic and copies ran while one was open for 0% of the time, Pallas kernels for 8%

profile of v6, /device:TPU:0, one launch (start us, length us, event | category | flops | bytes accessed | tf_op | source)
XLA Modules:
  0.0 66.9 jit_solution(11436084043552351676)
XLA Ops:
  0.6 7.3 %project.1 = (bf16[4,512,1280]{2,1,0:T(8,128)(2,1)S(1)}, bf16[4,512,1280]{2,1,0:T(8,128)(2,1)S(1)}, f32[64,128]{1,0:T(8,128)S(1)}, bf16[64,1280]{1,0:T(8,128)(2,...) custom-call(s32[1]{0:T(128)} %bitcast.own_ref, ...), custom_call_target="tpu_custom_call" | custom-call | flops 3758096384 | tf_op jit(solution)/shard_map/project/pallas_call | solution.py:115
  7.9 3.0 %collective-permute-start = (bf16[64,1280]{1,0:T(8,128)(2,1)S(1)}, bf16[64,1280]{1,0:T(8,128)(2,1)S(1)}, u32[]{:S(2)}, u32[]{:S(2)}) collective-permute-start(bf16[64,1280]{1,0:T(8,128)(2,1)S(1)} %get-tuple-element.26), channel_id=1, source_target_pairs={{0,8},{8,0},{16,24},{24,16},{1,9},{9,1},{17,25},{25,17},{2,10},{10... | collective-permute-start | bytes 491528 | tf_op jit(solution)/shard_map/ppermute | solution.py:449
  10.9 1.5 %collective-permute-start.1 = (bf16[64,1280]{1,0:T(8,128)(2,1)S(1)}, bf16[64,1280]{1,0:T(8,128)(2,1)S(1)}, u32[]{:S(2)}, u32[]{:S(2)}) collective-permute-start(bf16[64,1280]{1,0:T(8,128)(2,1)S(1)} %get-tuple-element.27), channel_id=1, source_target_pairs={{0,16},{8,24},{16,0},{24,8},{1,17},{9,25},{17,1},{25,9},{2,18},{10... | collective-permute-start | bytes 491528 | tf_op jit(solution)/shard_map/ppermute | solution.py:449
  12.5 0.0 collective-permute-start.2
  12.5 3.5 %collective-permute-done.refs_1_.refs_5_ = bf16[64,1280]{1,0:T(8,128)(2,1)S(1)} collective-permute-done((bf16[64,1280]{1,0:T(8,128)(2,1)S(1)}, bf16[64,1280]{1,0:T(8,128)(2,1)S(1)}, u32[]{:S(2)}, u32[]{:S(2)}) %collective-permute-start) | collective-permute-done | bytes 163872 | tf_op jit(solution)/shard_map/ppermute | solution.py:449
  16.0 4.1 %collective-permute-done.1.refs_2_.refs_6_ = bf16[64,1280]{1,0:T(8,128)(2,1)S(1)} collective-permute-done((bf16[64,1280]{1,0:T(8,128)(2,1)S(1)}, bf16[64,1280]{1,0:T(8,128)(2,1)S(1)}, u32[]{:S(2)}, u32[]{:S(2)}) %collective-permute-start.1) | collective-permute-done | bytes 163872 | tf_op jit(solution)/shard_map/ppermute | solution.py:449
  20.1 0.0 collective-permute-done.2.refs_3_.refs_7_
  20.1 0.9 %stats.1.refs_0_ = f32[32,128]{1,0:T(8,128)S(1)} custom-call(s32[1]{0:T(128)} %bitcast.own_ref, s32[1]{0:T(128)} %bitcast.1.shard_ref, f32[64,128]{1,0:T(8,128)S(1)} %get-tuple-element.24.meta_ref, bf16[64,1280]{1,0:T(8,128)(2,1)S(1)} %get-tuple-element.25.refs_0_.refs_4_, bf16[64,1280]{1,0:T(8,128)(2,1)S(1)} %collective-permute-done.refs_1_.refs_5_, ...), custom_call_target="tpu_custom_call" | custom-call | flops 13107200 | bytes 655360 | tf_op jit(solution)/shard_map/stats/pallas_call | solution.py:201
  21.0 0.1 collective-permute-start.3
  21.1 1.2 %collective-permute-done.3.refs_1_ = f32[32,128]{1,0:T(8,128)S(1)} collective-permute-done((f32[32,128]{1,0:T(8,128)S(1)}, f32[32,128]{1,0:T(8,128)S(1)}, u32[]{:S(2)}, u32[]{:S(2)}) %collective-permute-start.3) | collective-permute-done | bytes 16416 | tf_op jit(solution)/shard_map/ppermute | solution.py:449
  22.2 0.2 collective-permute-start.7
  22.5 3.6 %collective-permute-start.4 = (f32[32,128]{1,0:T(8,128)S(1)}, f32[32,128]{1,0:T(8,128)S(1)}, u32[]{:S(2)}, u32[]{:S(2)}) collective-permute-start(f32[32,128]{1,0:T(8,128)S(1)} %merge.1.refs_0_), channel_id=1, source_target_pairs={{0,6},{1,7},{2,4},{3,5},{4,2},{5,3},{6,0},{7,1},{8,14},{9,15},{10,... | collective-permute-start | bytes 49160 | tf_op jit(solution)/shard_map/ppermute | solution.py:449
  26.1 0.0 collective-permute-start.5
  26.1 0.8 %collective-permute-start.6 = (f32[32,128]{1,0:T(8,128)S(1)}, f32[32,128]{1,0:T(8,128)S(1)}, u32[]{:S(2)}, u32[]{:S(2)}) collective-permute-start(f32[32,128]{1,0:T(8,128)S(1)} %merge.1.refs_0_), channel_id=1, source_target_pairs={{0,2},{1,3},{2,0},{3,1},{4,6},{5,7},{6,4},{7,5},{8,10},{9,11},{10,... | collective-permute-start | bytes 49160 | tf_op jit(solution)/shard_map/ppermute | solution.py:449
  26.9 1.1 %collective-permute-done.4.refs_1_ = f32[32,128]{1,0:T(8,128)S(1)} collective-permute-done((f32[32,128]{1,0:T(8,128)S(1)}, f32[32,128]{1,0:T(8,128)S(1)}, u32[]{:S(2)}, u32[]{:S(2)}) %collective-permute-start.4) | collective-permute-done | bytes 16416 | tf_op jit(solution)/shard_map/ppermute | solution.py:449
  28.0 2.7 %collective-permute-done.5.refs_2_ = f32[32,128]{1,0:T(8,128)S(1)} collective-permute-done((f32[32,128]{1,0:T(8,128)S(1)}, f32[32,128]{1,0:T(8,128)S(1)}, u32[]{:S(2)}, u32[]{:S(2)}) %collective-permute-start.5) | collective-permute-done | bytes 16416 | tf_op jit(solution)/shard_map/ppermute | solution.py:449
  30.7 0.0 collective-permute-done.6.refs_3_
  30.7 0.9 %gradients.1 = (bf16[64,1280]{1,0:T(8,128)(2,1)S(1)}, bf16[64,1280]{1,0:T(8,128)(2,1)S(1)}, bf16[64,1280]{1,0:T(8,128)(2,1)S(1)}, bf16[64,1280]{1,0:T(8,128)(2,1...) custom-call(s32[1]{0:T(128)} %bitcast.own_ref, ...), custom_call_target="tpu_custom_call" | custom-call | flops 6553600 | bytes 1310720 | tf_op jit(solution)/shard_map/gradients/pallas_call | solution.py:278
  31.6 1.3 %collective-permute-start.8 = (bf16[64,1280]{1,0:T(8,128)(2,1)S(1)}, bf16[64,1280]{1,0:T(8,128)(2,1)S(1)}, u32[]{:S(2)}, u32[]{:S(2)}) collective-permute-start(bf16[64,1280]{1,0:T(8,128)(2,1)S(1)} %get-tuple-element.34), channel_id=1, source_target_pairs={{0,8},{8,0},{16,24},{24,16},{1,9},{9,1},{17,25},{25,17},{2,10},{10... | collective-permute-start | bytes 491528 | tf_op jit(solution)/shard_map/ppermute | solution.py:449
  32.9 0.8 %collective-permute-start.9 = (bf16[64,1280]{1,0:T(8,128)(2,1)S(1)}, bf16[64,1280]{1,0:T(8,128)(2,1)S(1)}, u32[]{:S(2)}, u32[]{:S(2)}) collective-permute-start(bf16[64,1280]{1,0:T(8,128)(2,1)S(1)} %get-tuple-element.35), channel_id=1, source_target_pairs={{0,16},{8,24},{16,0},{24,8},{1,17},{9,25},{17,1},{25,9},{2,18},{10... | collective-permute-start | bytes 491528 | tf_op jit(solution)/shard_map/ppermute | solution.py:449
  33.7 1.4 %collective-permute-start.10 = (bf16[64,1280]{1,0:T(8,128)(2,1)S(1)}, bf16[64,1280]{1,0:T(8,128)(2,1)S(1)}, u32[]{:S(2)}, u32[]{:S(2)}) collective-permute-start(bf16[64,1280]{1,0:T(8,128)(2,1)S(1)} %get-tuple-element.36), channel_id=1, source_target_pairs={{0,24},{8,16},{16,8},{24,0},{1,25},{9,17},{17,9},{25,1},{2,26},{10... | collective-permute-start | bytes 491528 | tf_op jit(solution)/shard_map/ppermute | solution.py:449
  35.2 0.0 collective-permute-start.11
  35.2 3.3 %collective-permute-done.8.refs_1_ = bf16[64,1280]{1,0:T(8,128)(2,1)S(1)} collective-permute-done((bf16[64,1280]{1,0:T(8,128)(2,1)S(1)}, bf16[64,1280]{1,0:T(8,128)(2,1)S(1)}, u32[]{:S(2)}, u32[]{:S(2)}) %collective-permute-start.8) | collective-permute-done | bytes 163872 | tf_op jit(solution)/shard_map/ppermute | solution.py:449
  38.5 0.0 collective-permute-start.12
  38.5 2.9 %collective-permute-done.9.refs_2_ = bf16[64,1280]{1,0:T(8,128)(2,1)S(1)} collective-permute-done((bf16[64,1280]{1,0:T(8,128)(2,1)S(1)}, bf16[64,1280]{1,0:T(8,128)(2,1)S(1)}, u32[]{:S(2)}, u32[]{:S(2)}) %collective-permute-start.9) | collective-permute-done | bytes 163872 | tf_op jit(solution)/shard_map/ppermute | solution.py:449
  41.4 0.0 collective-permute-start.13
  41.4 0.0 collective-permute-done.10.refs_3_
  41.5 0.5 collective-permute-start.14
  42.0 0.5 share.2.part_ref
  42.6 0.0 collective-permute-done.11.refs_0_
  42.6 0.0 collective-permute-done.12.refs_1_
  42.6 0.3 collective-permute-done.13.refs_2_
  42.8 0.2 collective-permute-done.14.refs_3_
  43.1 0.0 collective-permute-done.7.theirs_ref.refs_1_
  43.1 0.7 encode.2
  43.8 0.1 collective-permute-start.15
  43.9 1.0 %encode.3 = s16[528,256]{1,0:T(8,128)(2,1)S(1)} custom-call(s32[1]{0:T(128)} %bitcast.own_ref, s32[1]{0:T(128)} %bitcast.1.shard_ref, bf16[4,512,1280]{2,1,0:T(8,128)(2,1)S(1)} %get-tuple-element.30.mine_ref.refs_0_, bf16[4,512,1280]{2,1,0:T(8,128)(2,1)S(1)} %collective-permute-done.7.theirs_ref.refs_1_, bf16[256,1280]{1,0:T(8,128)(2,1)S(1)} %gather.2.grad_ref.refs_2_, ...), custom_call_target="tpu_custom_call" | custom-call | flops 1000 | tf_op jit(solution)/shard_map/encode/pallas_call | solution.py:309
  44.8 2.2 %collective-permute-start.20 = (s16[528,256]{1,0:T(8,128)(2,1)S(1)}, s16[528,256]{1,0:T(8,128)(2,1)S(1)}, u32[]{:S(2)}, u32[]{:S(2)}) collective-permute-start(s16[528,256]{1,0:T(8,128)(2,1)S(1)} %encode.3), channel_id=1, source_target_pairs={{0,2},{1,3},{2,0},{3,1},{4,6},{5,7},{6,4},{7,5},{8,10},{9,11},{10,... | collective-permute-start | bytes 811016 | tf_op jit(solution)/shard_map/ppermute | solution.py:449
  47.1 0.9 %share.3.value_ref = f32[512,256]{1,0:T(8,128)S(1)} custom-call(s32[1]{0:T(128)} %bitcast.own_ref, s32[1]{0:T(128)} %bitcast.1.shard_ref, bf16[4,512,1280]{2,1,0:T(8,128)(2,1)S(1)} %get-tuple-element.30.mine_ref.refs_0_, bf16[4,512,1280]{2,1,0:T(8,128)(2,1)S(1)} %collective-permute-done.7.theirs_ref.refs_1_, bf16[256,1280]{1,0:T(8,128)(2,1)S(1)} %gather.2.grad_ref.refs_2_, ...), custom_call_target="tpu_custom_call" | custom-call | flops 1000 | tf_op jit(solution)/shard_map/share/pallas_call | solution.py:309
  47.9 5.6 %collective-permute-done.15.refs_4_.coded_ref = s16[528,256]{1,0:T(8,128)(2,1)S(1)} collective-permute-done((s16[528,256]{1,0:T(8,128)(2,1)S(1)}, s16[528,256]{1,0:T(8,128)(2,1)S(1)}, u32[]{:S(2)}, u32[]{:S(2)}) %collective-permute-start.15) | collective-permute-done | bytes 270368 | tf_op jit(solution)/shard_map/ppermute | solution.py:453
  53.5 0.2 relay.1
  53.7 0.0 copy-start
  53.7 1.7 %collective-permute-start.19 = (s16[528,256]{1,0:T(8,128)(2,1)S(1)}, s16[528,256]{1,0:T(8,128)(2,1)S(1)}, u32[]{:S(2)}, u32[]{:S(2)}) collective-permute-start(s16[528,256]{1,0:T(8,128)(2,1)S(1)} %relay.1), channel_id=1, source_target_pairs={{0,6},{1,7},{2,4},{3,5},{4,2},{5,3},{6,0},{7,1},{8,14},{9,15},{10,... | collective-permute-start | bytes 811016 | tf_op jit(solution)/shard_map/ppermute | solution.py:449
  55.4 0.9 %keep.1.sum_ref = f32[512,256]{1,0:T(8,128)S(1)} custom-call(s32[1]{0:T(128)} %bitcast.own_ref, s32[1]{0:T(128)} %bitcast.1.shard_ref, bf16[4,512,1280]{2,1,0:T(8,128)(2,1)S(1)} %get-tuple-element.30.mine_ref.refs_0_, bf16[4,512,1280]{2,1,0:T(8,128)(2,1)S(1)} %collective-permute-done.7.theirs_ref.refs_1_, bf16[256,1280]{1,0:T(8,128)(2,1)S(1)} %gather.2.grad_ref.refs_2_, ...), custom_call_target="tpu_custom_call" | custom-call | flops 1000 | tf_op jit(solution)/shard_map/keep/pallas_call | solution.py:309
  56.3 1.0 %collective-permute-start.16 = (f32[64,128]{1,0:T(8,128)S(1)}, f32[64,128]{1,0:T(8,128)S(1)}, u32[]{:S(2)}, u32[]{:S(2)}) collective-permute-start(f32[64,128]{1,0:T(8,128)S(1)} %get-tuple-element.39), channel_id=1, source_target_pairs={{0,8},{8,0},{16,24},{24,16},{1,9},{9,1},{17,25},{25,17},{2,10},{10... | collective-permute-start | bytes 98312 | tf_op jit(solution)/shard_map/ppermute | solution.py:449
  57.3 1.3 %collective-permute-start.17 = (f32[64,128]{1,0:T(8,128)S(1)}, f32[64,128]{1,0:T(8,128)S(1)}, u32[]{:S(2)}, u32[]{:S(2)}) collective-permute-start(f32[64,128]{1,0:T(8,128)S(1)} %get-tuple-element.41), channel_id=1, source_target_pairs={{0,16},{8,24},{16,0},{24,8},{1,17},{9,25},{17,1},{25,9},{2,18},{10... | collective-permute-start | bytes 98312 | tf_op jit(solution)/shard_map/ppermute | solution.py:449
  58.6 1.3 %collective-permute-start.18 = (f32[64,128]{1,0:T(8,128)S(1)}, f32[64,128]{1,0:T(8,128)S(1)}, u32[]{:S(2)}, u32[]{:S(2)}) collective-permute-start(f32[64,128]{1,0:T(8,128)S(1)} %get-tuple-element.43), channel_id=1, source_target_pairs={{0,24},{8,16},{16,8},{24,0},{1,25},{9,17},{17,9},{25,1},{2,26},{10... | collective-permute-start | bytes 98312 | tf_op jit(solution)/shard_map/ppermute | solution.py:449
  59.8 0.8 %collective-permute-done.16.refs_1_ = f32[64,128]{1,0:T(8,128)S(1)} collective-permute-done((f32[64,128]{1,0:T(8,128)S(1)}, f32[64,128]{1,0:T(8,128)S(1)}, u32[]{:S(2)}, u32[]{:S(2)}) %collective-permute-start.16) | collective-permute-done | bytes 32800 | tf_op jit(solution)/shard_map/ppermute | solution.py:449
  60.6 0.7 %collective-permute-done.17.refs_2_ = f32[64,128]{1,0:T(8,128)S(1)} collective-permute-done((f32[64,128]{1,0:T(8,128)S(1)}, f32[64,128]{1,0:T(8,128)S(1)}, u32[]{:S(2)}, u32[]{:S(2)}) %collective-permute-start.17) | collective-permute-done | bytes 32800 | tf_op jit(solution)/shard_map/ppermute | solution.py:449
  61.3 2.0 %collective-permute-done.18.refs_3_ = f32[64,128]{1,0:T(8,128)S(1)} collective-permute-done((f32[64,128]{1,0:T(8,128)S(1)}, f32[64,128]{1,0:T(8,128)S(1)}, u32[]{:S(2)}, u32[]{:S(2)}) %collective-permute-start.18) | collective-permute-done | bytes 32800 | tf_op jit(solution)/shard_map/ppermute | solution.py:449
  63.4 0.0 copy-done
  63.4 0.9 %place.1 = (bf16[512,256]{1,0:T(8,128)(2,1)S(1)}, f32[1,512]{1,0:T(1,128)}) custom-call(s32[1]{0:T(128)} %bitcast.own_ref, s32[1]{0:T(128)} %bitcast.1.shard_ref, s32[1,512]{1,0:T(1,128)S(1)} %bitcast.5, f32[64,128]{1,0:T(8,128)S(1)} %get-tuple-element.37.refs_0_, f32[64,128]{1,0:T(8,128)S(1)} %collective-permute-done.16.refs_1_, ...), custom_call_target="tpu_custom_call" | custom-call | flops 134217728 | tf_op jit(solution)/shard_map/place/pallas_call | solution.py:309
  64.3 0.0 collective-permute-done.20.refs_1_
  64.3 0.9 %collective-permute-done.19.refs_0_ = s16[528,256]{1,0:T(8,128)(2,1)S(1)} collective-permute-done((s16[528,256]{1,0:T(8,128)(2,1)S(1)}, s16[528,256]{1,0:T(8,128)(2,1)S(1)}, u32[]{:S(2)}, u32[]{:S(2)}) %collective-permute-start.19) | collective-permute-done | bytes 270368 | tf_op jit(solution)/shard_map/ppermute | solution.py:449
  65.2 1.7 %finish.1 = f32[1,512,512]{2,1,0:T(8,128)} custom-call(bf16[512,256]{1,0:T(8,128)(2,1)S(1)} %get-tuple-element.44.place_ref, f32[512,256]{1,0:T(8,128)S(1)} %keep.1.sum_ref, s16[528,256]{1,0:T(8,128)(2,1)S(1)} %collective-permute-done.19.refs_0_, s16[528,256]{1,0:T(8,128)(2,1)S(1)} %collective-permute-done.20.refs_1_), custom_call_target="tpu_custom_call" | custom-call | flops 1000 | tf_op jit(solution)/shard_map/finish/pallas_call | solution.py:436
  (3 shorter events, 0.1 us)
Async XLA Ops:
  7.9 8.0 %collective-permute-start = (bf16[64,1280]{1,0:T(8,128)(2,1)S(1)}, bf16[64,1280]{1,0:T(8,128)(2,1)S(1)}, u32[]{:S(2)}, u32[]{:S(2)}) collective-permute-start(bf16[64,1280]{1,0:T(8,128)(2,1)S(1)} %get-tuple-element.26), channel_id=1, source_target_pairs={{0,8},{8,0},{16,24},{24,16},{1,9},{9,1},{17,25},{25,17},{2,10},{10... | collective-permute-start | bytes 491528 | tf_op jit(solution)/shard_map/ppermute | solution.py:449
  10.9 9.2 %collective-permute-start.1 = (bf16[64,1280]{1,0:T(8,128)(2,1)S(1)}, bf16[64,1280]{1,0:T(8,128)(2,1)S(1)}, u32[]{:S(2)}, u32[]{:S(2)}) collective-permute-start(bf16[64,1280]{1,0:T(8,128)(2,1)S(1)} %get-tuple-element.27), channel_id=1, source_target_pairs={{0,16},{8,24},{16,0},{24,8},{1,17},{9,25},{17,1},{25,9},{2,18},{10... | collective-permute-start | bytes 491528 | tf_op jit(solution)/shard_map/ppermute | solution.py:449
  12.5 7.7 %collective-permute-start.2 = (bf16[64,1280]{1,0:T(8,128)(2,1)S(1)}, bf16[64,1280]{1,0:T(8,128)(2,1)S(1)}, u32[]{:S(2)}, u32[]{:S(2)}) collective-permute-start(bf16[64,1280]{1,0:T(8,128)(2,1)S(1)} %get-tuple-element.28), channel_id=1, source_target_pairs={{0,24},{8,16},{16,8},{24,0},{1,25},{9,17},{17,9},{25,1},{2,26},{10... | collective-permute-start | bytes 491528 | tf_op jit(solution)/shard_map/ppermute | solution.py:449
  21.0 1.2 %collective-permute-start.3 = (f32[32,128]{1,0:T(8,128)S(1)}, f32[32,128]{1,0:T(8,128)S(1)}, u32[]{:S(2)}, u32[]{:S(2)}) collective-permute-start(f32[32,128]{1,0:T(8,128)S(1)} %stats.1.refs_0_), channel_id=1, source_target_pairs={{0,1},{1,0},{2,3},{3,2},{4,5},{5,4},{6,7},{7,6},{8,9},{9,8},{10,11... | collective-permute-start | bytes 49160 | tf_op jit(solution)/shard_map/ppermute | solution.py:449
  22.2 20.9 %collective-permute-start.7 = (bf16[4,512,1280]{2,1,0:T(8,128)(2,1)S(1)}, bf16[4,512,1280]{2,1,0:T(8,128)(2,1)S(1)}, u32[]{:S(2)}, u32[]{:S(2)}) collective-permute-start(bf16[4,512,1280]{2,1,0:T(8,128)(2,1)S(1)} %get-tuple-element.32), channel_id=1, source_target_pairs={{0,1},{1,0},{2,3},{3,2},{4,5},{5,4},{6,7},{7,6},{8,9},{9,8},{10,11... | collective-permute-start | bytes 15728648 | tf_op jit(solution)/shard_map/ppermute | solution.py:449
  22.5 5.5 %collective-permute-start.4 = (f32[32,128]{1,0:T(8,128)S(1)}, f32[32,128]{1,0:T(8,128)S(1)}, u32[]{:S(2)}, u32[]{:S(2)}) collective-permute-start(f32[32,128]{1,0:T(8,128)S(1)} %merge.1.refs_0_), channel_id=1, source_target_pairs={{0,6},{1,7},{2,4},{3,5},{4,2},{5,3},{6,0},{7,1},{8,14},{9,15},{10,... | collective-permute-start | bytes 49160 | tf_op jit(solution)/shard_map/ppermute | solution.py:449
  26.1 4.6 %collective-permute-start.5 = (f32[32,128]{1,0:T(8,128)S(1)}, f32[32,128]{1,0:T(8,128)S(1)}, u32[]{:S(2)}, u32[]{:S(2)}) collective-permute-start(f32[32,128]{1,0:T(8,128)S(1)} %merge.1.refs_0_), channel_id=1, source_target_pairs={{0,4},{1,5},{2,6},{3,7},{4,0},{5,1},{6,2},{7,3},{8,12},{9,13},{10,... | collective-permute-start | bytes 49160 | tf_op jit(solution)/shard_map/ppermute | solution.py:449
  26.1 4.6 %collective-permute-start.6 = (f32[32,128]{1,0:T(8,128)S(1)}, f32[32,128]{1,0:T(8,128)S(1)}, u32[]{:S(2)}, u32[]{:S(2)}) collective-permute-start(f32[32,128]{1,0:T(8,128)S(1)} %merge.1.refs_0_), channel_id=1, source_target_pairs={{0,2},{1,3},{2,0},{3,1},{4,6},{5,7},{6,4},{7,5},{8,10},{9,11},{10,... | collective-permute-start | bytes 49160 | tf_op jit(solution)/shard_map/ppermute | solution.py:449
  31.6 6.9 %collective-permute-start.8 = (bf16[64,1280]{1,0:T(8,128)(2,1)S(1)}, bf16[64,1280]{1,0:T(8,128)(2,1)S(1)}, u32[]{:S(2)}, u32[]{:S(2)}) collective-permute-start(bf16[64,1280]{1,0:T(8,128)(2,1)S(1)} %get-tuple-element.34), channel_id=1, source_target_pairs={{0,8},{8,0},{16,24},{24,16},{1,9},{9,1},{17,25},{25,17},{2,10},{10... | collective-permute-start | bytes 491528 | tf_op jit(solution)/shard_map/ppermute | solution.py:449
  32.9 8.5 %collective-permute-start.9 = (bf16[64,1280]{1,0:T(8,128)(2,1)S(1)}, bf16[64,1280]{1,0:T(8,128)(2,1)S(1)}, u32[]{:S(2)}, u32[]{:S(2)}) collective-permute-start(bf16[64,1280]{1,0:T(8,128)(2,1)S(1)} %get-tuple-element.35), channel_id=1, source_target_pairs={{0,16},{8,24},{16,0},{24,8},{1,17},{9,25},{17,1},{25,9},{2,18},{10... | collective-permute-start | bytes 491528 | tf_op jit(solution)/shard_map/ppermute | solution.py:449
  33.7 7.7 %collective-permute-start.10 = (bf16[64,1280]{1,0:T(8,128)(2,1)S(1)}, bf16[64,1280]{1,0:T(8,128)(2,1)S(1)}, u32[]{:S(2)}, u32[]{:S(2)}) collective-permute-start(bf16[64,1280]{1,0:T(8,128)(2,1)S(1)} %get-tuple-element.36), channel_id=1, source_target_pairs={{0,24},{8,16},{16,8},{24,0},{1,25},{9,17},{17,9},{25,1},{2,26},{10... | collective-permute-start | bytes 491528 | tf_op jit(solution)/shard_map/ppermute | solution.py:449
  35.2 7.4 %collective-permute-start.11 = (bf16[64,1280]{1,0:T(8,128)(2,1)S(1)}, bf16[64,1280]{1,0:T(8,128)(2,1)S(1)}, u32[]{:S(2)}, u32[]{:S(2)}) collective-permute-start(bf16[64,1280]{1,0:T(8,128)(2,1)S(1)} %get-tuple-element.33.refs_0_), channel_id=1, source_target_pairs={{0,1},{1,0},{2,3},{3,2},{4,5},{5,4},{6,7},{7,6},{8,9},{9,8},{10,11... | collective-permute-start | bytes 491528 | tf_op jit(solution)/shard_map/ppermute | solution.py:449
  38.5 4.1 %collective-permute-start.12 = (bf16[64,1280]{1,0:T(8,128)(2,1)S(1)}, bf16[64,1280]{1,0:T(8,128)(2,1)S(1)}, u32[]{:S(2)}, u32[]{:S(2)}) collective-permute-start(bf16[64,1280]{1,0:T(8,128)(2,1)S(1)} %collective-permute-done.8.refs_1_), channel_id=1, source_target_pairs={{0,1},{1,0},{2,3},{3,2},{4,5},{5,4},{6,7},{7,6},{8,9},{9,8},{10,11... | collective-permute-start | bytes 491528 | tf_op jit(solution)/shard_map/ppermute | solution.py:449
  41.4 1.4 %collective-permute-start.13 = (bf16[64,1280]{1,0:T(8,128)(2,1)S(1)}, bf16[64,1280]{1,0:T(8,128)(2,1)S(1)}, u32[]{:S(2)}, u32[]{:S(2)}) collective-permute-start(bf16[64,1280]{1,0:T(8,128)(2,1)S(1)} %collective-permute-done.9.refs_2_), channel_id=1, source_target_pairs={{0,1},{1,0},{2,3},{3,2},{4,5},{5,4},{6,7},{7,6},{8,9},{9,8},{10,11... | collective-permute-start | bytes 491528 | tf_op jit(solution)/shard_map/ppermute | solution.py:449
  41.5 1.6 %collective-permute-start.14 = (bf16[64,1280]{1,0:T(8,128)(2,1)S(1)}, bf16[64,1280]{1,0:T(8,128)(2,1)S(1)}, u32[]{:S(2)}, u32[]{:S(2)}) collective-permute-start(bf16[64,1280]{1,0:T(8,128)(2,1)S(1)} %collective-permute-done.10.refs_3_), channel_id=1, source_target_pairs={{0,1},{1,0},{2,3},{3,2},{4,5},{5,4},{6,7},{7,6},{8,9},{9,8},{10,11... | collective-permute-start | bytes 491528 | tf_op jit(solution)/shard_map/ppermute | solution.py:449
  43.8 9.7 %collective-permute-start.15 = (s16[528,256]{1,0:T(8,128)(2,1)S(1)}, s16[528,256]{1,0:T(8,128)(2,1)S(1)}, u32[]{:S(2)}, u32[]{:S(2)}) collective-permute-start(s16[528,256]{1,0:T(8,128)(2,1)S(1)} %encode.2), channel_id=1, source_target_pairs={{0,2},{1,3},{6,4},{7,5},{2,6},{3,7},{4,0},{5,1},{8,10},{9,11},{14,... | collective-permute-start | bytes 811016 | tf_op jit(solution)/shard_map/ppermute | solution.py:453
  44.8 19.4 %collective-permute-start.20 = (s16[528,256]{1,0:T(8,128)(2,1)S(1)}, s16[528,256]{1,0:T(8,128)(2,1)S(1)}, u32[]{:S(2)}, u32[]{:S(2)}) collective-permute-start(s16[528,256]{1,0:T(8,128)(2,1)S(1)} %encode.3), channel_id=1, source_target_pairs={{0,2},{1,3},{2,0},{3,1},{4,6},{5,7},{6,4},{7,5},{8,10},{9,11},{10,... | collective-permute-start | bytes 811016 | tf_op jit(solution)/shard_map/ppermute | solution.py:449
  53.7 9.6 %copy-start = (s32[512]{0:T(512)S(1)}, s32[512]{0:T(512)}, u32[]{:S(2)}) copy-start(s32[512]{0:T(512)} %param.6) | copy-start | bytes 6148
  53.7 11.5 %collective-permute-start.19 = (s16[528,256]{1,0:T(8,128)(2,1)S(1)}, s16[528,256]{1,0:T(8,128)(2,1)S(1)}, u32[]{:S(2)}, u32[]{:S(2)}) collective-permute-start(s16[528,256]{1,0:T(8,128)(2,1)S(1)} %relay.1), channel_id=1, source_target_pairs={{0,6},{1,7},{2,4},{3,5},{4,2},{5,3},{6,0},{7,1},{8,14},{9,15},{10,... | collective-permute-start | bytes 811016 | tf_op jit(solution)/shard_map/ppermute | solution.py:449
  56.3 4.3 %collective-permute-start.16 = (f32[64,128]{1,0:T(8,128)S(1)}, f32[64,128]{1,0:T(8,128)S(1)}, u32[]{:S(2)}, u32[]{:S(2)}) collective-permute-start(f32[64,128]{1,0:T(8,128)S(1)} %get-tuple-element.39), channel_id=1, source_target_pairs={{0,8},{8,0},{16,24},{24,16},{1,9},{9,1},{17,25},{25,17},{2,10},{10... | collective-permute-start | bytes 98312 | tf_op jit(solution)/shard_map/ppermute | solution.py:449
  57.3 4.0 %collective-permute-start.17 = (f32[64,128]{1,0:T(8,128)S(1)}, f32[64,128]{1,0:T(8,128)S(1)}, u32[]{:S(2)}, u32[]{:S(2)}) collective-permute-start(f32[64,128]{1,0:T(8,128)S(1)} %get-tuple-element.41), channel_id=1, source_target_pairs={{0,16},{8,24},{16,0},{24,8},{1,17},{9,25},{17,1},{25,9},{2,18},{10... | collective-permute-start | bytes 98312 | tf_op jit(solution)/shard_map/ppermute | solution.py:449
  58.6 4.8 %collective-permute-start.18 = (f32[64,128]{1,0:T(8,128)S(1)}, f32[64,128]{1,0:T(8,128)S(1)}, u32[]{:S(2)}, u32[]{:S(2)}) collective-permute-start(f32[64,128]{1,0:T(8,128)S(1)} %get-tuple-element.43), channel_id=1, source_target_pairs={{0,24},{8,16},{16,8},{24,0},{1,25},{9,17},{17,9},{25,1},{2,26},{10... | collective-permute-start | bytes 98312 | tf_op jit(solution)/shard_map/ppermute | solution.py:449
